TPU v7x, 32 devices: a whole 2x2x4 slice. The times are simulated.
32 devices in a mesh: pipe: 4 (over y, x), expert: 8 (over z, core).
Axes of the slice: x: 2, y: 2, z: 4, core: 2. Of those that a mesh axis runs over, the one named last changes fastest.
Arguments:
- stream_a: bfloat16 [4, 64, 3584], P('pipe', 'expert'), may hold values from -6 to 6
- stream_b: bfloat16 [4, 64, 3584], P('pipe', 'expert'), may hold values from -6 to 6
- routes: int32 [2, 2, 4, 64, 2], P(None, None, 'pipe', 'expert'), may hold values from 0 to 3, all different within a row; in each aligned block of 8 rows (0 to 7, 8 to 15, ..., all dimensions but the last counted through in order) at most 4 rows name the same one
- up_weight: bfloat16 [2, 4, 3584, 4096], P(None, 'pipe', None, 'expert'), as said below
- down_weight: bfloat16 [2, 4, 4096, 3584], P(None, 'pipe', 'expert'), as said below
- router_weight: bfloat16 [2, 4, 3584, 4], P(None, 'pipe'), as said below
Outputs:
- final_a: bfloat16 [4, 64, 3584], P('pipe', 'expert')
- final_b: bfloat16 [4, 64, 3584], P('pipe', 'expert')
- expert_load: float32 [4, 4], replicated
Inputs may be any that keep to these rules, and one draw needn't show every extreme that they name: `routes`: in each device's 8 rows of one tick, stream and section, every expert is named by exactly 4 rows, and each row names 2 different experts. up_weight[1, i] equals up_weight[0, 3 - i]. down_weight[1, i] equals down_weight[0, 3 - i]. router_weight[1, i] equals router_weight[0, 3 - i].
All inputs are finite; a program needn't handle non-finite values.
Results may differ from a plain program's by a relative error of at most 0.0065.
Values may be sent and summed in bfloat16 or wider, within the bound.
No kernel may reach another device: no remote copies, remote signals or barrier semaphores. Data moves between devices by JAX's collectives and lax.ppermute only.
A program may use at most 64 MiB of HBM per device.

v0:
```python
import jax
import jax.numpy as jnp
from jax import lax
from jax.sharding import PartitionSpec as P

TICKS = 2


EPS = 1e-06


def from_behind(array, axis, by):
    length = lax.axis_size(axis)
    return lax.ppermute(array, axis, [(i, (i + by) % length) for i in range(length)])


def normalize(section_rows):
    widened = section_rows.astype(jnp.float32)
    return (widened * lax.rsqrt(jnp.mean(widened * widened, axis=-1, keepdims=True) + EPS)).astype(
        jnp.bfloat16
    )


def routing(normed, router, picked):
    experts = router.shape[-1]
    affinity = jax.nn.sigmoid(jnp.dot(normed, router, preferred_element_type=jnp.float32))
    member = (picked[:, :, None] == jnp.arange(experts, dtype=jnp.int32)[None, None, :]).astype(
        jnp.float32
    )
    chosen = jnp.sum(member * affinity[:, None, :], axis=2)
    shares = chosen / jnp.sum(chosen, axis=1, keepdims=True)
    weights = jnp.sum(shares[:, :, None] * member, axis=1)
    selected = jnp.sum(member, axis=1)
    return (weights, selected)


def prepare(section_rows, router, picked, group_size):
    normed = normalize(section_rows)
    weights, selected = routing(normed, router, picked)
    experts = router.shape[-1]
    capacity = section_rows.shape[0] * picked.shape[1] // experts
    before = jnp.cumsum(selected, axis=0) - selected
    slot_match = (
        before.T[:, None, :] == jnp.arange(capacity, dtype=jnp.float32)[None, :, None]
    ).astype(jnp.float32)
    placing = selected.T[:, None, :] * slot_match
    packed = jnp.einsum(
        "ecr,rd->ecd", placing.astype(jnp.bfloat16), normed, preferred_element_type=jnp.float32
    ).astype(jnp.bfloat16)
    features = packed.shape[2]
    outgoing = jnp.broadcast_to(packed[:, None], (experts, group_size, capacity, features)).reshape(
        experts * group_size, capacity, features
    )
    return (outgoing, placing * weights.T[:, None, :], jnp.sum(weights, axis=0))


def expert_rows(arrived, lift_weight, lower_weight):
    sources, slot_count, features = arrived.shape
    hidden = jax.nn.silu(
        jnp.dot(
            arrived.reshape(sources * slot_count, features),
            lift_weight,
            preferred_element_type=jnp.float32,
        )
    ).astype(jnp.bfloat16)
    partial_value = jnp.dot(hidden, lower_weight, preferred_element_type=jnp.float32).astype(
        jnp.bfloat16
    )
    return partial_value.reshape(sources, slot_count, features)


def finish(section_rows, returned, scaled, experts):
    sources, slot_count, features = returned.shape
    summed = (
        returned.reshape(experts, sources // experts, slot_count, features)
        .astype(jnp.float32)
        .sum(axis=1)
    )
    mixture = jnp.einsum("ecr,ecd->rd", scaled, summed, precision=lax.Precision.HIGHEST)
    return (section_rows.astype(jnp.float32) + mixture).astype(jnp.bfloat16)


def send_apart(outgoing, lift_weight, lower_weight):
    return lax.all_to_all(
        expert_rows(
            lax.all_to_all(outgoing, "expert", split_axis=0, concat_axis=0, tiled=True),
            lift_weight,
            lower_weight,
        ),
        "expert",
        split_axis=0,
        concat_axis=0,
        tiled=True,
    )


def shards(stream_a, stream_b, routes, up_weight, down_weight, router_weight):
    experts = router_weight.shape[-1]
    group_size = lax.axis_size("expert") // experts
    current = [stream_a[0], stream_b[0]]
    masses = [jnp.zeros((experts,), jnp.float32), jnp.zeros((experts,), jnp.float32)]
    for step_index in range(TICKS):
        if step_index > 0:
            current = [from_behind(current[0], "pipe", 1), from_behind(current[1], "pipe", -1)]
        prepared = [
            prepare(
                current[stream], router_weight[stream, 0], routes[step_index, stream, 0], group_size
            )
            for stream in range(2)
        ]
        returned = [
            send_apart(prepared[stream][0], up_weight[stream, 0], down_weight[stream, 0])
            for stream in range(2)
        ]
        current = [
            finish(current[stream], returned[stream], prepared[stream][1], experts)
            for stream in range(2)
        ]
        masses = [masses[stream] + prepared[stream][2] for stream in range(2)]
    layers = lax.axis_size("pipe")
    position = lax.axis_index("pipe")
    ladder = jnp.arange(layers, dtype=jnp.int32)
    own_row = (ladder == position).astype(jnp.float32)[:, None]
    mirror_row = (ladder == layers - 1 - position).astype(jnp.float32)[:, None]
    totals = lax.psum((masses[0], masses[1]), "expert")
    spread_table = own_row * totals[0][None, :] + mirror_row * totals[1][None, :]
    load_table = lax.psum(spread_table, "pipe")
    tokens_total = 2 * TICKS * current[0].shape[0] * lax.axis_size("expert")
    return (current[0][None], current[1][None], load_table / tokens_total)


def solution(mesh):
    return jax.shard_map(
        shards,
        mesh=mesh,
        in_specs=(
            P("pipe", "expert", None),
            P("pipe", "expert", None),
            P(None, None, "pipe", "expert", None),
            P(None, "pipe", None, "expert"),
            P(None, "pipe", "expert", None),
            P(None, "pipe", None, None),
        ),
        out_specs=(P("pipe", "expert", None), P("pipe", "expert", None), P()),
        check_vma=False,
    )
```

profile of v0, /device:TPU:0, one launch (start us, length us, event | category | flops | bytes accessed | tf_op | source)
XLA Modules:
  0.0 129.3 jit_solution(8097245174908488930)
XLA Ops:
  1.4 1.0 fusion.50
  2.3 1.0 fusion.41
  3.7 1.0 convolution_convert_fusion.7
  5.5 6.3 %all-to-all-start = ((bf16[8,4,3584]{2,1,0:T(4,128)(2,1)}), bf16[8,4,3584]{2,1,0:T(4,128)(2,1)S(1)}, u32[]{:S(2)}, u32[]{:S(2)}) async-start(bf16[8,4,3584]{2,1,0:T(4,128)(2,1)} %bitcast.8), calls=%async_computation | async-start | bytes 458752 | tf_op jit(solution)/shard_map/all_to_all | solution.py:86
  11.8 1.0 fusion.53
  12.8 1.0 fusion.35
  14.2 1.0 convolution_convert_fusion.5
  15.3 5.6 %all-to-all-done = bf16[8,4,3584]{2,1,0:T(4,128)(2,1)S(1)} async-done(((bf16[8,4,3584]{2,1,0:T(4,128)(2,1)}), bf16[8,4,3584]{2,1,0:T(4,128)(2,1)S(1)}, u32[]{:S(2)}, u32[]{:S(2)}) %all-to-all-start) | async-done | bytes 229408 | tf_op jit(solution)/shard_map/all_to_all | solution.py:86
  21.6 3.4 %all-to-all-start.4 = ((bf16[8,4,3584]{2,1,0:T(4,128)(2,1)}), bf16[8,4,3584]{2,1,0:T(4,128)(2,1)S(1)}, u32[]{:S(2)}, u32[]{:S(2)}) async-start(bf16[8,4,3584]{2,1,0:T(4,128)(2,1)} %bitcast.30), calls=%async_computation.4 | async-start | bytes 458752 | tf_op jit(solution)/shard_map/all_to_all | solution.py:86
  25.1 4.6 %convolution_convert_fusion.3 = bf16[32,3584]{1,0:T(8,128)(2,1)S(1)} fusion(bf16[2,1,512,3584]{3,2,1,0:T(8,128)(2,1)} %param.10, bf16[32,3584]{1,0:T(8,128)(2,1)S(1)} %reshape.215, bf16[2,1,3584,512]{3,2,1,0:T(8,128)(2,1)} %param.9), kind=kOutput, calls=%fused_computation.3 | convolution fusion | flops 235077632 | bytes 7798784 | tf_op jit(solution)/shard_map/dot_general | solution.py:66
  30.5 3.5 %all-to-all-done.4 = bf16[8,4,3584]{2,1,0:T(4,128)(2,1)S(1)} async-done(((bf16[8,4,3584]{2,1,0:T(4,128)(2,1)}), bf16[8,4,3584]{2,1,0:T(4,128)(2,1)S(1)}, u32[]{:S(2)}, u32[]{:S(2)}) %all-to-all-start.4) | async-done | bytes 229408 | tf_op jit(solution)/shard_map/all_to_all | solution.py:86
  34.0 3.4 %all-to-all-start.1 = ((bf16[8,4,3584]{2,1,0:T(4,128)(2,1)}), bf16[8,4,3584]{2,1,0:T(4,128)(2,1)S(1)}, u32[]{:S(2)}, u32[]{:S(2)}) async-start(bf16[8,4,3584]{2,1,0:T(4,128)(2,1)} %reshape.216), calls=%async_computation.1 | async-start | bytes 458752 | tf_op jit(solution)/shard_map/all_to_all | solution.py:84
  37.5 4.6 %convolution_convert_fusion.1 = bf16[32,3584]{1,0:T(8,128)(2,1)S(1)} fusion(bf16[2,1,512,3584]{3,2,1,0:T(8,128)(2,1)} %param.10, bf16[32,3584]{1,0:T(8,128)(2,1)S(1)} %reshape.221, bf16[2,1,3584,512]{3,2,1,0:T(8,128)(2,1)} %param.9), kind=kOutput, calls=%fused_computation.1 | convolution fusion | flops 235077632 | bytes 7798784 | tf_op jit(solution)/shard_map/dot_general | solution.py:66
  42.1 0.8 reshape.222
  42.9 3.5 %all-to-all-done.1 = bf16[8,4,3584]{2,1,0:T(4,128)(2,1)S(1)} async-done(((bf16[8,4,3584]{2,1,0:T(4,128)(2,1)}), bf16[8,4,3584]{2,1,0:T(4,128)(2,1)S(1)}, u32[]{:S(2)}, u32[]{:S(2)}) %all-to-all-start.1) | async-done | bytes 229408 | tf_op jit(solution)/shard_map/all_to_all | solution.py:84
  46.4 3.4 %all-to-all-start.5 = ((bf16[8,4,3584]{2,1,0:T(4,128)(2,1)}), bf16[8,4,3584]{2,1,0:T(4,128)(2,1)S(1)}, u32[]{:S(2)}, u32[]{:S(2)}) async-start(bf16[8,4,3584]{2,1,0:T(4,128)(2,1)} %reshape.222), calls=%async_computation.5 | async-start | bytes 458752 | tf_op jit(solution)/shard_map/all_to_all | solution.py:84
  50.4 1.6 %collective-permute-start = (bf16[8,3584]{1,0:T(8,128)(2,1)S(1)}, bf16[8,3584]{1,0:T(8,128)(2,1)S(1)}, u32[]{:S(2)}, u32[]{:S(2)}) collective-permute-start(bf16[8,3584]{1,0:T(8,128)(2,1)S(1)} %fusion.7), channel_id=1, source_target_pairs={{0,8},{8,16},{16,24},{24,0},{1,9},{9,17},{17,25},{25,1},{2,10},{10... | collective-permute-start | bytes 172040 | tf_op jit(solution)/shard_map/ppermute | solution.py:14
  52.0 6.8 %all-to-all-done.5 = bf16[8,4,3584]{2,1,0:T(4,128)(2,1)S(1)} async-done(((bf16[8,4,3584]{2,1,0:T(4,128)(2,1)}), bf16[8,4,3584]{2,1,0:T(4,128)(2,1)S(1)}, u32[]{:S(2)}, u32[]{:S(2)}) %all-to-all-start.5) | async-done | bytes 229408 | tf_op jit(solution)/shard_map/all_to_all | solution.py:84
  59.4 2.5 %collective-permute-start.1 = (bf16[8,3584]{1,0:T(8,128)(2,1)S(1)}, bf16[8,3584]{1,0:T(8,128)(2,1)S(1)}, u32[]{:S(2)}, u32[]{:S(2)}) collective-permute-start(bf16[8,3584]{1,0:T(8,128)(2,1)S(1)} %fusion.5), channel_id=1, source_target_pairs={{0,24},{8,0},{16,8},{24,16},{1,25},{9,1},{17,9},{25,17},{2,26},{10... | collective-permute-start | bytes 172040 | tf_op jit(solution)/shard_map/ppermute | solution.py:14
  62.0 1.7 %collective-permute-done.1 = bf16[8,3584]{1,0:T(8,128)(2,1)S(1)} collective-permute-done((bf16[8,3584]{1,0:T(8,128)(2,1)S(1)}, bf16[8,3584]{1,0:T(8,128)(2,1)S(1)}, u32[]{:S(2)}, u32[]{:S(2)}) %collective-permute-start.1) | collective-permute-done | bytes 57376 | tf_op jit(solution)/shard_map/ppermute | solution.py:14
  65.7 3.4 %all-to-all-start.6 = ((bf16[8,4,3584]{2,1,0:T(4,128)(2,1)}), bf16[8,4,3584]{2,1,0:T(4,128)(2,1)S(1)}, u32[]{:S(2)}, u32[]{:S(2)}) async-start(bf16[8,4,3584]{2,1,0:T(4,128)(2,1)} %bitcast.40), calls=%async_computation.6 | async-start | bytes 458752 | tf_op jit(solution)/shard_map/all_to_all | solution.py:86
  69.3 17.1 %all-reduce = (f32[4]{0:T(128)S(1)}, f32[4]{0:T(128)S(1)}) all-reduce(f32[4]{0:T(128)S(1)} %add.101, f32[4]{0:T(128)S(1)} %add.100), channel_id=1, replica_groups=mesh['pipe'=4,'expert'=8] {'expert'}, use_global_device_ids=true, to_apply=%region_33.34 | all-reduce | flops 8 | bytes 64 | tf_op jit(solution)/shard_map/psum | solution.py:125
  87.4 3.4 %all-to-all-start.2 = ((bf16[8,4,3584]{2,1,0:T(4,128)(2,1)}), bf16[8,4,3584]{2,1,0:T(4,128)(2,1)S(1)}, u32[]{:S(2)}, u32[]{:S(2)}) async-start(bf16[8,4,3584]{2,1,0:T(4,128)(2,1)} %bitcast.18), calls=%async_computation.2 | async-start | bytes 458752 | tf_op jit(solution)/shard_map/all_to_all | solution.py:86
  90.9 4.6 %convolution_convert_fusion = bf16[32,3584]{1,0:T(8,128)(2,1)S(1)} fusion(bf16[2,1,512,3584]{3,2,1,0:T(8,128)(2,1)} %param.10, bf16[32,3584]{1,0:T(8,128)(2,1)S(1)} %reshape.224, bf16[2,1,3584,512]{3,2,1,0:T(8,128)(2,1)} %param.9), kind=kOutput, calls=%fused_computation | convolution fusion | flops 235077632 | bytes 7798784 | tf_op jit(solution)/shard_map/dot_general | solution.py:66
  96.2 3.6 %all-to-all-done.2 = bf16[8,4,3584]{2,1,0:T(4,128)(2,1)S(1)} async-done(((bf16[8,4,3584]{2,1,0:T(4,128)(2,1)}), bf16[8,4,3584]{2,1,0:T(4,128)(2,1)S(1)}, u32[]{:S(2)}, u32[]{:S(2)}) %all-to-all-start.2) | async-done | bytes 229408 | tf_op jit(solution)/shard_map/all_to_all | solution.py:86
  99.8 3.4 %all-to-all-start.7 = ((bf16[8,4,3584]{2,1,0:T(4,128)(2,1)}), bf16[8,4,3584]{2,1,0:T(4,128)(2,1)S(1)}, u32[]{:S(2)}, u32[]{:S(2)}) async-start(bf16[8,4,3584]{2,1,0:T(4,128)(2,1)} %reshape.225), calls=%async_computation.7 | async-start | bytes 458752 | tf_op jit(solution)/shard_map/all_to_all | solution.py:84
  103.2 4.6 %convolution_convert_fusion.2 = bf16[32,3584]{1,0:T(8,128)(2,1)S(1)} fusion(bf16[2,1,512,3584]{3,2,1,0:T(8,128)(2,1)} %param.10, bf16[32,3584]{1,0:T(8,128)(2,1)S(1)} %reshape.218, bf16[2,1,3584,512]{3,2,1,0:T(8,128)(2,1)} %param.9), kind=kOutput, calls=%fused_computation.2 | convolution fusion | flops 235077632 | bytes 7798784 | tf_op jit(solution)/shard_map/dot_general | solution.py:66
  108.6 3.5 %all-to-all-done.7 = bf16[8,4,3584]{2,1,0:T(4,128)(2,1)S(1)} async-done(((bf16[8,4,3584]{2,1,0:T(4,128)(2,1)}), bf16[8,4,3584]{2,1,0:T(4,128)(2,1)S(1)}, u32[]{:S(2)}, u32[]{:S(2)}) %all-to-all-start.7) | async-done | bytes 229408 | tf_op jit(solution)/shard_map/all_to_all | solution.py:84
  112.1 3.4 %all-to-all-start.3 = ((bf16[8,4,3584]{2,1,0:T(4,128)(2,1)}), bf16[8,4,3584]{2,1,0:T(4,128)(2,1)S(1)}, u32[]{:S(2)}, u32[]{:S(2)}) async-start(bf16[8,4,3584]{2,1,0:T(4,128)(2,1)} %reshape.219), calls=%async_computation.3 | async-start | bytes 458752 | tf_op jit(solution)/shard_map/all_to_all | solution.py:84
  115.6 10.7 %psum.23 = f32[4,4]{1,0:T(4,128)S(1)} all-reduce(f32[4,4]{1,0:T(4,128)S(1)} %multiply_add_fusion), channel_id=1, replica_groups=mesh['pipe'=4,'expert'=8] {'pipe'}, use_global_device_ids=true, to_apply=%region_34.35 | all-reduce | flops 16 | bytes 128 | tf_op jit(solution)/shard_map/psum | solution.py:127
  127.1 1.1 fusion.9
  128.2 1.1 fusion.8
  (65 shorter events, 10.8 us)
Async XLA Ops:
  5.5 15.4 %all-to-all-start = ((bf16[8,4,3584]{2,1,0:T(4,128)(2,1)}), bf16[8,4,3584]{2,1,0:T(4,128)(2,1)S(1)}, u32[]{:S(2)}, u32[]{:S(2)}) async-start(bf16[8,4,3584]{2,1,0:T(4,128)(2,1)} %bitcast.8), calls=%async_computation | async-start | bytes 458752 | tf_op jit(solution)/shard_map/all_to_all | solution.py:86
  21.6 12.4 %all-to-all-start.4 = ((bf16[8,4,3584]{2,1,0:T(4,128)(2,1)}), bf16[8,4,3584]{2,1,0:T(4,128)(2,1)S(1)}, u32[]{:S(2)}, u32[]{:S(2)}) async-start(bf16[8,4,3584]{2,1,0:T(4,128)(2,1)} %bitcast.30), calls=%async_computation.4 | async-start | bytes 458752 | tf_op jit(solution)/shard_map/all_to_all | solution.py:86
  29.7 20.2 %copy-start = (bf16[1,8,3584]{2,1,0:T(8,128)(2,1)S(1)}, bf16[1,8,3584]{2,1,0:T(8,128)(2,1)}, u32[]{:S(2)}) copy-start(bf16[1,8,3584]{2,1,0:T(8,128)(2,1)} %param.6) | copy-start | bytes 172036
  29.7 29.1 %copy-start.1 = (bf16[1,8,3584]{2,1,0:T(8,128)(2,1)S(1)}, bf16[1,8,3584]{2,1,0:T(8,128)(2,1)}, u32[]{:S(2)}) copy-start(bf16[1,8,3584]{2,1,0:T(8,128)(2,1)} %param.7) | copy-start | bytes 172036
  29.7 34.1 %copy-start.2 = (bf16[2,1,3584,4]{2,3,1,0:T(4,128)(2,1)S(1)}, bf16[2,1,3584,4]{2,3,1,0:T(4,128)(2,1)}, u32[]{:S(2)}) copy-start(bf16[2,1,3584,4]{2,3,1,0:T(4,128)(2,1)} %param.11) | copy-start | bytes 172036
  34.0 12.4 %all-to-all-start.1 = ((bf16[8,4,3584]{2,1,0:T(4,128)(2,1)}), bf16[8,4,3584]{2,1,0:T(4,128)(2,1)S(1)}, u32[]{:S(2)}, u32[]{:S(2)}) async-start(bf16[8,4,3584]{2,1,0:T(4,128)(2,1)} %reshape.216), calls=%async_computation.1 | async-start | bytes 458752 | tf_op jit(solution)/shard_map/all_to_all | solution.py:84
  46.4 12.4 %all-to-all-start.5 = ((bf16[8,4,3584]{2,1,0:T(4,128)(2,1)}), bf16[8,4,3584]{2,1,0:T(4,128)(2,1)S(1)}, u32[]{:S(2)}, u32[]{:S(2)}) async-start(bf16[8,4,3584]{2,1,0:T(4,128)(2,1)} %reshape.222), calls=%async_computation.5 | async-start | bytes 458752 | tf_op jit(solution)/shard_map/all_to_all | solution.py:84
  50.4 11.4 %collective-permute-start = (bf16[8,3584]{1,0:T(8,128)(2,1)S(1)}, bf16[8,3584]{1,0:T(8,128)(2,1)S(1)}, u32[]{:S(2)}, u32[]{:S(2)}) collective-permute-start(bf16[8,3584]{1,0:T(8,128)(2,1)S(1)} %fusion.7), channel_id=1, source_target_pairs={{0,8},{8,16},{16,24},{24,0},{1,9},{9,17},{17,25},{25,1},{2,10},{10... | collective-permute-start | bytes 172040 | tf_op jit(solution)/shard_map/ppermute | solution.py:14
  59.4 4.3 %collective-permute-start.1 = (bf16[8,3584]{1,0:T(8,128)(2,1)S(1)}, bf16[8,3584]{1,0:T(8,128)(2,1)S(1)}, u32[]{:S(2)}, u32[]{:S(2)}) collective-permute-start(bf16[8,3584]{1,0:T(8,128)(2,1)S(1)} %fusion.5), channel_id=1, source_target_pairs={{0,24},{8,0},{16,8},{24,16},{1,25},{9,1},{17,9},{25,17},{2,26},{10... | collective-permute-start | bytes 172040 | tf_op jit(solution)/shard_map/ppermute | solution.py:14
  65.7 20.9 %all-to-all-start.6 = ((bf16[8,4,3584]{2,1,0:T(4,128)(2,1)}), bf16[8,4,3584]{2,1,0:T(4,128)(2,1)S(1)}, u32[]{:S(2)}, u32[]{:S(2)}) async-start(bf16[8,4,3584]{2,1,0:T(4,128)(2,1)} %bitcast.40), calls=%async_computation.6 | async-start | bytes 458752 | tf_op jit(solution)/shard_map/all_to_all | solution.py:86
  87.4 12.4 %all-to-all-start.2 = ((bf16[8,4,3584]{2,1,0:T(4,128)(2,1)}), bf16[8,4,3584]{2,1,0:T(4,128)(2,1)S(1)}, u32[]{:S(2)}, u32[]{:S(2)}) async-start(bf16[8,4,3584]{2,1,0:T(4,128)(2,1)} %bitcast.18), calls=%async_computation.2 | async-start | bytes 458752 | tf_op jit(solution)/shard_map/all_to_all | solution.py:86
  99.8 12.4 %all-to-all-start.7 = ((bf16[8,4,3584]{2,1,0:T(4,128)(2,1)}), bf16[8,4,3584]{2,1,0:T(4,128)(2,1)S(1)}, u32[]{:S(2)}, u32[]{:S(2)}) async-start(bf16[8,4,3584]{2,1,0:T(4,128)(2,1)} %reshape.225), calls=%async_computation.7 | async-start | bytes 458752 | tf_op jit(solution)/shard_map/all_to_all | solution.py:84
  112.1 14.9 %all-to-all-start.3 = ((bf16[8,4,3584]{2,1,0:T(4,128)(2,1)}), bf16[8,4,3584]{2,1,0:T(4,128)(2,1)S(1)}, u32[]{:S(2)}, u32[]{:S(2)}) async-start(bf16[8,4,3584]{2,1,0:T(4,128)(2,1)} %reshape.219), calls=%async_computation.3 | async-start | bytes 458752 | tf_op jit(solution)/shard_map/all_to_all | solution.py:84
where the time goes:
time: 131 us; the launch traced here: 129 us
  starting transfers between devices  34.2 us (26%)
  waiting for transfers between devices  28.2 us (22%)
  blocking collectives  27.8 us (21%)
  matrix products  26.5 us (20%)
  local copies, waits for them, and re-layouts  6.97 us (5%)
  other arithmetic  4.74 us (4%)
    dot_general x4, matrix products, expert_rows(): jnp.dot(hidden, lower_weight, preferred_element_type=jnp.float32)  18.4 us
    psum x1, blocking collectives, shards(): totals = lax.psum((masses[0], masses[1]), 'expert')  17.1 us
    all_to_all x4, starting transfers between devices, send_apart(): lax.all_to_all(outgoing, 'expert', split_axis=0, concat_axis=0, tiled=True)  16.5 us
    all_to_all x4, waiting for transfers between devices, send_apart(): lax.all_to_all(expert_rows(lax.all_to_all(outgoing, 'expert', split_axis=...  13.8 us
    all_to_all x4, starting transfers between devices, send_apart(): lax.all_to_all(expert_rows(lax.all_to_all(outgoing, 'expert', split_axis=...  13.6 us
    all_to_all x4, waiting for transfers between devices, send_apart(): lax.all_to_all(outgoing, 'expert', split_axis=0, concat_axis=0, tiled=True)  12.7 us
    psum x1, blocking collectives, shards(): load_table = lax.psum(spread_table, 'pipe')  10.7 us
    ppermute x2, starting transfers between devices, from_behind(): lax.ppermute(array, axis, [(i, (i + by) % length) for i in range(length)])  4.07 us
  transfers between devices with their start and end apart: 10, of which 7 were waited for; matrix products, arithmetic and copies ran while one was open for 21% of the time, Pallas kernels for 0%

commit v1 on v0

v1 whole, which is shorter than its diff:
```python
import functools

import jax
import jax.numpy as jnp
from jax import lax
from jax.experimental import pallas as pl
from jax.experimental.pallas import tpu as pltpu
from jax.sharding import PartitionSpec as P

TICKS = 2


EPS = 1e-06

LANES = 128

STREAMS = 2

EARLY_FLOPS = 2 * 10**10

TABLE_ROWS = 64


def in_hbm(array):
    return pltpu.with_memory_space_constraint(array, pltpu.HBM)


def in_vmem(array):
    return pltpu.with_memory_space_constraint(array, pltpu.VMEM)


def call(
    body, outs, name, flops=0, size=0, in_specs=None, out_specs=None, scratch=(), inputs=0, held=()
):
    more = {}
    if held:
        in_specs = [pl.BlockSpec(memory_space=pltpu.VMEM)] * (inputs + len(held))

        def whole_body(*refs):
            body(*refs[:inputs], *refs[inputs + len(held) :])

        result = call(whole_body, outs, name, flops, size, in_specs, out_specs, scratch)
        return lambda *operands: result(*operands, *[in_vmem(value) for value in held])
    if in_specs is not None:
        more["in_specs"] = in_specs
    if out_specs is not None:
        more["out_specs"] = out_specs
    return pl.pallas_call(
        body,
        out_shape=outs,
        name=name,
        scratch_shapes=scratch,
        cost_estimate=pl.CostEstimate(flops=flops, bytes_accessed=size, transcendentals=0),
        compiler_params=pltpu.CompilerParams(vmem_limit_bytes=8 << 20),
        **more,
    )


def lane_ids(rows, width=LANES):
    return lax.broadcasted_iota(jnp.int32, (rows, width), 1)


def is_even(place, shape):
    return (lax.broadcasted_iota(jnp.int32, shape, 0) * 0 + place) % 2 == 0


def upright(row):
    n = row.shape[1]
    square = jnp.broadcast_to(row, (n, n))
    diagonal = lax.broadcasted_iota(jnp.int32, (n, n), 0) == lax.broadcasted_iota(
        jnp.int32, (n, n), 1
    )
    return jnp.sum(jnp.where(diagonal, square, 0.0), axis=1, keepdims=True)


def normalize(x):
    wide = x.astype(jnp.float32)
    return (wide * lax.rsqrt(jnp.mean(wide * wide, axis=-1, keepdims=True) + EPS)).astype(
        jnp.bfloat16
    )


def chosen_by(picks):
    return [upright(picks[i : i + 1, :].astype(jnp.float32)).astype(jnp.int32) for i in range(2)]


def place_rows(chosen, mine, rows, capacity):
    lanes = lane_ids(rows)
    rows_at = lax.broadcasted_iota(jnp.int32, (rows, LANES), 0)
    kind = lanes // capacity
    named = ((chosen[0] ^ mine) == kind) | ((chosen[1] ^ mine) == kind)
    named_f = jnp.where(named, 1.0, 0.0)
    before = jnp.zeros((rows, LANES), jnp.float32)
    for r in range(rows - 1):
        before = before + jnp.where(rows_at > r, named_f[r : r + 1, :], 0.0)
    slot = named & (before == (lanes % capacity).astype(jnp.float32))
    return jnp.where(slot, 1.0, 0.0)


def pack_rows(place, normed, slots):
    return jnp.dot(
        place.T[:slots].astype(jnp.bfloat16), normed, preferred_element_type=jnp.float32
    )


def gate_rows(normed, router, chosen, place, me, mine, experts, capacity, spare):
    rows = normed.shape[0]
    wide = normed.astype(jnp.float32)
    taken = [jnp.zeros((rows, 1), jnp.float32) for _ in range(2)]
    for e in range(experts):
        affinity = jax.nn.sigmoid(
            jnp.sum(wide * router[e : e + 1, :].astype(jnp.float32), axis=1, keepdims=True)
        )
        taken = [jnp.where(pick == e, affinity, old) for pick, old in zip(chosen, taken)]
    whole = taken[0] + taken[1]
    shares = [taken[0] / whole, taken[1] / whole]
    kind = lane_ids(rows) // capacity
    share_at = jnp.where((chosen[0] ^ mine) == kind, shares[0], 0.0) + jnp.where(
        (chosen[1] ^ mine) == kind, shares[1], 0.0
    )
    spread = lane_ids(rows, spare)
    masses = []
    for shift in (0, experts):
        base = me * 2 * experts + shift
        here = jnp.where(spread == chosen[0] + base, shares[0], 0.0)
        here = here + jnp.where(spread == chosen[1] + base, shares[1], 0.0)
        masses.append(jnp.sum(here, axis=0, keepdims=True))
    return place * share_at, jnp.concatenate(masses)


def carry_masses(masses):
    top = masses.astype(jnp.bfloat16).astype(jnp.float32)
    return top[:1] + (masses - top)[1:]


def store_blocks(packed, block_refs, capacity):
    features = packed[0].shape[1]
    for k, block_ref in enumerate(block_refs):
        rows = [part[k * capacity : (k + 1) * capacity] for part in packed]
        block_ref[:, :features] = jnp.concatenate(rows).astype(jnp.bfloat16)


def prepare_body(group, experts, capacity, *refs):
    sources, me_ref = refs[:4], refs[4]
    block_refs = refs[5 : 5 + experts]
    x_ref, normed_ref, place_ref, router_ref, routes_ref, sems = refs[5 + experts :]
    targets = [x_ref.at[0], x_ref.at[1], router_ref, routes_ref]
    copies = [
        pltpu.make_async_copy(source, target, sems.at[i])
        for i, (source, target) in enumerate(zip(sources, targets))
    ]
    for copy in copies:
        copy.start()
    mine = lax.div(me_ref[0, 0], group)
    rows = x_ref.shape[1]
    copies[3].wait()
    places = [
        place_rows(chosen_by(routes_ref[0, stream]), mine, rows, capacity)
        for stream in range(STREAMS)
    ]
    for copy in copies[:3]:
        copy.wait()
    packed = []
    for stream in range(STREAMS):
        normed = normalize(x_ref[stream])
        normed_ref[stream] = normed
        place_ref[stream] = places[stream]
        packed.append(pack_rows(places[stream], normed, experts * capacity))
    store_blocks(packed, block_refs, capacity)


def prepare(inputs, group, capacity):
    x, _, router, routes, _ = inputs
    rows, features = x.shape
    experts = router.shape[1]
    both = jax.ShapeDtypeStruct((STREAMS, rows, features), jnp.bfloat16)
    outs = [
        jax.ShapeDtypeStruct((STREAMS * capacity, features), jnp.bfloat16) for _ in range(experts)
    ]
    outs += [
        both,
        both,
        jax.ShapeDtypeStruct((STREAMS, rows, LANES), jnp.float32),
        jax.ShapeDtypeStruct(router.shape, router.dtype),
        jax.ShapeDtypeStruct(routes.shape, routes.dtype),
    ]
    result = call(
        functools.partial(prepare_body, group, experts, capacity),
        outs,
        "prepare",
        EARLY_FLOPS,
        4 * rows * features,
        [pl.BlockSpec(memory_space=pl.ANY)] * 4 + [pl.BlockSpec(memory_space=pltpu.VMEM)],
        None,
        [pltpu.SemaphoreType.DMA((4,))],
    )(*[in_hbm(value) for value in inputs[:4]], inputs[4])
    return result[:experts], result[experts:]


def gates_body(group, experts, capacity, spare, *refs):
    normed_ref, place_ref, router_ref, routes_ref, me_ref = refs[:5]
    coefficient_ref, mass_ref, next_ref = refs[5:]
    me = me_ref[0, 0]
    mine = lax.div(me, group)
    rows = normed_ref.shape[1]
    for stream in range(STREAMS):
        coefficient_ref[stream], mass_ref[stream] = gate_rows(
            normed_ref[stream],
            router_ref[stream],
            chosen_by(routes_ref[0, stream]),
            place_ref[stream],
            me,
            mine,
            experts,
            capacity,
            spare,
        )
        next_ref[stream] = place_rows(chosen_by(routes_ref[1, stream]), mine, rows, capacity)


def gates(normed, place, router, routes, me, group, capacity, spare):
    experts = router.shape[1]
    outs = [
        jax.ShapeDtypeStruct(place.shape, jnp.float32),
        jax.ShapeDtypeStruct((STREAMS, 2, spare), jnp.float32),
        jax.ShapeDtypeStruct(place.shape, jnp.float32),
    ]
    return call(
        functools.partial(gates_body, group, experts, capacity, spare),
        outs,
        "gates",
        32 * normed.size,
        4 * normed.size,
    )(normed, place, router, routes, me)


def repeat_body(group, experts, capacity, spare, *refs):
    far_ref, near_ref, place_ref, router_ref, routes_ref, old_ref, me_ref = refs[:7]
    block_refs = refs[7 : 7 + experts]
    x_ref, coefficient_ref = refs[7 + experts :]
    me = me_ref[0, 0]
    mine = lax.div(me, group)
    far, near = far_ref[...], near_ref[...]
    features = near.shape[1]
    even = is_even(me_ref[0, 1], near.shape)
    xs = [jnp.where(even, far, near), jnp.where(even, near, far)]
    packed, carried = [], []
    for stream in range(STREAMS):
        x_ref[stream] = xs[stream]
        normed = normalize(xs[stream])
        packed.append(pack_rows(place_ref[stream], normed, experts * capacity))
        coefficient, masses = gate_rows(
            normed,
            router_ref[stream],
            chosen_by(routes_ref[1, stream]),
            place_ref[stream],
            me,
            mine,
            experts,
            capacity,
            spare,
        )
        coefficient_ref[stream] = coefficient
        carried.append(
            jnp.broadcast_to(carry_masses(masses + old_ref[stream]), (capacity, spare))
        )
    store_blocks(packed, block_refs, capacity)
    carried = jnp.concatenate(carried).astype(jnp.bfloat16)
    for block_ref in block_refs:
        block_ref[:, features:] = carried


def repeat(inputs, group, capacity, spare, held):
    near, place, router = inputs[1:4]
    rows, features = near.shape
    experts = router.shape[1]
    outs = [
        jax.ShapeDtypeStruct((STREAMS * capacity, features + spare), jnp.bfloat16)
        for _ in range(experts)
    ]
    outs += [
        jax.ShapeDtypeStruct((STREAMS, rows, features), jnp.bfloat16),
        jax.ShapeDtypeStruct(place.shape, jnp.float32),
    ]
    result = call(
        functools.partial(repeat_body, group, experts, capacity, spare),
        outs,
        "prepare",
        512 * rows * features,
        4 * rows * features,
        inputs=len(inputs),
        held=held,
    )(*inputs)
    return result[:experts], result[experts:]


def order_of(experts):
    return [0, *range(experts - 1, 0, -1)]


def shuffled(parts):
    return [parts[k] for k in order_of(len(parts))]


def arranged(parts):
    order = order_of(len(parts))
    return [parts[order.index(k)] for k in range(len(parts))]


def join_body(capacity, experts, *refs):
    parts, out_ref = arranged(refs[:experts]), refs[-1]
    rows = [part[...].astype(jnp.float32) for part in parts]
    out_ref[...] = jnp.concatenate(
        [
            part[stream * capacity : (stream + 1) * capacity]
            for stream in range(STREAMS)
            for part in rows
        ]
    ).astype(out_ref.dtype)


def join(parts, capacity, after=()):
    shape = (sum(part.shape[0] for part in parts), parts[0].shape[1])
    return call(
        functools.partial(join_body, capacity, len(parts)),
        jax.ShapeDtypeStruct(shape, parts[0].dtype),
        "join",
        0,
        4 * shape[0] * shape[1],
        [pl.BlockSpec(memory_space=pltpu.VMEM)] * (len(parts) + len(after)),
    )(*shuffled(parts), *after)


def expert_body(group, capacity, experts, spare, layers, up_ref, down_ref, *refs):
    refs = list(refs)
    if spare:
        place_ref = refs.pop(0)
    batch_refs = refs[:group]
    out_refs = refs[group : 2 * group]
    features, hidden_width = up_ref.shape[1:]
    block = batch_refs[0].shape[0] // STREAMS
    for stream in range(STREAMS):
        mine = slice(stream * block, (stream + 1) * block)
        rows = jnp.concatenate([ref[mine, :features] for ref in batch_refs])
        raw = jnp.dot(rows, up_ref[stream], preferred_element_type=jnp.float32)
        hidden = jax.nn.silu(raw).astype(jnp.bfloat16)
        value = jnp.dot(hidden, down_ref[stream], preferred_element_type=jnp.float32)
        for h in range(group):
            out_refs[h][mine, :] = value[h * block : (h + 1) * block].astype(jnp.bfloat16)
    if spare:
        table_ref = refs[2 * group]
        place = place_ref[0, 1]
        rows = table_ref.shape[0]
        at = lane_ids(1, spare) % experts
        lanes = lane_ids(rows)
        ladder = lax.broadcasted_iota(jnp.int32, (rows, LANES), 0)
        table = jnp.zeros((rows, LANES), jnp.float32)
        for stream in range(STREAMS):
            total = jnp.zeros((1, spare), jnp.float32)
            for ref in batch_refs:
                values = ref[:, features:].astype(jnp.float32)
                for k in range(experts):
                    row = stream * block + k * capacity
                    total = total + values[row : row + 1]
            row = place if stream == 0 else layers - 1 - place
            for e in range(experts):
                value = jnp.sum(jnp.where(at == e, total, 0.0), axis=1, keepdims=True)
                table = table + jnp.where((ladder == row) & (lanes == e), value, 0.0)
        table_ref[...] = table


def expert_rows(batch, up, down, capacity, experts, spare, place=None, layers=0):
    group = len(batch)
    features, hidden_width = up.shape[1:]
    rows = batch[0].shape[0]
    outs = [jax.ShapeDtypeStruct((rows, features), jnp.bfloat16) for _ in range(group)]
    inputs = [in_vmem(up), in_vmem(down)]
    if spare:
        outs.append(jax.ShapeDtypeStruct((-(-layers // TABLE_ROWS) * TABLE_ROWS, LANES), jnp.float32))
        inputs.append(place)
    inputs += batch
    in_place = pl.BlockSpec(memory_space=pltpu.VMEM)
    return call(
        functools.partial(expert_body, group, capacity, experts, spare, layers),
        outs,
        "experts",
        4 * group * rows * features * hidden_width,
        2 * up.size,
        [in_place] * len(inputs),
    )(*inputs)


def add_body(experts, capacity, *refs):
    parts = refs[:-experts]
    summed = sum(part[...].astype(jnp.float32) for part in parts)
    block = summed.shape[0] // STREAMS
    for k in range(experts):
        refs[len(parts) + k][...] = jnp.concatenate(
            [
                summed[stream * block + k * capacity : stream * block + (k + 1) * capacity]
                for stream in range(STREAMS)
            ]
        ).astype(jnp.bfloat16)


def add_up(parts, experts, capacity, held=()):
    rows, features = parts[0].shape
    outs = [
        jax.ShapeDtypeStruct((rows // experts, features), jnp.bfloat16) for _ in range(experts)
    ]
    return call(
        functools.partial(add_body, experts, capacity),
        outs,
        "add_up",
        0,
        4 * rows * features,
        inputs=len(parts),
        held=held,
    )(*parts)


def finish_body(experts, capacity, scale, x_ref, me_ref, coefficient_ref, *refs):
    parts = [ref[...].astype(jnp.float32) for ref in arranged(refs[:experts])]
    rest = refs[experts:]
    results = []
    for stream in range(STREAMS):
        returned = jnp.concatenate(
            [part[stream * capacity : (stream + 1) * capacity] for part in parts]
        ).astype(jnp.bfloat16)
        coefficient = coefficient_ref[stream, :, : experts * capacity]
        high = coefficient.astype(jnp.bfloat16)
        low = (coefficient - high.astype(jnp.float32)).astype(jnp.bfloat16)
        mixture = jnp.dot(high, returned, preferred_element_type=jnp.float32) + jnp.dot(
            low, returned, preferred_element_type=jnp.float32
        )
        results.append(x_ref[stream].astype(jnp.float32) + mixture)
    if not scale:
        even = is_even(me_ref[0, 1], mixture.shape)
        results = [
            jnp.where(even, results[1], results[0]),
            jnp.where(even, results[0], results[1]),
        ]
    for out_ref, result in zip(rest[-STREAMS - 1 :] if scale else rest, results):
        out_ref[...] = result.astype(out_ref.dtype)
    if scale:
        layers = rest[-1].shape[0]
        table = sum(ref[:layers, :] for ref in rest[: -STREAMS - 1])
        rest[-1][...] = table[:, :experts] / scale


def finish(x, me, coefficient, parts, capacity, layers, tables=(), scale=0.0, held=()):
    experts = len(parts)
    rows, features = coefficient.shape[1], parts[0].shape[1]
    outs = [jax.ShapeDtypeStruct((rows, features), jnp.bfloat16) for _ in range(STREAMS)]
    if scale:
        outs.append(jax.ShapeDtypeStruct((layers, experts), jnp.float32))
    return call(
        functools.partial(finish_body, experts, capacity, scale),
        outs,
        "finish",
        128 * rows * features,
        12 * rows * features,
        inputs=3 + experts + len(tables),
        held=held,
    )(x, me, coefficient, *shuffled(parts), *tables)


class Ring:
    def __init__(self, experts):
        self.pipe = lax.axis_size("pipe")
        self.size = lax.axis_size("expert")
        self.experts = experts
        self.group = self.size // experts

    def across(self, blocks):
        moved = {0: blocks[0]}
        for k in sorted(range(1, self.experts), key=lambda k: -k):
            moved[k] = lax.ppermute(
                blocks[k], "expert", [(j, j ^ (k * self.group)) for j in range(self.size)]
            )
        return [moved[k] for k in range(self.experts)]

    def within(self, array, shift):
        pairs = [
            (j, j // self.group * self.group + (j + shift) % self.group) for j in range(self.size)
        ]
        return lax.ppermute(array, "expert", pairs)

    def far(self, array):
        steps = [(i + 1 if i % 2 else i - 1) % self.pipe for i in range(self.pipe)]
        return lax.ppermute(array, "pipe", list(enumerate(steps)))

    def near(self, array):
        return lax.ppermute(array, "pipe", [(i, i ^ 1) for i in range(self.pipe)])

    def over_sections(self, table):
        if self.pipe & (self.pipe - 1):
            return [lax.psum(table, "pipe")]
        parts = [table]
        step = 1
        while step < self.pipe:
            table = sum(parts[1:], parts[0])[: table.shape[0] if step == 1 else self.pipe]
            moved = lax.ppermute(table, "pipe", [(i, i ^ step) for i in range(self.pipe)])
            parts = [table, moved]
            step *= 2
        return parts


def shards(stream_a, stream_b, routes, up_weight, down_weight, router_weight):
    experts = router_weight.shape[-1]
    ring = Ring(experts)
    rows, features = stream_a.shape[1:]
    capacity = rows * routes.shape[-1] // experts
    me = jnp.stack([lax.axis_index("expert"), lax.axis_index("pipe")]).astype(jnp.int32)[None]
    router = jnp.swapaxes(router_weight[:, 0], 1, 2)
    picks = jnp.swapaxes(routes[:, :, 0], 2, 3)
    spare = -(-2 * experts * ring.size // LANES) * LANES
    tokens_total = 2 * TICKS * rows * ring.size
    up, down = up_weight[:, 0], down_weight[:, 0]
    held = ()
    for step in range(TICKS):
        first, last = step == 0, step == TICKS - 1
        room = spare if last else 0
        if first:
            blocks, others = prepare(
                [stream_a[0], stream_b[0], router, picks, me], ring.group, capacity
            )
            x, normed, slots, router, picks = others
            coefficient, mass, slots = gates(
                normed, slots, router, picks, me, ring.group, capacity, spare
            )
        else:
            blocks, (x, coefficient) = repeat(
                [*moved, slots, router, picks, mass, me], ring.group, capacity, spare, held
            )
        own = join(
            ring.across(blocks),
            capacity,
            [in_vmem(value) for value in held],
        )
        batch = [own] + [ring.within(own, h) for h in range(1, ring.group)]
        values = expert_rows(batch, up, down, capacity, experts, room, me, ring.pipe)
        held = () if last else (up, down)
        back = add_up(
            [values[0]] + [ring.within(values[h], -h) for h in range(1, ring.group)],
            experts,
            capacity,
            held,
        )
        tables = ring.over_sections(values[-1]) if last else ()
        result = finish(
            x,
            me,
            coefficient,
            ring.across(back),
            capacity,
            ring.pipe,
            tables,
            float(tokens_total) if last else 0.0,
            held,
        )
        if not last:
            moved = [ring.far(result[0]), ring.near(result[1])]
    return (result[0][None], result[1][None], result[2])


def solution(mesh):
    return jax.shard_map(
        shards,
        mesh=mesh,
        in_specs=(
            P("pipe", "expert", None),
            P("pipe", "expert", None),
            P(None, None, "pipe", "expert", None),
            P(None, "pipe", None, "expert"),
            P(None, "pipe", "expert", None),
            P(None, "pipe", None, None),
        ),
        out_specs=(P("pipe", "expert", None), P("pipe", "expert", None), P()),
        check_vma=False,
    )
```

time: 131 us -> 57.6 us (0.44); the launches traced: 129 us -> 57.5 us
  blocking collectives: 27.8 us -> 0 us
  matrix products: 26.5 us -> 0 us
  starting transfers between devices: 34.2 us -> 24.2 us
  Pallas kernels: 0 us -> 9.16 us
  local copies, waits for them, and re-layouts: 6.97 us -> 0.01 us
  waiting for transfers between devices: 28.2 us -> 23.3 us
  other arithmetic: 4.74 us -> 0.08 us
    all_to_all x8 -> x0, starting transfers between devices: 30.1 us -> none  [the longest x4 16.5 us: send_apart(): lax.all_to_all(outgoing, 'expert', split_axis=0, concat_axis=0, tiled=True)]
    psum x2 -> x0, blocking collectives: 27.8 us -> none  [the longest x1 17.1 us: shards(): totals = lax.psum((masses[0], masses[1]), 'expert')]
    all_to_all x8 -> x0, waiting for transfers between devices: 26.5 us -> none  [the longest x4 13.8 us: send_apart(): lax.all_to_all(expert_rows(lax.all_to_all(outgoing, 'expert', split_axis=...]
    dot_general x16 -> x0, matrix products: 26.5 us -> none  [the longest x4 18.4 us: expert_rows(): jnp.dot(hidden, lower_weight, preferred_element_type=jnp.float32)]
    ppermute x2 -> x20, waiting for transfers between devices: 1.68 us -> 23.3 us  [the longest x12 12 us: across(): lax.ppermute(blocks[k], 'expert', [(j, j ^ k * self.group) for j in range...]
    ppermute x2 -> x20, starting transfers between devices: 4.07 us -> 24.2 us  [the longest x12 19.1 us: across(): lax.ppermute(blocks[k], 'expert', [(j, j ^ k * self.group) for j in range...]
    pallas_call x0 -> x11, Pallas kernels: none -> 9.16 us  [the longest x2 5.56 us: expert_rows(): call(functools.partial(expert_body, group, capacity, experts, spare, laye...]
    reduce_sum x15 -> x0, other arithmetic: 3.24 us -> none  [the longest x4 2.21 us: normalize(): jnp.mean(widened * widened, axis=-1, keepdims=True) + EPS]
  transfers between devices with their start and end apart: 10 -> 20, of which waited for: 7 -> 14; matrix products, arithmetic and copies ran while one was open for 21% -> 0% of each run, Pallas kernels for 0% -> 1%
where the time goes in v1:
time: 57.6 us; the launch traced here: 57.5 us
  starting transfers between devices  24.2 us (42%)
  waiting for transfers between devices  23.3 us (40%)
  Pallas kernels  9.16 us (16%)
  between operations  0.72 us (1%)
    ppermute x12, starting transfers between devices, across(): lax.ppermute(blocks[k], 'expert', [(j, j ^ k * self.group) for j in range...  19.1 us
    ppermute x12, waiting for transfers between devices, across(): lax.ppermute(blocks[k], 'expert', [(j, j ^ k * self.group) for j in range...  12 us
    pallas_call x2, Pallas kernels, expert_rows(): call(functools.partial(expert_body, group, capacity, experts, spare, laye...  5.56 us
    ppermute x4, waiting for transfers between devices, within(): return lax.ppermute(array, 'expert', pairs)  4.79 us
    ppermute x2, waiting for transfers between devices, over_sections(): lax.ppermute(table, 'pipe', [(i, i ^ step) for i in range(self.pipe)])  2.89 us
    ppermute x1, starting transfers between devices, far(): return lax.ppermute(array, 'pipe', list(enumerate(steps)))  2.52 us
    ppermute x1, waiting for transfers between devices, far(): return lax.ppermute(array, 'pipe', list(enumerate(steps)))  2.42 us
    ppermute x2, starting transfers between devices, over_sections(): lax.ppermute(table, 'pipe', [(i, i ^ step) for i in range(self.pipe)])  1.58 us
  transfers between devices with their start and end apart: 20, of which 14 were waited for; matrix products, arithmetic and copies ran while one was open for 0% of the time, Pallas kernels for 1%

profile of v1, /device:TPU:0, one launch (start us, length us, event | category | flops | bytes accessed | tf_op | source)
XLA Modules:
  0.0 57.5 jit_solution(6917824821307126933)
XLA Ops:
  0.7 1.4 %prepare.2 = (bf16[8,3584]{1,0:T(8,128)(2,1)S(1)}, bf16[8,3584]{1,0:T(8,128)(2,1)S(1)}, bf16[8,3584]{1,0:T(8,128)(2,1)S(1)}, bf16[8,3584]{1,0:T(8,128)(2,1)S(1)}...) custom-call(bf16[8,3584]{1,0:T(8,128)(2,1)} %bitcast.28, ...), custom_call_target="tpu_custom_call" | custom-call | flops 20000000000 | bytes 114688 | tf_op jit(solution)/shard_map/prepare/pallas_call | solution.py:187
  2.1 5.1 %collective-permute-start = (bf16[8,3584]{1,0:T(8,128)(2,1)S(1)}, bf16[8,3584]{1,0:T(8,128)(2,1)S(1)}, u32[]{:S(2)}, u32[]{:S(2)}) collective-permute-start(bf16[8,3584]{1,0:T(8,128)(2,1)S(1)} %get-tuple-element.46), channel_id=1, source_target_pairs={{0,6},{1,7},{2,4},{3,5},{4,2},{5,3},{6,0},{7,1},{8,14},{9,15},{10,... | collective-permute-start | bytes 172040 | tf_op jit(solution)/shard_map/ppermute | solution.py:478
  7.2 0.6 %collective-permute-start.2 = (bf16[8,3584]{1,0:T(8,128)(2,1)S(1)}, bf16[8,3584]{1,0:T(8,128)(2,1)S(1)}, u32[]{:S(2)}, u32[]{:S(2)}) collective-permute-start(bf16[8,3584]{1,0:T(8,128)(2,1)S(1)} %get-tuple-element.48), channel_id=1, source_target_pairs={{0,2},{1,3},{2,0},{3,1},{4,6},{5,7},{6,4},{7,5},{8,10},{9,11},{10,... | collective-permute-start | bytes 172040 | tf_op jit(solution)/shard_map/ppermute | solution.py:478
  7.9 1.8 %collective-permute-done.refs_1_ = bf16[8,3584]{1,0:T(8,128)(2,1)S(1)} collective-permute-done((bf16[8,3584]{1,0:T(8,128)(2,1)S(1)}, bf16[8,3584]{1,0:T(8,128)(2,1)S(1)}, u32[]{:S(2)}, u32[]{:S(2)}) %collective-permute-start) | collective-permute-done | bytes 57376 | tf_op jit(solution)/shard_map/ppermute | solution.py:478
  9.6 2.7 %collective-permute-done.1.refs_2_ = bf16[8,3584]{1,0:T(8,128)(2,1)S(1)} collective-permute-done((bf16[8,3584]{1,0:T(8,128)(2,1)S(1)}, bf16[8,3584]{1,0:T(8,128)(2,1)S(1)}, u32[]{:S(2)}, u32[]{:S(2)}) %collective-permute-start.1) | collective-permute-done | bytes 57376 | tf_op jit(solution)/shard_map/ppermute | solution.py:478
  12.5 1.5 %collective-permute-done.3.refs_1_ = bf16[32,3584]{1,0:T(8,128)(2,1)S(1)} collective-permute-done((bf16[32,3584]{1,0:T(8,128)(2,1)S(1)}, bf16[32,3584]{1,0:T(8,128)(2,1)S(1)}, u32[]{:S(2)}, u32[]{:S(2)}) %collective-permute-start.3) | collective-permute-done | bytes 229408 | tf_op jit(solution)/shard_map/ppermute | solution.py:487
  13.9 2.8 %experts.2 = (bf16[32,3584]{1,0:T(8,128)(2,1)S(1)}, bf16[32,3584]{1,0:T(8,128)(2,1)S(1)}) custom-call(bf16[2,3584,512]{2,1,0:T(8,128)(2,1)S(1)} %bitcast.16, bf16[2,512,3584]{2,1,0:T(8,128)(2,1)S(1)} %bitcast.22, bf16[32,3584]{1,0:T(8,128)(2,1)S(1)} %join.2.refs_0_, bf16[32,3584]{1,0:T(8,128)(2,1)S(1)} %collective-permute-done.3.refs_1_), custom_call_target="tpu_custom_call" | custom-call | flops 469762048 | bytes 7340032 | tf_op jit(solution)/shard_map/experts/pallas_call | solution.py:383
  16.9 1.4 %collective-permute-done.4.refs_1_ = bf16[32,3584]{1,0:T(8,128)(2,1)S(1)} collective-permute-done((bf16[32,3584]{1,0:T(8,128)(2,1)S(1)}, bf16[32,3584]{1,0:T(8,128)(2,1)S(1)}, u32[]{:S(2)}, u32[]{:S(2)}) %collective-permute-start.4) | collective-permute-done | bytes 229408 | tf_op jit(solution)/shard_map/ppermute | solution.py:487
  18.3 2.7 %collective-permute-start.5 = (bf16[8,3584]{1,0:T(8,128)(2,1)S(1)}, bf16[8,3584]{1,0:T(8,128)(2,1)S(1)}, u32[]{:S(2)}, u32[]{:S(2)}) collective-permute-start(bf16[8,3584]{1,0:T(8,128)(2,1)S(1)} %get-tuple-element.52), channel_id=1, source_target_pairs={{0,6},{1,7},{2,4},{3,5},{4,2},{5,3},{6,0},{7,1},{8,14},{9,15},{10,... | collective-permute-start | bytes 172040 | tf_op jit(solution)/shard_map/ppermute | solution.py:478
  21.0 1.8 %collective-permute-start.7 = (bf16[8,3584]{1,0:T(8,128)(2,1)S(1)}, bf16[8,3584]{1,0:T(8,128)(2,1)S(1)}, u32[]{:S(2)}, u32[]{:S(2)}) collective-permute-start(bf16[8,3584]{1,0:T(8,128)(2,1)S(1)} %get-tuple-element.54), channel_id=1, source_target_pairs={{0,2},{1,3},{2,0},{3,1},{4,6},{5,7},{6,4},{7,5},{8,10},{9,11},{10,... | collective-permute-start | bytes 172040 | tf_op jit(solution)/shard_map/ppermute | solution.py:478
  22.8 0.2 gates.1
  23.0 1.9 %collective-permute-done.5.refs_4_ = bf16[8,3584]{1,0:T(8,128)(2,1)S(1)} collective-permute-done((bf16[8,3584]{1,0:T(8,128)(2,1)S(1)}, bf16[8,3584]{1,0:T(8,128)(2,1)S(1)}, u32[]{:S(2)}, u32[]{:S(2)}) %collective-permute-start.5) | collective-permute-done | bytes 57376 | tf_op jit(solution)/shard_map/ppermute | solution.py:478
  25.0 1.9 %collective-permute-done.6.refs_5_ = bf16[8,3584]{1,0:T(8,128)(2,1)S(1)} collective-permute-done((bf16[8,3584]{1,0:T(8,128)(2,1)S(1)}, bf16[8,3584]{1,0:T(8,128)(2,1)S(1)}, u32[]{:S(2)}, u32[]{:S(2)}) %collective-permute-start.6) | collective-permute-done | bytes 57376 | tf_op jit(solution)/shard_map/ppermute | solution.py:478
  26.8 0.3 finish.2
  27.1 2.5 %collective-permute-start.8 = (bf16[8,3584]{1,0:T(8,128)(2,1)S(1)}, bf16[8,3584]{1,0:T(8,128)(2,1)S(1)}, u32[]{:S(2)}, u32[]{:S(2)}) collective-permute-start(bf16[8,3584]{1,0:T(8,128)(2,1)S(1)} %get-tuple-element.55), channel_id=1, source_target_pairs={{0,24},{8,16},{16,8},{24,0},{1,25},{9,17},{17,9},{25,1},{2,26},{10... | collective-permute-start | bytes 172040 | tf_op jit(solution)/shard_map/ppermute | solution.py:491
  29.6 0.5 collective-permute-start.9
  30.2 2.4 %collective-permute-done.8.refs_0_ = bf16[8,3584]{1,0:T(8,128)(2,1)S(1)} collective-permute-done((bf16[8,3584]{1,0:T(8,128)(2,1)S(1)}, bf16[8,3584]{1,0:T(8,128)(2,1)S(1)}, u32[]{:S(2)}, u32[]{:S(2)}) %collective-permute-start.8) | collective-permute-done | bytes 57376 | tf_op jit(solution)/shard_map/ppermute | solution.py:491
  32.6 1.2 %collective-permute-done.9.refs_1_ = bf16[8,3584]{1,0:T(8,128)(2,1)S(1)} collective-permute-done((bf16[8,3584]{1,0:T(8,128)(2,1)S(1)}, bf16[8,3584]{1,0:T(8,128)(2,1)S(1)}, u32[]{:S(2)}, u32[]{:S(2)}) %collective-permute-start.9) | collective-permute-done | bytes 57376 | tf_op jit(solution)/shard_map/ppermute | solution.py:494
  33.8 0.5 prepare.3
  34.3 2.5 %collective-permute-start.10 = (bf16[8,3712]{1,0:T(8,128)(2,1)S(1)}, bf16[8,3712]{1,0:T(8,128)(2,1)S(1)}, u32[]{:S(2)}, u32[]{:S(2)}) collective-permute-start(bf16[8,3712]{1,0:T(8,128)(2,1)S(1)} %get-tuple-element.62), channel_id=1, source_target_pairs={{0,6},{1,7},{2,4},{3,5},{4,2},{5,3},{6,0},{7,1},{8,14},{9,15},{10,... | collective-permute-start | bytes 178184 | tf_op jit(solution)/shard_map/ppermute | solution.py:478
  36.8 2.0 %collective-permute-start.12 = (bf16[8,3712]{1,0:T(8,128)(2,1)S(1)}, bf16[8,3712]{1,0:T(8,128)(2,1)S(1)}, u32[]{:S(2)}, u32[]{:S(2)}) collective-permute-start(bf16[8,3712]{1,0:T(8,128)(2,1)S(1)} %get-tuple-element.64), channel_id=1, source_target_pairs={{0,2},{1,3},{2,0},{3,1},{4,6},{5,7},{6,4},{7,5},{8,10},{9,11},{10,... | collective-permute-start | bytes 178184 | tf_op jit(solution)/shard_map/ppermute | solution.py:478
  38.7 2.0 %collective-permute-done.10.refs_1_ = bf16[8,3712]{1,0:T(8,128)(2,1)S(1)} collective-permute-done((bf16[8,3712]{1,0:T(8,128)(2,1)S(1)}, bf16[8,3712]{1,0:T(8,128)(2,1)S(1)}, u32[]{:S(2)}, u32[]{:S(2)}) %collective-permute-start.10) | collective-permute-done | bytes 59424 | tf_op jit(solution)/shard_map/ppermute | solution.py:478
  40.7 1.5 %collective-permute-done.11.refs_2_ = bf16[8,3712]{1,0:T(8,128)(2,1)S(1)} collective-permute-done((bf16[8,3712]{1,0:T(8,128)(2,1)S(1)}, bf16[8,3712]{1,0:T(8,128)(2,1)S(1)}, u32[]{:S(2)}, u32[]{:S(2)}) %collective-permute-start.11) | collective-permute-done | bytes 59424 | tf_op jit(solution)/shard_map/ppermute | solution.py:478
  42.4 1.5 %collective-permute-done.13.refs_2_ = bf16[32,3712]{1,0:T(8,128)(2,1)S(1)} collective-permute-done((bf16[32,3712]{1,0:T(8,128)(2,1)S(1)}, bf16[32,3712]{1,0:T(8,128)(2,1)S(1)}, u32[]{:S(2)}, u32[]{:S(2)}) %collective-permute-start.13) | collective-permute-done | bytes 237600 | tf_op jit(solution)/shard_map/ppermute | solution.py:487
  43.9 2.8 %experts.3 = (bf16[32,3584]{1,0:T(8,128)(2,1)S(1)}, bf16[32,3584]{1,0:T(8,128)(2,1)S(1)}, f32[64,128]{1,0:T(8,128)S(1)}) custom-call(bf16[2,3584,512]{2,1,0:T(8,128)(2,1)S(1)} %bitcast.21, bf16[2,512,3584]{2,1,0:T(8,128)(2,1)S(1)} %bitcast.27, s32[1,2]{1,0:T(1,128)S(1)} %add_bitcast_fusion.refs_4_.refs_1_.refs_6_.refs_0_.me_ref, ...), custom_call_target="tpu_custom_call" | custom-call | flops 469762048 | bytes 7340032 | tf_op jit(solution)/shard_map/experts/pallas_call | solution.py:383
  46.9 0.9 %collective-permute-start.18 = (f32[64,128]{1,0:T(8,128)S(1)}, f32[64,128]{1,0:T(8,128)S(1)}, u32[]{:S(2)}, u32[]{:S(2)}) collective-permute-start(f32[64,128]{1,0:T(8,128)S(1)} %get-tuple-element.71), channel_id=1, source_target_pairs={{0,8},{8,0},{16,24},{24,16},{1,9},{9,1},{17,25},{25,17},{2,10},{10... | collective-permute-start | bytes 98312 | tf_op jit(solution)/shard_map/ppermute | solution.py:503
  47.7 0.5 collective-permute-done.14.refs_1_
  48.3 2.4 %collective-permute-start.15 = (bf16[8,3584]{1,0:T(8,128)(2,1)S(1)}, bf16[8,3584]{1,0:T(8,128)(2,1)S(1)}, u32[]{:S(2)}, u32[]{:S(2)}) collective-permute-start(bf16[8,3584]{1,0:T(8,128)(2,1)S(1)} %get-tuple-element.68), channel_id=1, source_target_pairs={{0,6},{1,7},{2,4},{3,5},{4,2},{5,3},{6,0},{7,1},{8,14},{9,15},{10,... | collective-permute-start | bytes 172040 | tf_op jit(solution)/shard_map/ppermute | solution.py:478
  50.7 2.1 %collective-permute-start.17 = (bf16[8,3584]{1,0:T(8,128)(2,1)S(1)}, bf16[8,3584]{1,0:T(8,128)(2,1)S(1)}, u32[]{:S(2)}, u32[]{:S(2)}) collective-permute-start(bf16[8,3584]{1,0:T(8,128)(2,1)S(1)} %get-tuple-element.70), channel_id=1, source_target_pairs={{0,2},{1,3},{2,0},{3,1},{4,6},{5,7},{6,4},{7,5},{8,10},{9,11},{10,... | collective-permute-start | bytes 172040 | tf_op jit(solution)/shard_map/ppermute | solution.py:478
  52.8 0.7 %collective-permute-start.19 = (f32[4,128]{1,0:T(4,128)S(1)}, f32[4,128]{1,0:T(4,128)S(1)}, u32[]{:S(2)}, u32[]{:S(2)}) collective-permute-start(f32[4,128]{1,0:T(4,128)S(1)} %slice_add_fusion.refs_4_), channel_id=1, source_target_pairs={{0,16},{8,24},{16,0},{24,8},{1,17},{9,25},{17,1},{25,9},{2,18},{10... | collective-permute-start | bytes 6152 | tf_op jit(solution)/shard_map/ppermute | solution.py:503
  53.5 2.9 %collective-permute-done.19.refs_5_ = f32[4,128]{1,0:T(4,128)S(1)} collective-permute-done((f32[4,128]{1,0:T(4,128)S(1)}, f32[4,128]{1,0:T(4,128)S(1)}, u32[]{:S(2)}, u32[]{:S(2)}) %collective-permute-start.19) | collective-permute-done | bytes 2080 | tf_op jit(solution)/shard_map/ppermute | solution.py:503
  56.6 0.9 %finish.3 = (bf16[8,3584]{1,0:T(8,128)(2,1)}, bf16[8,3584]{1,0:T(8,128)(2,1)}, f32[4,4]{1,0:T(4,128)}) custom-call(bf16[2,8,3584]{2,1,0:T(8,128)(2,1)S(1)} %get-tuple-element.59.x_ref, s32[1,2]{1,0:T(1,128)S(1)} %add_bitcast_fusion.refs_4_.refs_1_.refs_6_.refs_0_.me_ref, f32[2,8,128]{2,1,0:T(8,128)S(1)} %get-tuple-element.60.coefficient_ref, ...), custom_call_target="tpu_custom_call" | custom-call | flops 3670016 | bytes 344064 | tf_op jit(solution)/shard_map/finish/pallas_call | solution.py:457
  (25 shorter events, 1.1 us)
Async XLA Ops:
  0.7 13.2 %copy-start = (bf16[2,1,3584,512]{3,2,1,0:T(8,128)(2,1)S(1)}, bf16[2,1,3584,512]{3,2,1,0:T(8,128)(2,1)}, u32[]{:S(2)}) copy-start(bf16[2,1,3584,512]{3,2,1,0:T(8,128)(2,1)} %param.9) | copy-start | bytes 22020100
  0.7 13.2 %copy-start.1 = (bf16[2,1,512,3584]{3,2,1,0:T(8,128)(2,1)S(1)}, bf16[2,1,512,3584]{3,2,1,0:T(8,128)(2,1)}, u32[]{:S(2)}) copy-start(bf16[2,1,512,3584]{3,2,1,0:T(8,128)(2,1)} %param.10) | copy-start | bytes 22020100
  2.1 7.5 %collective-permute-start = (bf16[8,3584]{1,0:T(8,128)(2,1)S(1)}, bf16[8,3584]{1,0:T(8,128)(2,1)S(1)}, u32[]{:S(2)}, u32[]{:S(2)}) collective-permute-start(bf16[8,3584]{1,0:T(8,128)(2,1)S(1)} %get-tuple-element.46), channel_id=1, source_target_pairs={{0,6},{1,7},{2,4},{3,5},{4,2},{5,3},{6,0},{7,1},{8,14},{9,15},{10,... | collective-permute-start | bytes 172040 | tf_op jit(solution)/shard_map/ppermute | solution.py:478
  7.2 5.1 %collective-permute-start.1 = (bf16[8,3584]{1,0:T(8,128)(2,1)S(1)}, bf16[8,3584]{1,0:T(8,128)(2,1)S(1)}, u32[]{:S(2)}, u32[]{:S(2)}) collective-permute-start(bf16[8,3584]{1,0:T(8,128)(2,1)S(1)} %get-tuple-element.47), channel_id=1, source_target_pairs={{0,4},{1,5},{2,6},{3,7},{4,0},{5,1},{6,2},{7,3},{8,12},{9,13},{10,... | collective-permute-start | bytes 172040 | tf_op jit(solution)/shard_map/ppermute | solution.py:478
  7.2 5.1 %collective-permute-start.2 = (bf16[8,3584]{1,0:T(8,128)(2,1)S(1)}, bf16[8,3584]{1,0:T(8,128)(2,1)S(1)}, u32[]{:S(2)}, u32[]{:S(2)}) collective-permute-start(bf16[8,3584]{1,0:T(8,128)(2,1)S(1)} %get-tuple-element.48), channel_id=1, source_target_pairs={{0,2},{1,3},{2,0},{3,1},{4,6},{5,7},{6,4},{7,5},{8,10},{9,11},{10,... | collective-permute-start | bytes 172040 | tf_op jit(solution)/shard_map/ppermute | solution.py:478
  12.4 1.6 %collective-permute-start.3 = (bf16[32,3584]{1,0:T(8,128)(2,1)S(1)}, bf16[32,3584]{1,0:T(8,128)(2,1)S(1)}, u32[]{:S(2)}, u32[]{:S(2)}) collective-permute-start(bf16[32,3584]{1,0:T(8,128)(2,1)S(1)} %join.2.refs_0_), channel_id=1, source_target_pairs={{0,1},{1,0},{2,3},{3,2},{4,5},{5,4},{6,7},{7,6},{8,9},{9,8},{10,11... | collective-permute-start | bytes 688136 | tf_op jit(solution)/shard_map/ppermute | solution.py:487
  16.7 1.5 %collective-permute-start.4 = (bf16[32,3584]{1,0:T(8,128)(2,1)S(1)}, bf16[32,3584]{1,0:T(8,128)(2,1)S(1)}, u32[]{:S(2)}, u32[]{:S(2)}) collective-permute-start(bf16[32,3584]{1,0:T(8,128)(2,1)S(1)} %get-tuple-element.50), channel_id=1, source_target_pairs={{0,1},{1,0},{2,3},{3,2},{4,5},{5,4},{6,7},{7,6},{8,9},{9,8},{10,11... | collective-permute-start | bytes 688136 | tf_op jit(solution)/shard_map/ppermute | solution.py:487
  18.3 6.6 %collective-permute-start.5 = (bf16[8,3584]{1,0:T(8,128)(2,1)S(1)}, bf16[8,3584]{1,0:T(8,128)(2,1)S(1)}, u32[]{:S(2)}, u32[]{:S(2)}) collective-permute-start(bf16[8,3584]{1,0:T(8,128)(2,1)S(1)} %get-tuple-element.52), channel_id=1, source_target_pairs={{0,6},{1,7},{2,4},{3,5},{4,2},{5,3},{6,0},{7,1},{8,14},{9,15},{10,... | collective-permute-start | bytes 172040 | tf_op jit(solution)/shard_map/ppermute | solution.py:478
  21.0 5.8 %collective-permute-start.6 = (bf16[8,3584]{1,0:T(8,128)(2,1)S(1)}, bf16[8,3584]{1,0:T(8,128)(2,1)S(1)}, u32[]{:S(2)}, u32[]{:S(2)}) collective-permute-start(bf16[8,3584]{1,0:T(8,128)(2,1)S(1)} %get-tuple-element.53), channel_id=1, source_target_pairs={{0,4},{1,5},{2,6},{3,7},{4,0},{5,1},{6,2},{7,3},{8,12},{9,13},{10,... | collective-permute-start | bytes 172040 | tf_op jit(solution)/shard_map/ppermute | solution.py:478
  21.0 5.8 %collective-permute-start.7 = (bf16[8,3584]{1,0:T(8,128)(2,1)S(1)}, bf16[8,3584]{1,0:T(8,128)(2,1)S(1)}, u32[]{:S(2)}, u32[]{:S(2)}) collective-permute-start(bf16[8,3584]{1,0:T(8,128)(2,1)S(1)} %get-tuple-element.54), channel_id=1, source_target_pairs={{0,2},{1,3},{2,0},{3,1},{4,6},{5,7},{6,4},{7,5},{8,10},{9,11},{10,... | collective-permute-start | bytes 172040 | tf_op jit(solution)/shard_map/ppermute | solution.py:478
  27.1 5.5 %collective-permute-start.8 = (bf16[8,3584]{1,0:T(8,128)(2,1)S(1)}, bf16[8,3584]{1,0:T(8,128)(2,1)S(1)}, u32[]{:S(2)}, u32[]{:S(2)}) collective-permute-start(bf16[8,3584]{1,0:T(8,128)(2,1)S(1)} %get-tuple-element.55), channel_id=1, source_target_pairs={{0,24},{8,16},{16,8},{24,0},{1,25},{9,17},{17,9},{25,1},{2,26},{10... | collective-permute-start | bytes 172040 | tf_op jit(solution)/shard_map/ppermute | solution.py:491
  29.6 4.2 %collective-permute-start.9 = (bf16[8,3584]{1,0:T(8,128)(2,1)S(1)}, bf16[8,3584]{1,0:T(8,128)(2,1)S(1)}, u32[]{:S(2)}, u32[]{:S(2)}) collective-permute-start(bf16[8,3584]{1,0:T(8,128)(2,1)S(1)} %get-tuple-element.56), channel_id=1, source_target_pairs={{0,8},{8,0},{16,24},{24,16},{1,9},{9,1},{17,25},{25,17},{2,10},{10... | collective-permute-start | bytes 172040 | tf_op jit(solution)/shard_map/ppermute | solution.py:494
  34.3 6.4 %collective-permute-start.10 = (bf16[8,3712]{1,0:T(8,128)(2,1)S(1)}, bf16[8,3712]{1,0:T(8,128)(2,1)S(1)}, u32[]{:S(2)}, u32[]{:S(2)}) collective-permute-start(bf16[8,3712]{1,0:T(8,128)(2,1)S(1)} %get-tuple-element.62), channel_id=1, source_target_pairs={{0,6},{1,7},{2,4},{3,5},{4,2},{5,3},{6,0},{7,1},{8,14},{9,15},{10,... | collective-permute-start | bytes 178184 | tf_op jit(solution)/shard_map/ppermute | solution.py:478
  36.8 5.5 %collective-permute-start.11 = (bf16[8,3712]{1,0:T(8,128)(2,1)S(1)}, bf16[8,3712]{1,0:T(8,128)(2,1)S(1)}, u32[]{:S(2)}, u32[]{:S(2)}) collective-permute-start(bf16[8,3712]{1,0:T(8,128)(2,1)S(1)} %get-tuple-element.63), channel_id=1, source_target_pairs={{0,4},{1,5},{2,6},{3,7},{4,0},{5,1},{6,2},{7,3},{8,12},{9,13},{10,... | collective-permute-start | bytes 178184 | tf_op jit(solution)/shard_map/ppermute | solution.py:478
  36.8 5.5 %collective-permute-start.12 = (bf16[8,3712]{1,0:T(8,128)(2,1)S(1)}, bf16[8,3712]{1,0:T(8,128)(2,1)S(1)}, u32[]{:S(2)}, u32[]{:S(2)}) collective-permute-start(bf16[8,3712]{1,0:T(8,128)(2,1)S(1)} %get-tuple-element.64), channel_id=1, source_target_pairs={{0,2},{1,3},{2,0},{3,1},{4,6},{5,7},{6,4},{7,5},{8,10},{9,11},{10,... | collective-permute-start | bytes 178184 | tf_op jit(solution)/shard_map/ppermute | solution.py:478
  42.3 1.6 %collective-permute-start.13 = (bf16[32,3712]{1,0:T(8,128)(2,1)S(1)}, bf16[32,3712]{1,0:T(8,128)(2,1)S(1)}, u32[]{:S(2)}, u32[]{:S(2)}) collective-permute-start(bf16[32,3712]{1,0:T(8,128)(2,1)S(1)} %join.3.refs_1_), channel_id=1, source_target_pairs={{0,1},{1,0},{2,3},{3,2},{4,5},{5,4},{6,7},{7,6},{8,9},{9,8},{10,11... | collective-permute-start | bytes 712712 | tf_op jit(solution)/shard_map/ppermute | solution.py:487
  46.7 1.5 %collective-permute-start.14 = (bf16[32,3584]{1,0:T(8,128)(2,1)S(1)}, bf16[32,3584]{1,0:T(8,128)(2,1)S(1)}, u32[]{:S(2)}, u32[]{:S(2)}) collective-permute-start(bf16[32,3584]{1,0:T(8,128)(2,1)S(1)} %get-tuple-element.66), channel_id=1, source_target_pairs={{0,1},{1,0},{2,3},{3,2},{4,5},{5,4},{6,7},{7,6},{8,9},{9,8},{10,11... | collective-permute-start | bytes 688136 | tf_op jit(solution)/shard_map/ppermute | solution.py:487
  46.9 5.9 %collective-permute-start.18 = (f32[64,128]{1,0:T(8,128)S(1)}, f32[64,128]{1,0:T(8,128)S(1)}, u32[]{:S(2)}, u32[]{:S(2)}) collective-permute-start(f32[64,128]{1,0:T(8,128)S(1)} %get-tuple-element.71), channel_id=1, source_target_pairs={{0,8},{8,0},{16,24},{24,16},{1,9},{9,1},{17,25},{25,17},{2,10},{10... | collective-permute-start | bytes 98312 | tf_op jit(solution)/shard_map/ppermute | solution.py:503
  48.3 8.1 %collective-permute-start.15 = (bf16[8,3584]{1,0:T(8,128)(2,1)S(1)}, bf16[8,3584]{1,0:T(8,128)(2,1)S(1)}, u32[]{:S(2)}, u32[]{:S(2)}) collective-permute-start(bf16[8,3584]{1,0:T(8,128)(2,1)S(1)} %get-tuple-element.68), channel_id=1, source_target_pairs={{0,6},{1,7},{2,4},{3,5},{4,2},{5,3},{6,0},{7,1},{8,14},{9,15},{10,... | collective-permute-start | bytes 172040 | tf_op jit(solution)/shard_map/ppermute | solution.py:478
  50.7 5.9 %collective-permute-start.16 = (bf16[8,3584]{1,0:T(8,128)(2,1)S(1)}, bf16[8,3584]{1,0:T(8,128)(2,1)S(1)}, u32[]{:S(2)}, u32[]{:S(2)}) collective-permute-start(bf16[8,3584]{1,0:T(8,128)(2,1)S(1)} %get-tuple-element.69), channel_id=1, source_target_pairs={{0,4},{1,5},{2,6},{3,7},{4,0},{5,1},{6,2},{7,3},{8,12},{9,13},{10,... | collective-permute-start | bytes 172040 | tf_op jit(solution)/shard_map/ppermute | solution.py:478
  50.7 5.9 %collective-permute-start.17 = (bf16[8,3584]{1,0:T(8,128)(2,1)S(1)}, bf16[8,3584]{1,0:T(8,128)(2,1)S(1)}, u32[]{:S(2)}, u32[]{:S(2)}) collective-permute-start(bf16[8,3584]{1,0:T(8,128)(2,1)S(1)} %get-tuple-element.70), channel_id=1, source_target_pairs={{0,2},{1,3},{2,0},{3,1},{4,6},{5,7},{6,4},{7,5},{8,10},{9,11},{10,... | collective-permute-start | bytes 172040 | tf_op jit(solution)/shard_map/ppermute | solution.py:478
  52.8 3.6 %collective-permute-start.19 = (f32[4,128]{1,0:T(4,128)S(1)}, f32[4,128]{1,0:T(4,128)S(1)}, u32[]{:S(2)}, u32[]{:S(2)}) collective-permute-start(f32[4,128]{1,0:T(4,128)S(1)} %slice_add_fusion.refs_4_), channel_id=1, source_target_pairs={{0,16},{8,24},{16,0},{24,8},{1,17},{9,25},{17,1},{25,9},{2,18},{10... | collective-permute-start | bytes 6152 | tf_op jit(solution)/shard_map/ppermute | solution.py:503

commit v2 on v1

--- a/solution.py
+++ b/solution.py
@@ -294,21 +294,21 @@
     return result[:experts], result[experts:]
 
 
-def order_of(experts):
-    return [0, *range(experts - 1, 0, -1)]
-
-
-def shuffled(parts):
-    return [parts[k] for k in order_of(len(parts))]
-
-
-def arranged(parts):
-    order = order_of(len(parts))
+def order_of(experts, out):
+    return [0, *range(2, experts), 1] if out else [0, *range(experts - 1, 0, -1)]
+
+
+def shuffled(parts, out):
+    return [parts[k] for k in order_of(len(parts), out)]
+
+
+def arranged(parts, out):
+    order = order_of(len(parts), out)
     return [parts[order.index(k)] for k in range(len(parts))]
 
 
 def join_body(capacity, experts, *refs):
-    parts, out_ref = arranged(refs[:experts]), refs[-1]
+    parts, out_ref = arranged(refs[:experts], True), refs[-1]
     rows = [part[...].astype(jnp.float32) for part in parts]
     out_ref[...] = jnp.concatenate(
         [
@@ -328,7 +328,7 @@
         0,
         4 * shape[0] * shape[1],
         [pl.BlockSpec(memory_space=pltpu.VMEM)] * (len(parts) + len(after)),
-    )(*shuffled(parts), *after)
+    )(*shuffled(parts, True), *after)
 
 
 def expert_body(group, capacity, experts, spare, layers, up_ref, down_ref, *refs):
@@ -420,7 +420,7 @@
 
 
 def finish_body(experts, capacity, scale, x_ref, me_ref, coefficient_ref, *refs):
-    parts = [ref[...].astype(jnp.float32) for ref in arranged(refs[:experts])]
+    parts = [ref[...].astype(jnp.float32) for ref in arranged(refs[:experts], False)]
     rest = refs[experts:]
     results = []
     for stream in range(STREAMS):
@@ -462,7 +462,7 @@
         12 * rows * features,
         inputs=3 + experts + len(tables),
         held=held,
-    )(x, me, coefficient, *shuffled(parts), *tables)
+    )(x, me, coefficient, *shuffled(parts, False), *tables)
 
 
 class Ring:

time: 57.6 us -> 57.6 us (level)
  starting transfers between devices: 24.2 us -> 22.9 us
  waiting for transfers between devices: 23.3 us -> 24.6 us
    ppermute x12, starting transfers between devices: 19.1 us -> 18.1 us  [across(): lax.ppermute(blocks[k], 'expert', [(j, j ^ k * self.group) for j in range...]
    ppermute x12, waiting for transfers between devices: 12 us -> 12.9 us  [across(): lax.ppermute(blocks[k], 'expert', [(j, j ^ k * self.group) for j in range...]
  transfers between devices with their start and end apart: 20 -> 20, of which waited for: 14 -> 16; matrix products, arithmetic and copies ran while one was open for 0% -> 0% of each run, Pallas kernels for 1% -> 1%
where the time goes in v2:
time: 57.6 us; the launch traced here: 57.4 us
  waiting for transfers between devices  24.6 us (43%)
  starting transfers between devices  22.9 us (40%)
  Pallas kernels  9.15 us (16%)
  between operations  0.72 us (1%)
    ppermute x12, starting transfers between devices, across(): lax.ppermute(blocks[k], 'expert', [(j, j ^ k * self.group) for j in range...  18.1 us
    ppermute x12, waiting for transfers between devices, across(): lax.ppermute(blocks[k], 'expert', [(j, j ^ k * self.group) for j in range...  12.9 us
    pallas_call x2, Pallas kernels, expert_rows(): call(functools.partial(expert_body, group, capacity, experts, spare, laye...  5.56 us
    ppermute x4, waiting for transfers between devices, within(): return lax.ppermute(array, 'expert', pairs)  4.98 us
    ppermute x2, waiting for transfers between devices, over_sections(): lax.ppermute(table, 'pipe', [(i, i ^ step) for i in range(self.pipe)])  3.08 us
    ppermute x1, starting transfers between devices, far(): return lax.ppermute(array, 'pipe', list(enumerate(steps)))  2.51 us
    ppermute x1, waiting for transfers between devices, far(): return lax.ppermute(array, 'pipe', list(enumerate(steps)))  2.45 us
    pallas_call x1, Pallas kernels, prepare(): call(functools.partial(prepare_body, group, experts, capacity), outs, 'pr...  1.38 us
  transfers between devices with their start and end apart: 20, of which 16 were waited for; matrix products, arithmetic and copies ran while one was open for 0% of the time, Pallas kernels for 1%

profile of v2, /device:TPU:0, one launch (start us, length us, event | category | flops | bytes accessed | tf_op | source)
XLA Modules:
  0.0 57.4 jit_solution(12075677057696280188)
XLA Ops:
  0.7 1.4 %prepare.2 = (bf16[8,3584]{1,0:T(8,128)(2,1)S(1)}, bf16[8,3584]{1,0:T(8,128)(2,1)S(1)}, bf16[8,3584]{1,0:T(8,128)(2,1)S(1)}, bf16[8,3584]{1,0:T(8,128)(2,1)S(1)}...) custom-call(bf16[8,3584]{1,0:T(8,128)(2,1)} %bitcast.28, ...), custom_call_target="tpu_custom_call" | custom-call | flops 20000000000 | bytes 114688 | tf_op jit(solution)/shard_map/prepare/pallas_call | solution.py:187
  2.1 4.1 %collective-permute-start = (bf16[8,3584]{1,0:T(8,128)(2,1)S(1)}, bf16[8,3584]{1,0:T(8,128)(2,1)S(1)}, u32[]{:S(2)}, u32[]{:S(2)}) collective-permute-start(bf16[8,3584]{1,0:T(8,128)(2,1)S(1)} %get-tuple-element.46), channel_id=1, source_target_pairs={{0,4},{1,5},{2,6},{3,7},{4,0},{5,1},{6,2},{7,3},{8,12},{9,13},{10,... | collective-permute-start | bytes 172040 | tf_op jit(solution)/shard_map/ppermute | solution.py:478
  6.2 1.3 %collective-permute-start.1 = (bf16[8,3584]{1,0:T(8,128)(2,1)S(1)}, bf16[8,3584]{1,0:T(8,128)(2,1)S(1)}, u32[]{:S(2)}, u32[]{:S(2)}) collective-permute-start(bf16[8,3584]{1,0:T(8,128)(2,1)S(1)} %get-tuple-element.47), channel_id=1, source_target_pairs={{0,6},{1,7},{2,4},{3,5},{4,2},{5,3},{6,0},{7,1},{8,14},{9,15},{10,... | collective-permute-start | bytes 172040 | tf_op jit(solution)/shard_map/ppermute | solution.py:478
  7.8 1.2 %collective-permute-done.refs_1_ = bf16[8,3584]{1,0:T(8,128)(2,1)S(1)} collective-permute-done((bf16[8,3584]{1,0:T(8,128)(2,1)S(1)}, bf16[8,3584]{1,0:T(8,128)(2,1)S(1)}, u32[]{:S(2)}, u32[]{:S(2)}) %collective-permute-start) | collective-permute-done | bytes 57376 | tf_op jit(solution)/shard_map/ppermute | solution.py:478
  9.0 3.3 %collective-permute-done.1.refs_2_ = bf16[8,3584]{1,0:T(8,128)(2,1)S(1)} collective-permute-done((bf16[8,3584]{1,0:T(8,128)(2,1)S(1)}, bf16[8,3584]{1,0:T(8,128)(2,1)S(1)}, u32[]{:S(2)}, u32[]{:S(2)}) %collective-permute-start.1) | collective-permute-done | bytes 57376 | tf_op jit(solution)/shard_map/ppermute | solution.py:478
  12.5 1.5 %collective-permute-done.3.refs_1_ = bf16[32,3584]{1,0:T(8,128)(2,1)S(1)} collective-permute-done((bf16[32,3584]{1,0:T(8,128)(2,1)S(1)}, bf16[32,3584]{1,0:T(8,128)(2,1)S(1)}, u32[]{:S(2)}, u32[]{:S(2)}) %collective-permute-start.3) | collective-permute-done | bytes 229408 | tf_op jit(solution)/shard_map/ppermute | solution.py:487
  14.0 2.8 %experts.2 = (bf16[32,3584]{1,0:T(8,128)(2,1)S(1)}, bf16[32,3584]{1,0:T(8,128)(2,1)S(1)}) custom-call(bf16[2,3584,512]{2,1,0:T(8,128)(2,1)S(1)} %bitcast.16, bf16[2,512,3584]{2,1,0:T(8,128)(2,1)S(1)} %bitcast.22, bf16[32,3584]{1,0:T(8,128)(2,1)S(1)} %join.2.refs_0_, bf16[32,3584]{1,0:T(8,128)(2,1)S(1)} %collective-permute-done.3.refs_1_), custom_call_target="tpu_custom_call" | custom-call | flops 469762048 | bytes 7340032 | tf_op jit(solution)/shard_map/experts/pallas_call | solution.py:383
  16.9 1.4 %collective-permute-done.4.refs_1_ = bf16[32,3584]{1,0:T(8,128)(2,1)S(1)} collective-permute-done((bf16[32,3584]{1,0:T(8,128)(2,1)S(1)}, bf16[32,3584]{1,0:T(8,128)(2,1)S(1)}, u32[]{:S(2)}, u32[]{:S(2)}) %collective-permute-start.4) | collective-permute-done | bytes 229408 | tf_op jit(solution)/shard_map/ppermute | solution.py:487
  18.4 2.6 %collective-permute-start.5 = (bf16[8,3584]{1,0:T(8,128)(2,1)S(1)}, bf16[8,3584]{1,0:T(8,128)(2,1)S(1)}, u32[]{:S(2)}, u32[]{:S(2)}) collective-permute-start(bf16[8,3584]{1,0:T(8,128)(2,1)S(1)} %get-tuple-element.52), channel_id=1, source_target_pairs={{0,6},{1,7},{2,4},{3,5},{4,2},{5,3},{6,0},{7,1},{8,14},{9,15},{10,... | collective-permute-start | bytes 172040 | tf_op jit(solution)/shard_map/ppermute | solution.py:478
  21.0 1.8 %collective-permute-start.7 = (bf16[8,3584]{1,0:T(8,128)(2,1)S(1)}, bf16[8,3584]{1,0:T(8,128)(2,1)S(1)}, u32[]{:S(2)}, u32[]{:S(2)}) collective-permute-start(bf16[8,3584]{1,0:T(8,128)(2,1)S(1)} %get-tuple-element.54), channel_id=1, source_target_pairs={{0,2},{1,3},{2,0},{3,1},{4,6},{5,7},{6,4},{7,5},{8,10},{9,11},{10,... | collective-permute-start | bytes 172040 | tf_op jit(solution)/shard_map/ppermute | solution.py:478
  23.1 1.9 %collective-permute-done.5.refs_4_ = bf16[8,3584]{1,0:T(8,128)(2,1)S(1)} collective-permute-done((bf16[8,3584]{1,0:T(8,128)(2,1)S(1)}, bf16[8,3584]{1,0:T(8,128)(2,1)S(1)}, u32[]{:S(2)}, u32[]{:S(2)}) %collective-permute-start.5) | collective-permute-done | bytes 57376 | tf_op jit(solution)/shard_map/ppermute | solution.py:478
  25.0 1.9 %collective-permute-done.6.refs_5_ = bf16[8,3584]{1,0:T(8,128)(2,1)S(1)} collective-permute-done((bf16[8,3584]{1,0:T(8,128)(2,1)S(1)}, bf16[8,3584]{1,0:T(8,128)(2,1)S(1)}, u32[]{:S(2)}, u32[]{:S(2)}) %collective-permute-start.6) | collective-permute-done | bytes 57376 | tf_op jit(solution)/shard_map/ppermute | solution.py:478
  27.2 2.5 %collective-permute-start.8 = (bf16[8,3584]{1,0:T(8,128)(2,1)S(1)}, bf16[8,3584]{1,0:T(8,128)(2,1)S(1)}, u32[]{:S(2)}, u32[]{:S(2)}) collective-permute-start(bf16[8,3584]{1,0:T(8,128)(2,1)S(1)} %get-tuple-element.55), channel_id=1, source_target_pairs={{0,24},{8,16},{16,8},{24,0},{1,25},{9,17},{17,9},{25,1},{2,26},{10... | collective-permute-start | bytes 172040 | tf_op jit(solution)/shard_map/ppermute | solution.py:491
  29.7 0.5 collective-permute-start.9
  30.2 2.5 %collective-permute-done.8.refs_0_ = bf16[8,3584]{1,0:T(8,128)(2,1)S(1)} collective-permute-done((bf16[8,3584]{1,0:T(8,128)(2,1)S(1)}, bf16[8,3584]{1,0:T(8,128)(2,1)S(1)}, u32[]{:S(2)}, u32[]{:S(2)}) %collective-permute-start.8) | collective-permute-done | bytes 57376 | tf_op jit(solution)/shard_map/ppermute | solution.py:491
  32.7 1.2 %collective-permute-done.9.refs_1_ = bf16[8,3584]{1,0:T(8,128)(2,1)S(1)} collective-permute-done((bf16[8,3584]{1,0:T(8,128)(2,1)S(1)}, bf16[8,3584]{1,0:T(8,128)(2,1)S(1)}, u32[]{:S(2)}, u32[]{:S(2)}) %collective-permute-start.9) | collective-permute-done | bytes 57376 | tf_op jit(solution)/shard_map/ppermute | solution.py:494
  33.8 0.5 prepare.3
  34.3 1.3 %collective-permute-start.10 = (bf16[8,3712]{1,0:T(8,128)(2,1)S(1)}, bf16[8,3712]{1,0:T(8,128)(2,1)S(1)}, u32[]{:S(2)}, u32[]{:S(2)}) collective-permute-start(bf16[8,3712]{1,0:T(8,128)(2,1)S(1)} %get-tuple-element.62), channel_id=1, source_target_pairs={{0,4},{1,5},{2,6},{3,7},{4,0},{5,1},{6,2},{7,3},{8,12},{9,13},{10,... | collective-permute-start | bytes 178184 | tf_op jit(solution)/shard_map/ppermute | solution.py:478
  35.6 1.7 %collective-permute-start.11 = (bf16[8,3712]{1,0:T(8,128)(2,1)S(1)}, bf16[8,3712]{1,0:T(8,128)(2,1)S(1)}, u32[]{:S(2)}, u32[]{:S(2)}) collective-permute-start(bf16[8,3712]{1,0:T(8,128)(2,1)S(1)} %get-tuple-element.63), channel_id=1, source_target_pairs={{0,6},{1,7},{2,4},{3,5},{4,2},{5,3},{6,0},{7,1},{8,14},{9,15},{10,... | collective-permute-start | bytes 178184 | tf_op jit(solution)/shard_map/ppermute | solution.py:478
  37.3 0.5 collective-permute-start.12
  37.9 2.6 %collective-permute-done.10.refs_1_ = bf16[8,3712]{1,0:T(8,128)(2,1)S(1)} collective-permute-done((bf16[8,3712]{1,0:T(8,128)(2,1)S(1)}, bf16[8,3712]{1,0:T(8,128)(2,1)S(1)}, u32[]{:S(2)}, u32[]{:S(2)}) %collective-permute-start.10) | collective-permute-done | bytes 59424 | tf_op jit(solution)/shard_map/ppermute | solution.py:478
  40.5 1.3 %collective-permute-done.11.refs_2_ = bf16[8,3712]{1,0:T(8,128)(2,1)S(1)} collective-permute-done((bf16[8,3712]{1,0:T(8,128)(2,1)S(1)}, bf16[8,3712]{1,0:T(8,128)(2,1)S(1)}, u32[]{:S(2)}, u32[]{:S(2)}) %collective-permute-start.11) | collective-permute-done | bytes 59424 | tf_op jit(solution)/shard_map/ppermute | solution.py:478
  41.8 0.4 collective-permute-done.12.refs_3_
  42.3 1.5 %collective-permute-done.13.refs_2_ = bf16[32,3712]{1,0:T(8,128)(2,1)S(1)} collective-permute-done((bf16[32,3712]{1,0:T(8,128)(2,1)S(1)}, bf16[32,3712]{1,0:T(8,128)(2,1)S(1)}, u32[]{:S(2)}, u32[]{:S(2)}) %collective-permute-start.13) | collective-permute-done | bytes 237600 | tf_op jit(solution)/shard_map/ppermute | solution.py:487
  43.8 2.8 %experts.3 = (bf16[32,3584]{1,0:T(8,128)(2,1)S(1)}, bf16[32,3584]{1,0:T(8,128)(2,1)S(1)}, f32[64,128]{1,0:T(8,128)S(1)}) custom-call(bf16[2,3584,512]{2,1,0:T(8,128)(2,1)S(1)} %bitcast.21, bf16[2,512,3584]{2,1,0:T(8,128)(2,1)S(1)} %bitcast.27, s32[1,2]{1,0:T(1,128)S(1)} %add_bitcast_fusion.refs_4_.refs_1_.refs_6_.refs_0_.me_ref, ...), custom_call_target="tpu_custom_call" | custom-call | flops 469762048 | bytes 7340032 | tf_op jit(solution)/shard_map/experts/pallas_call | solution.py:383
  46.8 0.7 %collective-permute-start.18 = (f32[64,128]{1,0:T(8,128)S(1)}, f32[64,128]{1,0:T(8,128)S(1)}, u32[]{:S(2)}, u32[]{:S(2)}) collective-permute-start(f32[64,128]{1,0:T(8,128)S(1)} %get-tuple-element.71), channel_id=1, source_target_pairs={{0,8},{8,0},{16,24},{24,16},{1,9},{9,1},{17,25},{25,17},{2,10},{10... | collective-permute-start | bytes 98312 | tf_op jit(solution)/shard_map/ppermute | solution.py:503
  47.5 0.7 %collective-permute-done.14.refs_1_ = bf16[32,3584]{1,0:T(8,128)(2,1)S(1)} collective-permute-done((bf16[32,3584]{1,0:T(8,128)(2,1)S(1)}, bf16[32,3584]{1,0:T(8,128)(2,1)S(1)}, u32[]{:S(2)}, u32[]{:S(2)}) %collective-permute-start.14) | collective-permute-done | bytes 229408 | tf_op jit(solution)/shard_map/ppermute | solution.py:487
  48.2 2.0 %collective-permute-start.15 = (bf16[8,3584]{1,0:T(8,128)(2,1)S(1)}, bf16[8,3584]{1,0:T(8,128)(2,1)S(1)}, u32[]{:S(2)}, u32[]{:S(2)}) collective-permute-start(bf16[8,3584]{1,0:T(8,128)(2,1)S(1)} %get-tuple-element.68), channel_id=1, source_target_pairs={{0,6},{1,7},{2,4},{3,5},{4,2},{5,3},{6,0},{7,1},{8,14},{9,15},{10,... | collective-permute-start | bytes 172040 | tf_op jit(solution)/shard_map/ppermute | solution.py:478
  50.2 2.5 %collective-permute-start.17 = (bf16[8,3584]{1,0:T(8,128)(2,1)S(1)}, bf16[8,3584]{1,0:T(8,128)(2,1)S(1)}, u32[]{:S(2)}, u32[]{:S(2)}) collective-permute-start(bf16[8,3584]{1,0:T(8,128)(2,1)S(1)} %get-tuple-element.70), channel_id=1, source_target_pairs={{0,2},{1,3},{2,0},{3,1},{4,6},{5,7},{6,4},{7,5},{8,10},{9,11},{10,... | collective-permute-start | bytes 172040 | tf_op jit(solution)/shard_map/ppermute | solution.py:478
  52.7 0.5 collective-permute-start.19
  53.2 3.1 %collective-permute-done.19.refs_5_ = f32[4,128]{1,0:T(4,128)S(1)} collective-permute-done((f32[4,128]{1,0:T(4,128)S(1)}, f32[4,128]{1,0:T(4,128)S(1)}, u32[]{:S(2)}, u32[]{:S(2)}) %collective-permute-start.19) | collective-permute-done | bytes 2080 | tf_op jit(solution)/shard_map/ppermute | solution.py:503
  56.5 0.9 %finish.3 = (bf16[8,3584]{1,0:T(8,128)(2,1)}, bf16[8,3584]{1,0:T(8,128)(2,1)}, f32[4,4]{1,0:T(4,128)}) custom-call(bf16[2,8,3584]{2,1,0:T(8,128)(2,1)S(1)} %get-tuple-element.59.x_ref, s32[1,2]{1,0:T(1,128)S(1)} %add_bitcast_fusion.refs_4_.refs_1_.refs_6_.refs_0_.me_ref, f32[2,8,128]{2,1,0:T(8,128)S(1)} %get-tuple-element.60.coefficient_ref, ...), custom_call_target="tpu_custom_call" | custom-call | flops 3670016 | bytes 344064 | tf_op jit(solution)/shard_map/finish/pallas_call | solution.py:457
  (25 shorter events, 1.9 us)
Async XLA Ops:
  0.7 13.3 %copy-start = (bf16[2,1,3584,512]{3,2,1,0:T(8,128)(2,1)S(1)}, bf16[2,1,3584,512]{3,2,1,0:T(8,128)(2,1)}, u32[]{:S(2)}) copy-start(bf16[2,1,3584,512]{3,2,1,0:T(8,128)(2,1)} %param.9) | copy-start | bytes 22020100
  0.7 13.3 %copy-start.1 = (bf16[2,1,512,3584]{3,2,1,0:T(8,128)(2,1)S(1)}, bf16[2,1,512,3584]{3,2,1,0:T(8,128)(2,1)}, u32[]{:S(2)}) copy-start(bf16[2,1,512,3584]{3,2,1,0:T(8,128)(2,1)} %param.10) | copy-start | bytes 22020100
  2.1 6.9 %collective-permute-start = (bf16[8,3584]{1,0:T(8,128)(2,1)S(1)}, bf16[8,3584]{1,0:T(8,128)(2,1)S(1)}, u32[]{:S(2)}, u32[]{:S(2)}) collective-permute-start(bf16[8,3584]{1,0:T(8,128)(2,1)S(1)} %get-tuple-element.46), channel_id=1, source_target_pairs={{0,4},{1,5},{2,6},{3,7},{4,0},{5,1},{6,2},{7,3},{8,12},{9,13},{10,... | collective-permute-start | bytes 172040 | tf_op jit(solution)/shard_map/ppermute | solution.py:478
  6.2 6.1 %collective-permute-start.1 = (bf16[8,3584]{1,0:T(8,128)(2,1)S(1)}, bf16[8,3584]{1,0:T(8,128)(2,1)S(1)}, u32[]{:S(2)}, u32[]{:S(2)}) collective-permute-start(bf16[8,3584]{1,0:T(8,128)(2,1)S(1)} %get-tuple-element.47), channel_id=1, source_target_pairs={{0,6},{1,7},{2,4},{3,5},{4,2},{5,3},{6,0},{7,1},{8,14},{9,15},{10,... | collective-permute-start | bytes 172040 | tf_op jit(solution)/shard_map/ppermute | solution.py:478
  7.6 4.8 %collective-permute-start.2 = (bf16[8,3584]{1,0:T(8,128)(2,1)S(1)}, bf16[8,3584]{1,0:T(8,128)(2,1)S(1)}, u32[]{:S(2)}, u32[]{:S(2)}) collective-permute-start(bf16[8,3584]{1,0:T(8,128)(2,1)S(1)} %get-tuple-element.48), channel_id=1, source_target_pairs={{0,2},{1,3},{2,0},{3,1},{4,6},{5,7},{6,4},{7,5},{8,10},{9,11},{10,... | collective-permute-start | bytes 172040 | tf_op jit(solution)/shard_map/ppermute | solution.py:478
  12.4 1.6 %collective-permute-start.3 = (bf16[32,3584]{1,0:T(8,128)(2,1)S(1)}, bf16[32,3584]{1,0:T(8,128)(2,1)S(1)}, u32[]{:S(2)}, u32[]{:S(2)}) collective-permute-start(bf16[32,3584]{1,0:T(8,128)(2,1)S(1)} %join.2.refs_0_), channel_id=1, source_target_pairs={{0,1},{1,0},{2,3},{3,2},{4,5},{5,4},{6,7},{7,6},{8,9},{9,8},{10,11... | collective-permute-start | bytes 688136 | tf_op jit(solution)/shard_map/ppermute | solution.py:487
  16.8 1.5 %collective-permute-start.4 = (bf16[32,3584]{1,0:T(8,128)(2,1)S(1)}, bf16[32,3584]{1,0:T(8,128)(2,1)S(1)}, u32[]{:S(2)}, u32[]{:S(2)}) collective-permute-start(bf16[32,3584]{1,0:T(8,128)(2,1)S(1)} %get-tuple-element.50), channel_id=1, source_target_pairs={{0,1},{1,0},{2,3},{3,2},{4,5},{5,4},{6,7},{7,6},{8,9},{9,8},{10,11... | collective-permute-start | bytes 688136 | tf_op jit(solution)/shard_map/ppermute | solution.py:487
  18.4 6.6 %collective-permute-start.5 = (bf16[8,3584]{1,0:T(8,128)(2,1)S(1)}, bf16[8,3584]{1,0:T(8,128)(2,1)S(1)}, u32[]{:S(2)}, u32[]{:S(2)}) collective-permute-start(bf16[8,3584]{1,0:T(8,128)(2,1)S(1)} %get-tuple-element.52), channel_id=1, source_target_pairs={{0,6},{1,7},{2,4},{3,5},{4,2},{5,3},{6,0},{7,1},{8,14},{9,15},{10,... | collective-permute-start | bytes 172040 | tf_op jit(solution)/shard_map/ppermute | solution.py:478
  21.0 5.9 %collective-permute-start.6 = (bf16[8,3584]{1,0:T(8,128)(2,1)S(1)}, bf16[8,3584]{1,0:T(8,128)(2,1)S(1)}, u32[]{:S(2)}, u32[]{:S(2)}) collective-permute-start(bf16[8,3584]{1,0:T(8,128)(2,1)S(1)} %get-tuple-element.53), channel_id=1, source_target_pairs={{0,4},{1,5},{2,6},{3,7},{4,0},{5,1},{6,2},{7,3},{8,12},{9,13},{10,... | collective-permute-start | bytes 172040 | tf_op jit(solution)/shard_map/ppermute | solution.py:478
  21.0 5.9 %collective-permute-start.7 = (bf16[8,3584]{1,0:T(8,128)(2,1)S(1)}, bf16[8,3584]{1,0:T(8,128)(2,1)S(1)}, u32[]{:S(2)}, u32[]{:S(2)}) collective-permute-start(bf16[8,3584]{1,0:T(8,128)(2,1)S(1)} %get-tuple-element.54), channel_id=1, source_target_pairs={{0,2},{1,3},{2,0},{3,1},{4,6},{5,7},{6,4},{7,5},{8,10},{9,11},{10,... | collective-permute-start | bytes 172040 | tf_op jit(solution)/shard_map/ppermute | solution.py:478
  27.2 5.5 %collective-permute-start.8 = (bf16[8,3584]{1,0:T(8,128)(2,1)S(1)}, bf16[8,3584]{1,0:T(8,128)(2,1)S(1)}, u32[]{:S(2)}, u32[]{:S(2)}) collective-permute-start(bf16[8,3584]{1,0:T(8,128)(2,1)S(1)} %get-tuple-element.55), channel_id=1, source_target_pairs={{0,24},{8,16},{16,8},{24,0},{1,25},{9,17},{17,9},{25,1},{2,26},{10... | collective-permute-start | bytes 172040 | tf_op jit(solution)/shard_map/ppermute | solution.py:491
  29.7 4.2 %collective-permute-start.9 = (bf16[8,3584]{1,0:T(8,128)(2,1)S(1)}, bf16[8,3584]{1,0:T(8,128)(2,1)S(1)}, u32[]{:S(2)}, u32[]{:S(2)}) collective-permute-start(bf16[8,3584]{1,0:T(8,128)(2,1)S(1)} %get-tuple-element.56), channel_id=1, source_target_pairs={{0,8},{8,0},{16,24},{24,16},{1,9},{9,1},{17,25},{25,17},{2,10},{10... | collective-permute-start | bytes 172040 | tf_op jit(solution)/shard_map/ppermute | solution.py:494
  34.3 6.1 %collective-permute-start.10 = (bf16[8,3712]{1,0:T(8,128)(2,1)S(1)}, bf16[8,3712]{1,0:T(8,128)(2,1)S(1)}, u32[]{:S(2)}, u32[]{:S(2)}) collective-permute-start(bf16[8,3712]{1,0:T(8,128)(2,1)S(1)} %get-tuple-element.62), channel_id=1, source_target_pairs={{0,4},{1,5},{2,6},{3,7},{4,0},{5,1},{6,2},{7,3},{8,12},{9,13},{10,... | collective-permute-start | bytes 178184 | tf_op jit(solution)/shard_map/ppermute | solution.py:478
  35.6 6.2 %collective-permute-start.11 = (bf16[8,3712]{1,0:T(8,128)(2,1)S(1)}, bf16[8,3712]{1,0:T(8,128)(2,1)S(1)}, u32[]{:S(2)}, u32[]{:S(2)}) collective-permute-start(bf16[8,3712]{1,0:T(8,128)(2,1)S(1)} %get-tuple-element.63), channel_id=1, source_target_pairs={{0,6},{1,7},{2,4},{3,5},{4,2},{5,3},{6,0},{7,1},{8,14},{9,15},{10,... | collective-permute-start | bytes 178184 | tf_op jit(solution)/shard_map/ppermute | solution.py:478
  37.3 4.8 %collective-permute-start.12 = (bf16[8,3712]{1,0:T(8,128)(2,1)S(1)}, bf16[8,3712]{1,0:T(8,128)(2,1)S(1)}, u32[]{:S(2)}, u32[]{:S(2)}) collective-permute-start(bf16[8,3712]{1,0:T(8,128)(2,1)S(1)} %get-tuple-element.64), channel_id=1, source_target_pairs={{0,2},{1,3},{2,0},{3,1},{4,6},{5,7},{6,4},{7,5},{8,10},{9,11},{10,... | collective-permute-start | bytes 178184 | tf_op jit(solution)/shard_map/ppermute | solution.py:478
  42.3 1.6 %collective-permute-start.13 = (bf16[32,3712]{1,0:T(8,128)(2,1)S(1)}, bf16[32,3712]{1,0:T(8,128)(2,1)S(1)}, u32[]{:S(2)}, u32[]{:S(2)}) collective-permute-start(bf16[32,3712]{1,0:T(8,128)(2,1)S(1)} %join.3.refs_1_), channel_id=1, source_target_pairs={{0,1},{1,0},{2,3},{3,2},{4,5},{5,4},{6,7},{7,6},{8,9},{9,8},{10,11... | collective-permute-start | bytes 712712 | tf_op jit(solution)/shard_map/ppermute | solution.py:487
  46.6 1.5 %collective-permute-start.14 = (bf16[32,3584]{1,0:T(8,128)(2,1)S(1)}, bf16[32,3584]{1,0:T(8,128)(2,1)S(1)}, u32[]{:S(2)}, u32[]{:S(2)}) collective-permute-start(bf16[32,3584]{1,0:T(8,128)(2,1)S(1)} %get-tuple-element.66), channel_id=1, source_target_pairs={{0,1},{1,0},{2,3},{3,2},{4,5},{5,4},{6,7},{7,6},{8,9},{9,8},{10,11... | collective-permute-start | bytes 688136 | tf_op jit(solution)/shard_map/ppermute | solution.py:487
  46.8 5.9 %collective-permute-start.18 = (f32[64,128]{1,0:T(8,128)S(1)}, f32[64,128]{1,0:T(8,128)S(1)}, u32[]{:S(2)}, u32[]{:S(2)}) collective-permute-start(f32[64,128]{1,0:T(8,128)S(1)} %get-tuple-element.71), channel_id=1, source_target_pairs={{0,8},{8,0},{16,24},{24,16},{1,9},{9,1},{17,25},{25,17},{2,10},{10... | collective-permute-start | bytes 98312 | tf_op jit(solution)/shard_map/ppermute | solution.py:503
  48.2 8.1 %collective-permute-start.15 = (bf16[8,3584]{1,0:T(8,128)(2,1)S(1)}, bf16[8,3584]{1,0:T(8,128)(2,1)S(1)}, u32[]{:S(2)}, u32[]{:S(2)}) collective-permute-start(bf16[8,3584]{1,0:T(8,128)(2,1)S(1)} %get-tuple-element.68), channel_id=1, source_target_pairs={{0,6},{1,7},{2,4},{3,5},{4,2},{5,3},{6,0},{7,1},{8,14},{9,15},{10,... | collective-permute-start | bytes 172040 | tf_op jit(solution)/shard_map/ppermute | solution.py:478
  50.2 6.3 %collective-permute-start.16 = (bf16[8,3584]{1,0:T(8,128)(2,1)S(1)}, bf16[8,3584]{1,0:T(8,128)(2,1)S(1)}, u32[]{:S(2)}, u32[]{:S(2)}) collective-permute-start(bf16[8,3584]{1,0:T(8,128)(2,1)S(1)} %get-tuple-element.69), channel_id=1, source_target_pairs={{0,4},{1,5},{2,6},{3,7},{4,0},{5,1},{6,2},{7,3},{8,12},{9,13},{10,... | collective-permute-start | bytes 172040 | tf_op jit(solution)/shard_map/ppermute | solution.py:478
  50.2 6.3 %collective-permute-start.17 = (bf16[8,3584]{1,0:T(8,128)(2,1)S(1)}, bf16[8,3584]{1,0:T(8,128)(2,1)S(1)}, u32[]{:S(2)}, u32[]{:S(2)}) collective-permute-start(bf16[8,3584]{1,0:T(8,128)(2,1)S(1)} %get-tuple-element.70), channel_id=1, source_target_pairs={{0,2},{1,3},{2,0},{3,1},{4,6},{5,7},{6,4},{7,5},{8,10},{9,11},{10,... | collective-permute-start | bytes 172040 | tf_op jit(solution)/shard_map/ppermute | solution.py:478
  52.7 3.6 %collective-permute-start.19 = (f32[4,128]{1,0:T(4,128)S(1)}, f32[4,128]{1,0:T(4,128)S(1)}, u32[]{:S(2)}, u32[]{:S(2)}) collective-permute-start(f32[4,128]{1,0:T(4,128)S(1)} %slice_add_fusion.refs_4_), channel_id=1, source_target_pairs={{0,16},{8,24},{16,0},{24,8},{1,17},{9,25},{17,1},{25,9},{2,18},{10... | collective-permute-start | bytes 6152 | tf_op jit(solution)/shard_map/ppermute | solution.py:503

commit v3 on v2

--- a/solution.py
+++ b/solution.py
@@ -339,12 +339,15 @@
     out_refs = refs[group : 2 * group]
     features, hidden_width = up_ref.shape[1:]
     block = batch_refs[0].shape[0] // STREAMS
+    hidden = []
     for stream in range(STREAMS):
         mine = slice(stream * block, (stream + 1) * block)
         rows = jnp.concatenate([ref[mine, :features] for ref in batch_refs])
         raw = jnp.dot(rows, up_ref[stream], preferred_element_type=jnp.float32)
-        hidden = jax.nn.silu(raw).astype(jnp.bfloat16)
-        value = jnp.dot(hidden, down_ref[stream], preferred_element_type=jnp.float32)
+        hidden.append(jax.nn.silu(raw).astype(jnp.bfloat16))
+    for stream in range(STREAMS):
+        mine = slice(stream * block, (stream + 1) * block)
+        value = jnp.dot(hidden[stream], down_ref[stream], preferred_element_type=jnp.float32)
         for h in range(group):
             out_refs[h][mine, :] = value[h * block : (h + 1) * block].astype(jnp.bfloat16)
     if spare:

time: 57.6 us -> 57.3 us (level)
  no operation moved by 1% of the time
where the time goes in v3:
time: 57.3 us; the launch traced here: 57.1 us
  waiting for transfers between devices  24.6 us (43%)
  starting transfers between devices  22.9 us (40%)
  Pallas kernels  8.85 us (15%)
  between operations  0.72 us (1%)
    ppermute x12, starting transfers between devices, across(): lax.ppermute(blocks[k], 'expert', [(j, j ^ k * self.group) for j in range...  18.1 us
    ppermute x12, waiting for transfers between devices, across(): lax.ppermute(blocks[k], 'expert', [(j, j ^ k * self.group) for j in range...  12.9 us
    pallas_call x2, Pallas kernels, expert_rows(): call(functools.partial(expert_body, group, capacity, experts, spare, laye...  5.26 us
    ppermute x4, waiting for transfers between devices, within(): return lax.ppermute(array, 'expert', pairs)  4.98 us
    ppermute x2, waiting for transfers between devices, over_sections(): lax.ppermute(table, 'pipe', [(i, i ^ step) for i in range(self.pipe)])  3.08 us
    ppermute x1, starting transfers between devices, far(): return lax.ppermute(array, 'pipe', list(enumerate(steps)))  2.51 us
    ppermute x1, waiting for transfers between devices, far(): return lax.ppermute(array, 'pipe', list(enumerate(steps)))  2.45 us
    pallas_call x1, Pallas kernels, prepare(): call(functools.partial(prepare_body, group, experts, capacity), outs, 'pr...  1.38 us
  transfers between devices with their start and end apart: 20, of which 16 were waited for; matrix products, arithmetic and copies ran while one was open for 0% of the time, Pallas kernels for 1%

profile of v3, /device:TPU:0, one launch (start us, length us, event | category | flops | bytes accessed | tf_op | source)
XLA Modules:
  0.0 57.1 jit_solution(5835500401275339662)
XLA Ops:
  0.7 1.4 %prepare.2 = (bf16[8,3584]{1,0:T(8,128)(2,1)S(1)}, bf16[8,3584]{1,0:T(8,128)(2,1)S(1)}, bf16[8,3584]{1,0:T(8,128)(2,1)S(1)}, bf16[8,3584]{1,0:T(8,128)(2,1)S(1)}...) custom-call(bf16[8,3584]{1,0:T(8,128)(2,1)} %bitcast.28, ...), custom_call_target="tpu_custom_call" | custom-call | flops 20000000000 | bytes 114688 | tf_op jit(solution)/shard_map/prepare/pallas_call | solution.py:187
  2.1 4.1 %collective-permute-start = (bf16[8,3584]{1,0:T(8,128)(2,1)S(1)}, bf16[8,3584]{1,0:T(8,128)(2,1)S(1)}, u32[]{:S(2)}, u32[]{:S(2)}) collective-permute-start(bf16[8,3584]{1,0:T(8,128)(2,1)S(1)} %get-tuple-element.46), channel_id=1, source_target_pairs={{0,4},{1,5},{2,6},{3,7},{4,0},{5,1},{6,2},{7,3},{8,12},{9,13},{10,... | collective-permute-start | bytes 172040 | tf_op jit(solution)/shard_map/ppermute | solution.py:481
  6.2 1.3 %collective-permute-start.1 = (bf16[8,3584]{1,0:T(8,128)(2,1)S(1)}, bf16[8,3584]{1,0:T(8,128)(2,1)S(1)}, u32[]{:S(2)}, u32[]{:S(2)}) collective-permute-start(bf16[8,3584]{1,0:T(8,128)(2,1)S(1)} %get-tuple-element.47), channel_id=1, source_target_pairs={{0,6},{1,7},{2,4},{3,5},{4,2},{5,3},{6,0},{7,1},{8,14},{9,15},{10,... | collective-permute-start | bytes 172040 | tf_op jit(solution)/shard_map/ppermute | solution.py:481
  7.8 1.2 %collective-permute-done.refs_1_ = bf16[8,3584]{1,0:T(8,128)(2,1)S(1)} collective-permute-done((bf16[8,3584]{1,0:T(8,128)(2,1)S(1)}, bf16[8,3584]{1,0:T(8,128)(2,1)S(1)}, u32[]{:S(2)}, u32[]{:S(2)}) %collective-permute-start) | collective-permute-done | bytes 57376 | tf_op jit(solution)/shard_map/ppermute | solution.py:481
  9.0 3.3 %collective-permute-done.1.refs_2_ = bf16[8,3584]{1,0:T(8,128)(2,1)S(1)} collective-permute-done((bf16[8,3584]{1,0:T(8,128)(2,1)S(1)}, bf16[8,3584]{1,0:T(8,128)(2,1)S(1)}, u32[]{:S(2)}, u32[]{:S(2)}) %collective-permute-start.1) | collective-permute-done | bytes 57376 | tf_op jit(solution)/shard_map/ppermute | solution.py:481
  12.5 1.5 %collective-permute-done.3.refs_1_ = bf16[32,3584]{1,0:T(8,128)(2,1)S(1)} collective-permute-done((bf16[32,3584]{1,0:T(8,128)(2,1)S(1)}, bf16[32,3584]{1,0:T(8,128)(2,1)S(1)}, u32[]{:S(2)}, u32[]{:S(2)}) %collective-permute-start.3) | collective-permute-done | bytes 229408 | tf_op jit(solution)/shard_map/ppermute | solution.py:490
  14.0 2.6 %experts.2 = (bf16[32,3584]{1,0:T(8,128)(2,1)S(1)}, bf16[32,3584]{1,0:T(8,128)(2,1)S(1)}) custom-call(bf16[2,3584,512]{2,1,0:T(8,128)(2,1)S(1)} %bitcast.16, bf16[2,512,3584]{2,1,0:T(8,128)(2,1)S(1)} %bitcast.22, bf16[32,3584]{1,0:T(8,128)(2,1)S(1)} %join.2.refs_0_, bf16[32,3584]{1,0:T(8,128)(2,1)S(1)} %collective-permute-done.3.refs_1_), custom_call_target="tpu_custom_call" | custom-call | flops 469762048 | bytes 7340032 | tf_op jit(solution)/shard_map/experts/pallas_call | solution.py:386
  16.8 1.4 %collective-permute-done.4.refs_1_ = bf16[32,3584]{1,0:T(8,128)(2,1)S(1)} collective-permute-done((bf16[32,3584]{1,0:T(8,128)(2,1)S(1)}, bf16[32,3584]{1,0:T(8,128)(2,1)S(1)}, u32[]{:S(2)}, u32[]{:S(2)}) %collective-permute-start.4) | collective-permute-done | bytes 229408 | tf_op jit(solution)/shard_map/ppermute | solution.py:490
  18.2 2.6 %collective-permute-start.5 = (bf16[8,3584]{1,0:T(8,128)(2,1)S(1)}, bf16[8,3584]{1,0:T(8,128)(2,1)S(1)}, u32[]{:S(2)}, u32[]{:S(2)}) collective-permute-start(bf16[8,3584]{1,0:T(8,128)(2,1)S(1)} %get-tuple-element.52), channel_id=1, source_target_pairs={{0,6},{1,7},{2,4},{3,5},{4,2},{5,3},{6,0},{7,1},{8,14},{9,15},{10,... | collective-permute-start | bytes 172040 | tf_op jit(solution)/shard_map/ppermute | solution.py:481
  20.8 1.8 %collective-permute-start.7 = (bf16[8,3584]{1,0:T(8,128)(2,1)S(1)}, bf16[8,3584]{1,0:T(8,128)(2,1)S(1)}, u32[]{:S(2)}, u32[]{:S(2)}) collective-permute-start(bf16[8,3584]{1,0:T(8,128)(2,1)S(1)} %get-tuple-element.54), channel_id=1, source_target_pairs={{0,2},{1,3},{2,0},{3,1},{4,6},{5,7},{6,4},{7,5},{8,10},{9,11},{10,... | collective-permute-start | bytes 172040 | tf_op jit(solution)/shard_map/ppermute | solution.py:481
  22.9 1.9 %collective-permute-done.5.refs_4_ = bf16[8,3584]{1,0:T(8,128)(2,1)S(1)} collective-permute-done((bf16[8,3584]{1,0:T(8,128)(2,1)S(1)}, bf16[8,3584]{1,0:T(8,128)(2,1)S(1)}, u32[]{:S(2)}, u32[]{:S(2)}) %collective-permute-start.5) | collective-permute-done | bytes 57376 | tf_op jit(solution)/shard_map/ppermute | solution.py:481
  24.9 1.9 %collective-permute-done.6.refs_5_ = bf16[8,3584]{1,0:T(8,128)(2,1)S(1)} collective-permute-done((bf16[8,3584]{1,0:T(8,128)(2,1)S(1)}, bf16[8,3584]{1,0:T(8,128)(2,1)S(1)}, u32[]{:S(2)}, u32[]{:S(2)}) %collective-permute-start.6) | collective-permute-done | bytes 57376 | tf_op jit(solution)/shard_map/ppermute | solution.py:481
  27.0 2.5 %collective-permute-start.8 = (bf16[8,3584]{1,0:T(8,128)(2,1)S(1)}, bf16[8,3584]{1,0:T(8,128)(2,1)S(1)}, u32[]{:S(2)}, u32[]{:S(2)}) collective-permute-start(bf16[8,3584]{1,0:T(8,128)(2,1)S(1)} %get-tuple-element.55), channel_id=1, source_target_pairs={{0,24},{8,16},{16,8},{24,0},{1,25},{9,17},{17,9},{25,1},{2,26},{10... | collective-permute-start | bytes 172040 | tf_op jit(solution)/shard_map/ppermute | solution.py:494
  29.5 0.5 collective-permute-start.9
  30.1 2.5 %collective-permute-done.8.refs_0_ = bf16[8,3584]{1,0:T(8,128)(2,1)S(1)} collective-permute-done((bf16[8,3584]{1,0:T(8,128)(2,1)S(1)}, bf16[8,3584]{1,0:T(8,128)(2,1)S(1)}, u32[]{:S(2)}, u32[]{:S(2)}) %collective-permute-start.8) | collective-permute-done | bytes 57376 | tf_op jit(solution)/shard_map/ppermute | solution.py:494
  32.5 1.2 %collective-permute-done.9.refs_1_ = bf16[8,3584]{1,0:T(8,128)(2,1)S(1)} collective-permute-done((bf16[8,3584]{1,0:T(8,128)(2,1)S(1)}, bf16[8,3584]{1,0:T(8,128)(2,1)S(1)}, u32[]{:S(2)}, u32[]{:S(2)}) %collective-permute-start.9) | collective-permute-done | bytes 57376 | tf_op jit(solution)/shard_map/ppermute | solution.py:497
  33.7 0.5 prepare.3
  34.2 1.3 %collective-permute-start.10 = (bf16[8,3712]{1,0:T(8,128)(2,1)S(1)}, bf16[8,3712]{1,0:T(8,128)(2,1)S(1)}, u32[]{:S(2)}, u32[]{:S(2)}) collective-permute-start(bf16[8,3712]{1,0:T(8,128)(2,1)S(1)} %get-tuple-element.62), channel_id=1, source_target_pairs={{0,4},{1,5},{2,6},{3,7},{4,0},{5,1},{6,2},{7,3},{8,12},{9,13},{10,... | collective-permute-start | bytes 178184 | tf_op jit(solution)/shard_map/ppermute | solution.py:481
  35.5 1.7 %collective-permute-start.11 = (bf16[8,3712]{1,0:T(8,128)(2,1)S(1)}, bf16[8,3712]{1,0:T(8,128)(2,1)S(1)}, u32[]{:S(2)}, u32[]{:S(2)}) collective-permute-start(bf16[8,3712]{1,0:T(8,128)(2,1)S(1)} %get-tuple-element.63), channel_id=1, source_target_pairs={{0,6},{1,7},{2,4},{3,5},{4,2},{5,3},{6,0},{7,1},{8,14},{9,15},{10,... | collective-permute-start | bytes 178184 | tf_op jit(solution)/shard_map/ppermute | solution.py:481
  37.2 0.5 collective-permute-start.12
  37.7 2.6 %collective-permute-done.10.refs_1_ = bf16[8,3712]{1,0:T(8,128)(2,1)S(1)} collective-permute-done((bf16[8,3712]{1,0:T(8,128)(2,1)S(1)}, bf16[8,3712]{1,0:T(8,128)(2,1)S(1)}, u32[]{:S(2)}, u32[]{:S(2)}) %collective-permute-start.10) | collective-permute-done | bytes 59424 | tf_op jit(solution)/shard_map/ppermute | solution.py:481
  40.3 1.3 %collective-permute-done.11.refs_2_ = bf16[8,3712]{1,0:T(8,128)(2,1)S(1)} collective-permute-done((bf16[8,3712]{1,0:T(8,128)(2,1)S(1)}, bf16[8,3712]{1,0:T(8,128)(2,1)S(1)}, u32[]{:S(2)}, u32[]{:S(2)}) %collective-permute-start.11) | collective-permute-done | bytes 59424 | tf_op jit(solution)/shard_map/ppermute | solution.py:481
  41.6 0.4 collective-permute-done.12.refs_3_
  42.2 1.5 %collective-permute-done.13.refs_2_ = bf16[32,3712]{1,0:T(8,128)(2,1)S(1)} collective-permute-done((bf16[32,3712]{1,0:T(8,128)(2,1)S(1)}, bf16[32,3712]{1,0:T(8,128)(2,1)S(1)}, u32[]{:S(2)}, u32[]{:S(2)}) %collective-permute-start.13) | collective-permute-done | bytes 237600 | tf_op jit(solution)/shard_map/ppermute | solution.py:490
  43.7 2.6 %experts.3 = (bf16[32,3584]{1,0:T(8,128)(2,1)S(1)}, bf16[32,3584]{1,0:T(8,128)(2,1)S(1)}, f32[64,128]{1,0:T(8,128)S(1)}) custom-call(bf16[2,3584,512]{2,1,0:T(8,128)(2,1)S(1)} %bitcast.21, bf16[2,512,3584]{2,1,0:T(8,128)(2,1)S(1)} %bitcast.27, s32[1,2]{1,0:T(1,128)S(1)} %add_bitcast_fusion.refs_4_.refs_1_.refs_6_.refs_0_.me_ref, ...), custom_call_target="tpu_custom_call" | custom-call | flops 469762048 | bytes 7340032 | tf_op jit(solution)/shard_map/experts/pallas_call | solution.py:386
  46.5 0.7 %collective-permute-start.18 = (f32[64,128]{1,0:T(8,128)S(1)}, f32[64,128]{1,0:T(8,128)S(1)}, u32[]{:S(2)}, u32[]{:S(2)}) collective-permute-start(f32[64,128]{1,0:T(8,128)S(1)} %get-tuple-element.71), channel_id=1, source_target_pairs={{0,8},{8,0},{16,24},{24,16},{1,9},{9,1},{17,25},{25,17},{2,10},{10... | collective-permute-start | bytes 98312 | tf_op jit(solution)/shard_map/ppermute | solution.py:506
  47.2 0.7 %collective-permute-done.14.refs_1_ = bf16[32,3584]{1,0:T(8,128)(2,1)S(1)} collective-permute-done((bf16[32,3584]{1,0:T(8,128)(2,1)S(1)}, bf16[32,3584]{1,0:T(8,128)(2,1)S(1)}, u32[]{:S(2)}, u32[]{:S(2)}) %collective-permute-start.14) | collective-permute-done | bytes 229408 | tf_op jit(solution)/shard_map/ppermute | solution.py:490
  47.9 2.0 %collective-permute-start.15 = (bf16[8,3584]{1,0:T(8,128)(2,1)S(1)}, bf16[8,3584]{1,0:T(8,128)(2,1)S(1)}, u32[]{:S(2)}, u32[]{:S(2)}) collective-permute-start(bf16[8,3584]{1,0:T(8,128)(2,1)S(1)} %get-tuple-element.68), channel_id=1, source_target_pairs={{0,6},{1,7},{2,4},{3,5},{4,2},{5,3},{6,0},{7,1},{8,14},{9,15},{10,... | collective-permute-start | bytes 172040 | tf_op jit(solution)/shard_map/ppermute | solution.py:481
  49.9 2.5 %collective-permute-start.17 = (bf16[8,3584]{1,0:T(8,128)(2,1)S(1)}, bf16[8,3584]{1,0:T(8,128)(2,1)S(1)}, u32[]{:S(2)}, u32[]{:S(2)}) collective-permute-start(bf16[8,3584]{1,0:T(8,128)(2,1)S(1)} %get-tuple-element.70), channel_id=1, source_target_pairs={{0,2},{1,3},{2,0},{3,1},{4,6},{5,7},{6,4},{7,5},{8,10},{9,11},{10,... | collective-permute-start | bytes 172040 | tf_op jit(solution)/shard_map/ppermute | solution.py:481
  52.4 0.5 collective-permute-start.19
  52.9 3.1 %collective-permute-done.19.refs_5_ = f32[4,128]{1,0:T(4,128)S(1)} collective-permute-done((f32[4,128]{1,0:T(4,128)S(1)}, f32[4,128]{1,0:T(4,128)S(1)}, u32[]{:S(2)}, u32[]{:S(2)}) %collective-permute-start.19) | collective-permute-done | bytes 2080 | tf_op jit(solution)/shard_map/ppermute | solution.py:506
  56.2 0.9 %finish.3 = (bf16[8,3584]{1,0:T(8,128)(2,1)}, bf16[8,3584]{1,0:T(8,128)(2,1)}, f32[4,4]{1,0:T(4,128)}) custom-call(bf16[2,8,3584]{2,1,0:T(8,128)(2,1)S(1)} %get-tuple-element.59.x_ref, s32[1,2]{1,0:T(1,128)S(1)} %add_bitcast_fusion.refs_4_.refs_1_.refs_6_.refs_0_.me_ref, f32[2,8,128]{2,1,0:T(8,128)S(1)} %get-tuple-element.60.coefficient_ref, ...), custom_call_target="tpu_custom_call" | custom-call | flops 3670016 | bytes 344064 | tf_op jit(solution)/shard_map/finish/pallas_call | solution.py:460
  (25 shorter events, 1.9 us)
Async XLA Ops:
  0.7 13.3 %copy-start = (bf16[2,1,3584,512]{3,2,1,0:T(8,128)(2,1)S(1)}, bf16[2,1,3584,512]{3,2,1,0:T(8,128)(2,1)}, u32[]{:S(2)}) copy-start(bf16[2,1,3584,512]{3,2,1,0:T(8,128)(2,1)} %param.9) | copy-start | bytes 22020100
  0.7 13.3 %copy-start.1 = (bf16[2,1,512,3584]{3,2,1,0:T(8,128)(2,1)S(1)}, bf16[2,1,512,3584]{3,2,1,0:T(8,128)(2,1)}, u32[]{:S(2)}) copy-start(bf16[2,1,512,3584]{3,2,1,0:T(8,128)(2,1)} %param.10) | copy-start | bytes 22020100
  2.1 6.9 %collective-permute-start = (bf16[8,3584]{1,0:T(8,128)(2,1)S(1)}, bf16[8,3584]{1,0:T(8,128)(2,1)S(1)}, u32[]{:S(2)}, u32[]{:S(2)}) collective-permute-start(bf16[8,3584]{1,0:T(8,128)(2,1)S(1)} %get-tuple-element.46), channel_id=1, source_target_pairs={{0,4},{1,5},{2,6},{3,7},{4,0},{5,1},{6,2},{7,3},{8,12},{9,13},{10,... | collective-permute-start | bytes 172040 | tf_op jit(solution)/shard_map/ppermute | solution.py:481
  6.2 6.1 %collective-permute-start.1 = (bf16[8,3584]{1,0:T(8,128)(2,1)S(1)}, bf16[8,3584]{1,0:T(8,128)(2,1)S(1)}, u32[]{:S(2)}, u32[]{:S(2)}) collective-permute-start(bf16[8,3584]{1,0:T(8,128)(2,1)S(1)} %get-tuple-element.47), channel_id=1, source_target_pairs={{0,6},{1,7},{2,4},{3,5},{4,2},{5,3},{6,0},{7,1},{8,14},{9,15},{10,... | collective-permute-start | bytes 172040 | tf_op jit(solution)/shard_map/ppermute | solution.py:481
  7.6 4.8 %collective-permute-start.2 = (bf16[8,3584]{1,0:T(8,128)(2,1)S(1)}, bf16[8,3584]{1,0:T(8,128)(2,1)S(1)}, u32[]{:S(2)}, u32[]{:S(2)}) collective-permute-start(bf16[8,3584]{1,0:T(8,128)(2,1)S(1)} %get-tuple-element.48), channel_id=1, source_target_pairs={{0,2},{1,3},{2,0},{3,1},{4,6},{5,7},{6,4},{7,5},{8,10},{9,11},{10,... | collective-permute-start | bytes 172040 | tf_op jit(solution)/shard_map/ppermute | solution.py:481
  12.4 1.6 %collective-permute-start.3 = (bf16[32,3584]{1,0:T(8,128)(2,1)S(1)}, bf16[32,3584]{1,0:T(8,128)(2,1)S(1)}, u32[]{:S(2)}, u32[]{:S(2)}) collective-permute-start(bf16[32,3584]{1,0:T(8,128)(2,1)S(1)} %join.2.refs_0_), channel_id=1, source_target_pairs={{0,1},{1,0},{2,3},{3,2},{4,5},{5,4},{6,7},{7,6},{8,9},{9,8},{10,11... | collective-permute-start | bytes 688136 | tf_op jit(solution)/shard_map/ppermute | solution.py:490
  16.6 1.5 %collective-permute-start.4 = (bf16[32,3584]{1,0:T(8,128)(2,1)S(1)}, bf16[32,3584]{1,0:T(8,128)(2,1)S(1)}, u32[]{:S(2)}, u32[]{:S(2)}) collective-permute-start(bf16[32,3584]{1,0:T(8,128)(2,1)S(1)} %get-tuple-element.50), channel_id=1, source_target_pairs={{0,1},{1,0},{2,3},{3,2},{4,5},{5,4},{6,7},{7,6},{8,9},{9,8},{10,11... | collective-permute-start | bytes 688136 | tf_op jit(solution)/shard_map/ppermute | solution.py:490
  18.2 6.6 %collective-permute-start.5 = (bf16[8,3584]{1,0:T(8,128)(2,1)S(1)}, bf16[8,3584]{1,0:T(8,128)(2,1)S(1)}, u32[]{:S(2)}, u32[]{:S(2)}) collective-permute-start(bf16[8,3584]{1,0:T(8,128)(2,1)S(1)} %get-tuple-element.52), channel_id=1, source_target_pairs={{0,6},{1,7},{2,4},{3,5},{4,2},{5,3},{6,0},{7,1},{8,14},{9,15},{10,... | collective-permute-start | bytes 172040 | tf_op jit(solution)/shard_map/ppermute | solution.py:481
  20.8 5.9 %collective-permute-start.6 = (bf16[8,3584]{1,0:T(8,128)(2,1)S(1)}, bf16[8,3584]{1,0:T(8,128)(2,1)S(1)}, u32[]{:S(2)}, u32[]{:S(2)}) collective-permute-start(bf16[8,3584]{1,0:T(8,128)(2,1)S(1)} %get-tuple-element.53), channel_id=1, source_target_pairs={{0,4},{1,5},{2,6},{3,7},{4,0},{5,1},{6,2},{7,3},{8,12},{9,13},{10,... | collective-permute-start | bytes 172040 | tf_op jit(solution)/shard_map/ppermute | solution.py:481
  20.8 5.9 %collective-permute-start.7 = (bf16[8,3584]{1,0:T(8,128)(2,1)S(1)}, bf16[8,3584]{1,0:T(8,128)(2,1)S(1)}, u32[]{:S(2)}, u32[]{:S(2)}) collective-permute-start(bf16[8,3584]{1,0:T(8,128)(2,1)S(1)} %get-tuple-element.54), channel_id=1, source_target_pairs={{0,2},{1,3},{2,0},{3,1},{4,6},{5,7},{6,4},{7,5},{8,10},{9,11},{10,... | collective-permute-start | bytes 172040 | tf_op jit(solution)/shard_map/ppermute | solution.py:481
  27.0 5.5 %collective-permute-start.8 = (bf16[8,3584]{1,0:T(8,128)(2,1)S(1)}, bf16[8,3584]{1,0:T(8,128)(2,1)S(1)}, u32[]{:S(2)}, u32[]{:S(2)}) collective-permute-start(bf16[8,3584]{1,0:T(8,128)(2,1)S(1)} %get-tuple-element.55), channel_id=1, source_target_pairs={{0,24},{8,16},{16,8},{24,0},{1,25},{9,17},{17,9},{25,1},{2,26},{10... | collective-permute-start | bytes 172040 | tf_op jit(solution)/shard_map/ppermute | solution.py:494
  29.5 4.2 %collective-permute-start.9 = (bf16[8,3584]{1,0:T(8,128)(2,1)S(1)}, bf16[8,3584]{1,0:T(8,128)(2,1)S(1)}, u32[]{:S(2)}, u32[]{:S(2)}) collective-permute-start(bf16[8,3584]{1,0:T(8,128)(2,1)S(1)} %get-tuple-element.56), channel_id=1, source_target_pairs={{0,8},{8,0},{16,24},{24,16},{1,9},{9,1},{17,25},{25,17},{2,10},{10... | collective-permute-start | bytes 172040 | tf_op jit(solution)/shard_map/ppermute | solution.py:497
  34.2 6.1 %collective-permute-start.10 = (bf16[8,3712]{1,0:T(8,128)(2,1)S(1)}, bf16[8,3712]{1,0:T(8,128)(2,1)S(1)}, u32[]{:S(2)}, u32[]{:S(2)}) collective-permute-start(bf16[8,3712]{1,0:T(8,128)(2,1)S(1)} %get-tuple-element.62), channel_id=1, source_target_pairs={{0,4},{1,5},{2,6},{3,7},{4,0},{5,1},{6,2},{7,3},{8,12},{9,13},{10,... | collective-permute-start | bytes 178184 | tf_op jit(solution)/shard_map/ppermute | solution.py:481
  35.5 6.2 %collective-permute-start.11 = (bf16[8,3712]{1,0:T(8,128)(2,1)S(1)}, bf16[8,3712]{1,0:T(8,128)(2,1)S(1)}, u32[]{:S(2)}, u32[]{:S(2)}) collective-permute-start(bf16[8,3712]{1,0:T(8,128)(2,1)S(1)} %get-tuple-element.63), channel_id=1, source_target_pairs={{0,6},{1,7},{2,4},{3,5},{4,2},{5,3},{6,0},{7,1},{8,14},{9,15},{10,... | collective-permute-start | bytes 178184 | tf_op jit(solution)/shard_map/ppermute | solution.py:481
  37.2 4.8 %collective-permute-start.12 = (bf16[8,3712]{1,0:T(8,128)(2,1)S(1)}, bf16[8,3712]{1,0:T(8,128)(2,1)S(1)}, u32[]{:S(2)}, u32[]{:S(2)}) collective-permute-start(bf16[8,3712]{1,0:T(8,128)(2,1)S(1)} %get-tuple-element.64), channel_id=1, source_target_pairs={{0,2},{1,3},{2,0},{3,1},{4,6},{5,7},{6,4},{7,5},{8,10},{9,11},{10,... | collective-permute-start | bytes 178184 | tf_op jit(solution)/shard_map/ppermute | solution.py:481
  42.1 1.6 %collective-permute-start.13 = (bf16[32,3712]{1,0:T(8,128)(2,1)S(1)}, bf16[32,3712]{1,0:T(8,128)(2,1)S(1)}, u32[]{:S(2)}, u32[]{:S(2)}) collective-permute-start(bf16[32,3712]{1,0:T(8,128)(2,1)S(1)} %join.3.refs_1_), channel_id=1, source_target_pairs={{0,1},{1,0},{2,3},{3,2},{4,5},{5,4},{6,7},{7,6},{8,9},{9,8},{10,11... | collective-permute-start | bytes 712712 | tf_op jit(solution)/shard_map/ppermute | solution.py:490
  46.3 1.5 %collective-permute-start.14 = (bf16[32,3584]{1,0:T(8,128)(2,1)S(1)}, bf16[32,3584]{1,0:T(8,128)(2,1)S(1)}, u32[]{:S(2)}, u32[]{:S(2)}) collective-permute-start(bf16[32,3584]{1,0:T(8,128)(2,1)S(1)} %get-tuple-element.66), channel_id=1, source_target_pairs={{0,1},{1,0},{2,3},{3,2},{4,5},{5,4},{6,7},{7,6},{8,9},{9,8},{10,11... | collective-permute-start | bytes 688136 | tf_op jit(solution)/shard_map/ppermute | solution.py:490
  46.5 5.9 %collective-permute-start.18 = (f32[64,128]{1,0:T(8,128)S(1)}, f32[64,128]{1,0:T(8,128)S(1)}, u32[]{:S(2)}, u32[]{:S(2)}) collective-permute-start(f32[64,128]{1,0:T(8,128)S(1)} %get-tuple-element.71), channel_id=1, source_target_pairs={{0,8},{8,0},{16,24},{24,16},{1,9},{9,1},{17,25},{25,17},{2,10},{10... | collective-permute-start | bytes 98312 | tf_op jit(solution)/shard_map/ppermute | solution.py:506
  47.9 8.1 %collective-permute-start.15 = (bf16[8,3584]{1,0:T(8,128)(2,1)S(1)}, bf16[8,3584]{1,0:T(8,128)(2,1)S(1)}, u32[]{:S(2)}, u32[]{:S(2)}) collective-permute-start(bf16[8,3584]{1,0:T(8,128)(2,1)S(1)} %get-tuple-element.68), channel_id=1, source_target_pairs={{0,6},{1,7},{2,4},{3,5},{4,2},{5,3},{6,0},{7,1},{8,14},{9,15},{10,... | collective-permute-start | bytes 172040 | tf_op jit(solution)/shard_map/ppermute | solution.py:481
  49.9 6.3 %collective-permute-start.16 = (bf16[8,3584]{1,0:T(8,128)(2,1)S(1)}, bf16[8,3584]{1,0:T(8,128)(2,1)S(1)}, u32[]{:S(2)}, u32[]{:S(2)}) collective-permute-start(bf16[8,3584]{1,0:T(8,128)(2,1)S(1)} %get-tuple-element.69), channel_id=1, source_target_pairs={{0,4},{1,5},{2,6},{3,7},{4,0},{5,1},{6,2},{7,3},{8,12},{9,13},{10,... | collective-permute-start | bytes 172040 | tf_op jit(solution)/shard_map/ppermute | solution.py:481
  49.9 6.3 %collective-permute-start.17 = (bf16[8,3584]{1,0:T(8,128)(2,1)S(1)}, bf16[8,3584]{1,0:T(8,128)(2,1)S(1)}, u32[]{:S(2)}, u32[]{:S(2)}) collective-permute-start(bf16[8,3584]{1,0:T(8,128)(2,1)S(1)} %get-tuple-element.70), channel_id=1, source_target_pairs={{0,2},{1,3},{2,0},{3,1},{4,6},{5,7},{6,4},{7,5},{8,10},{9,11},{10,... | collective-permute-start | bytes 172040 | tf_op jit(solution)/shard_map/ppermute | solution.py:481
  52.4 3.6 %collective-permute-start.19 = (f32[4,128]{1,0:T(4,128)S(1)}, f32[4,128]{1,0:T(4,128)S(1)}, u32[]{:S(2)}, u32[]{:S(2)}) collective-permute-start(f32[4,128]{1,0:T(4,128)S(1)} %slice_add_fusion.refs_4_), channel_id=1, source_target_pairs={{0,16},{8,24},{16,0},{24,8},{1,17},{9,25},{17,1},{25,9},{2,18},{10... | collective-permute-start | bytes 6152 | tf_op jit(solution)/shard_map/ppermute | solution.py:506

commit v4 on v3

--- a/solution.py
+++ b/solution.py
@@ -97,10 +97,12 @@
     return jnp.where(slot, 1.0, 0.0)
 
 
-def pack_rows(place, normed, slots):
-    return jnp.dot(
-        place.T[:slots].astype(jnp.bfloat16), normed, preferred_element_type=jnp.float32
-    )
+def turned(place, slots):
+    return place.T[:slots].astype(jnp.bfloat16)
+
+
+def pack_rows(turned_place, normed):
+    return jnp.dot(turned_place, normed, preferred_element_type=jnp.float32)
 
 
 def gate_rows(normed, router, chosen, place, me, mine, experts, capacity, spare):
@@ -165,7 +167,7 @@
         normed = normalize(x_ref[stream])
         normed_ref[stream] = normed
         place_ref[stream] = places[stream]
-        packed.append(pack_rows(places[stream], normed, experts * capacity))
+        packed.append(pack_rows(turned(places[stream], experts * capacity), normed))
     store_blocks(packed, block_refs, capacity)
 
 
@@ -199,7 +201,7 @@
 
 def gates_body(group, experts, capacity, spare, *refs):
     normed_ref, place_ref, router_ref, routes_ref, me_ref = refs[:5]
-    coefficient_ref, mass_ref, next_ref = refs[5:]
+    coefficient_ref, mass_ref, next_ref, turned_ref = refs[5:]
     me = me_ref[0, 0]
     mine = lax.div(me, group)
     rows = normed_ref.shape[1]
@@ -215,7 +217,9 @@
             capacity,
             spare,
         )
-        next_ref[stream] = place_rows(chosen_by(routes_ref[1, stream]), mine, rows, capacity)
+        place = place_rows(chosen_by(routes_ref[1, stream]), mine, rows, capacity)
+        next_ref[stream] = place
+        turned_ref[stream] = turned(place, experts * capacity)
 
 
 def gates(normed, place, router, routes, me, group, capacity, spare):
@@ -224,6 +228,7 @@
         jax.ShapeDtypeStruct(place.shape, jnp.float32),
         jax.ShapeDtypeStruct((STREAMS, 2, spare), jnp.float32),
         jax.ShapeDtypeStruct(place.shape, jnp.float32),
+        jax.ShapeDtypeStruct((STREAMS, experts * capacity, place.shape[1]), jnp.bfloat16),
     ]
     return call(
         functools.partial(gates_body, group, experts, capacity, spare),
@@ -235,9 +240,9 @@
 
 
 def repeat_body(group, experts, capacity, spare, *refs):
-    far_ref, near_ref, place_ref, router_ref, routes_ref, old_ref, me_ref = refs[:7]
-    block_refs = refs[7 : 7 + experts]
-    x_ref, coefficient_ref = refs[7 + experts :]
+    far_ref, near_ref, place_ref, router_ref, routes_ref, old_ref, me_ref, turned_ref = refs[:8]
+    block_refs = refs[8 : 8 + experts]
+    x_ref, coefficient_ref = refs[8 + experts :]
     me = me_ref[0, 0]
     mine = lax.div(me, group)
     far, near = far_ref[...], near_ref[...]
@@ -248,7 +253,7 @@
     for stream in range(STREAMS):
         x_ref[stream] = xs[stream]
         normed = normalize(xs[stream])
-        packed.append(pack_rows(place_ref[stream], normed, experts * capacity))
+        packed.append(pack_rows(turned_ref[stream], normed))
         coefficient, masses = gate_rows(
             normed,
             router_ref[stream],
@@ -431,11 +436,11 @@
             [part[stream * capacity : (stream + 1) * capacity] for part in parts]
         ).astype(jnp.bfloat16)
         coefficient = coefficient_ref[stream, :, : experts * capacity]
-        high = coefficient.astype(jnp.bfloat16)
-        low = (coefficient - high.astype(jnp.float32)).astype(jnp.bfloat16)
-        mixture = jnp.dot(high, returned, preferred_element_type=jnp.float32) + jnp.dot(
-            low, returned, preferred_element_type=jnp.float32
-        )
+        high = coefficient.astype(jnp.bfloat16).astype(jnp.float32)
+        halves = jnp.concatenate([high, coefficient - high]).astype(jnp.bfloat16)
+        mixtures = jnp.dot(halves, returned, preferred_element_type=jnp.float32)
+        rows = high.shape[0]
+        mixture = mixtures[:rows] + mixtures[rows:]
         results.append(x_ref[stream].astype(jnp.float32) + mixture)
     if not scale:
         even = is_even(me_ref[0, 1], mixture.shape)
@@ -529,12 +534,12 @@
                 [stream_a[0], stream_b[0], router, picks, me], ring.group, capacity
             )
             x, normed, slots, router, picks = others
-            coefficient, mass, slots = gates(
+            coefficient, mass, slots, packing = gates(
                 normed, slots, router, picks, me, ring.group, capacity, spare
             )
         else:
             blocks, (x, coefficient) = repeat(
-                [*moved, slots, router, picks, mass, me], ring.group, capacity, spare, held
+                [*moved, slots, router, picks, mass, me, packing], ring.group, capacity, spare, held
             )
         own = join(
             ring.across(blocks),

time: 57.3 us -> 57.2 us (level)
  no operation moved by 1% of the time
where the time goes in v4:
time: 57.2 us; the launch traced here: 57 us
  waiting for transfers between devices  24.6 us (43%)
  starting transfers between devices  22.9 us (40%)
  Pallas kernels  8.76 us (15%)
  between operations  0.72 us (1%)
    ppermute x12, starting transfers between devices, across(): lax.ppermute(blocks[k], 'expert', [(j, j ^ k * self.group) for j in range...  18.1 us
    ppermute x12, waiting for transfers between devices, across(): lax.ppermute(blocks[k], 'expert', [(j, j ^ k * self.group) for j in range...  12.9 us
    pallas_call x2, Pallas kernels, expert_rows(): call(functools.partial(expert_body, group, capacity, experts, spare, laye...  5.26 us
    ppermute x4, waiting for transfers between devices, within(): return lax.ppermute(array, 'expert', pairs)  4.98 us
    ppermute x2, waiting for transfers between devices, over_sections(): lax.ppermute(table, 'pipe', [(i, i ^ step) for i in range(self.pipe)])  3.08 us
    ppermute x1, starting transfers between devices, far(): return lax.ppermute(array, 'pipe', list(enumerate(steps)))  2.51 us
    ppermute x1, waiting for transfers between devices, far(): return lax.ppermute(array, 'pipe', list(enumerate(steps)))  2.45 us
    pallas_call x1, Pallas kernels, prepare(): call(functools.partial(prepare_body, group, experts, capacity), outs, 'pr...  1.38 us
  transfers between devices with their start and end apart: 20, of which 16 were waited for; matrix products, arithmetic and copies ran while one was open for 0% of the time, Pallas kernels for 1%

profile of v4, /device:TPU:0, one launch (start us, length us, event | category | flops | bytes accessed | tf_op | source)
XLA Modules:
  0.0 57.0 jit_solution(17728633039114854720)
XLA Ops:
  0.7 1.4 %prepare.2 = (bf16[8,3584]{1,0:T(8,128)(2,1)S(1)}, bf16[8,3584]{1,0:T(8,128)(2,1)S(1)}, bf16[8,3584]{1,0:T(8,128)(2,1)S(1)}, bf16[8,3584]{1,0:T(8,128)(2,1)S(1)}...) custom-call(bf16[8,3584]{1,0:T(8,128)(2,1)} %bitcast.28, ...), custom_call_target="tpu_custom_call" | custom-call | flops 20000000000 | bytes 114688 | tf_op jit(solution)/shard_map/prepare/pallas_call | solution.py:189
  2.1 4.1 %collective-permute-start = (bf16[8,3584]{1,0:T(8,128)(2,1)S(1)}, bf16[8,3584]{1,0:T(8,128)(2,1)S(1)}, u32[]{:S(2)}, u32[]{:S(2)}) collective-permute-start(bf16[8,3584]{1,0:T(8,128)(2,1)S(1)} %get-tuple-element.47), channel_id=1, source_target_pairs={{0,4},{1,5},{2,6},{3,7},{4,0},{5,1},{6,2},{7,3},{8,12},{9,13},{10,... | collective-permute-start | bytes 172040 | tf_op jit(solution)/shard_map/ppermute | solution.py:486
  6.2 1.3 %collective-permute-start.1 = (bf16[8,3584]{1,0:T(8,128)(2,1)S(1)}, bf16[8,3584]{1,0:T(8,128)(2,1)S(1)}, u32[]{:S(2)}, u32[]{:S(2)}) collective-permute-start(bf16[8,3584]{1,0:T(8,128)(2,1)S(1)} %get-tuple-element.48), channel_id=1, source_target_pairs={{0,6},{1,7},{2,4},{3,5},{4,2},{5,3},{6,0},{7,1},{8,14},{9,15},{10,... | collective-permute-start | bytes 172040 | tf_op jit(solution)/shard_map/ppermute | solution.py:486
  7.8 1.2 %collective-permute-done.refs_1_ = bf16[8,3584]{1,0:T(8,128)(2,1)S(1)} collective-permute-done((bf16[8,3584]{1,0:T(8,128)(2,1)S(1)}, bf16[8,3584]{1,0:T(8,128)(2,1)S(1)}, u32[]{:S(2)}, u32[]{:S(2)}) %collective-permute-start) | collective-permute-done | bytes 57376 | tf_op jit(solution)/shard_map/ppermute | solution.py:486
  9.0 3.3 %collective-permute-done.1.refs_2_ = bf16[8,3584]{1,0:T(8,128)(2,1)S(1)} collective-permute-done((bf16[8,3584]{1,0:T(8,128)(2,1)S(1)}, bf16[8,3584]{1,0:T(8,128)(2,1)S(1)}, u32[]{:S(2)}, u32[]{:S(2)}) %collective-permute-start.1) | collective-permute-done | bytes 57376 | tf_op jit(solution)/shard_map/ppermute | solution.py:486
  12.5 1.5 %collective-permute-done.3.refs_1_ = bf16[32,3584]{1,0:T(8,128)(2,1)S(1)} collective-permute-done((bf16[32,3584]{1,0:T(8,128)(2,1)S(1)}, bf16[32,3584]{1,0:T(8,128)(2,1)S(1)}, u32[]{:S(2)}, u32[]{:S(2)}) %collective-permute-start.3) | collective-permute-done | bytes 229408 | tf_op jit(solution)/shard_map/ppermute | solution.py:495
  14.0 2.6 %experts.2 = (bf16[32,3584]{1,0:T(8,128)(2,1)S(1)}, bf16[32,3584]{1,0:T(8,128)(2,1)S(1)}) custom-call(bf16[2,3584,512]{2,1,0:T(8,128)(2,1)S(1)} %bitcast.16, bf16[2,512,3584]{2,1,0:T(8,128)(2,1)S(1)} %bitcast.22, bf16[32,3584]{1,0:T(8,128)(2,1)S(1)} %join.2.refs_0_, bf16[32,3584]{1,0:T(8,128)(2,1)S(1)} %collective-permute-done.3.refs_1_), custom_call_target="tpu_custom_call" | custom-call | flops 469762048 | bytes 7340032 | tf_op jit(solution)/shard_map/experts/pallas_call | solution.py:391
  16.8 1.4 %collective-permute-done.4.refs_1_ = bf16[32,3584]{1,0:T(8,128)(2,1)S(1)} collective-permute-done((bf16[32,3584]{1,0:T(8,128)(2,1)S(1)}, bf16[32,3584]{1,0:T(8,128)(2,1)S(1)}, u32[]{:S(2)}, u32[]{:S(2)}) %collective-permute-start.4) | collective-permute-done | bytes 229408 | tf_op jit(solution)/shard_map/ppermute | solution.py:495
  18.2 2.6 %collective-permute-start.5 = (bf16[8,3584]{1,0:T(8,128)(2,1)S(1)}, bf16[8,3584]{1,0:T(8,128)(2,1)S(1)}, u32[]{:S(2)}, u32[]{:S(2)}) collective-permute-start(bf16[8,3584]{1,0:T(8,128)(2,1)S(1)} %get-tuple-element.53), channel_id=1, source_target_pairs={{0,6},{1,7},{2,4},{3,5},{4,2},{5,3},{6,0},{7,1},{8,14},{9,15},{10,... | collective-permute-start | bytes 172040 | tf_op jit(solution)/shard_map/ppermute | solution.py:486
  20.8 1.8 %collective-permute-start.7 = (bf16[8,3584]{1,0:T(8,128)(2,1)S(1)}, bf16[8,3584]{1,0:T(8,128)(2,1)S(1)}, u32[]{:S(2)}, u32[]{:S(2)}) collective-permute-start(bf16[8,3584]{1,0:T(8,128)(2,1)S(1)} %get-tuple-element.55), channel_id=1, source_target_pairs={{0,2},{1,3},{2,0},{3,1},{4,6},{5,7},{6,4},{7,5},{8,10},{9,11},{10,... | collective-permute-start | bytes 172040 | tf_op jit(solution)/shard_map/ppermute | solution.py:486
  22.9 1.9 %collective-permute-done.5.refs_4_ = bf16[8,3584]{1,0:T(8,128)(2,1)S(1)} collective-permute-done((bf16[8,3584]{1,0:T(8,128)(2,1)S(1)}, bf16[8,3584]{1,0:T(8,128)(2,1)S(1)}, u32[]{:S(2)}, u32[]{:S(2)}) %collective-permute-start.5) | collective-permute-done | bytes 57376 | tf_op jit(solution)/shard_map/ppermute | solution.py:486
  24.9 1.9 %collective-permute-done.6.refs_5_ = bf16[8,3584]{1,0:T(8,128)(2,1)S(1)} collective-permute-done((bf16[8,3584]{1,0:T(8,128)(2,1)S(1)}, bf16[8,3584]{1,0:T(8,128)(2,1)S(1)}, u32[]{:S(2)}, u32[]{:S(2)}) %collective-permute-start.6) | collective-permute-done | bytes 57376 | tf_op jit(solution)/shard_map/ppermute | solution.py:486
  27.0 2.5 %collective-permute-start.8 = (bf16[8,3584]{1,0:T(8,128)(2,1)S(1)}, bf16[8,3584]{1,0:T(8,128)(2,1)S(1)}, u32[]{:S(2)}, u32[]{:S(2)}) collective-permute-start(bf16[8,3584]{1,0:T(8,128)(2,1)S(1)} %get-tuple-element.56), channel_id=1, source_target_pairs={{0,24},{8,16},{16,8},{24,0},{1,25},{9,17},{17,9},{25,1},{2,26},{10... | collective-permute-start | bytes 172040 | tf_op jit(solution)/shard_map/ppermute | solution.py:499
  29.5 0.5 collective-permute-start.9
  30.0 2.5 %collective-permute-done.8.refs_0_ = bf16[8,3584]{1,0:T(8,128)(2,1)S(1)} collective-permute-done((bf16[8,3584]{1,0:T(8,128)(2,1)S(1)}, bf16[8,3584]{1,0:T(8,128)(2,1)S(1)}, u32[]{:S(2)}, u32[]{:S(2)}) %collective-permute-start.8) | collective-permute-done | bytes 57376 | tf_op jit(solution)/shard_map/ppermute | solution.py:499
  32.5 1.2 %collective-permute-done.9.refs_1_ = bf16[8,3584]{1,0:T(8,128)(2,1)S(1)} collective-permute-done((bf16[8,3584]{1,0:T(8,128)(2,1)S(1)}, bf16[8,3584]{1,0:T(8,128)(2,1)S(1)}, u32[]{:S(2)}, u32[]{:S(2)}) %collective-permute-start.9) | collective-permute-done | bytes 57376 | tf_op jit(solution)/shard_map/ppermute | solution.py:502
  33.6 0.5 prepare.3
  34.1 1.3 %collective-permute-start.10 = (bf16[8,3712]{1,0:T(8,128)(2,1)S(1)}, bf16[8,3712]{1,0:T(8,128)(2,1)S(1)}, u32[]{:S(2)}, u32[]{:S(2)}) collective-permute-start(bf16[8,3712]{1,0:T(8,128)(2,1)S(1)} %get-tuple-element.64), channel_id=1, source_target_pairs={{0,4},{1,5},{2,6},{3,7},{4,0},{5,1},{6,2},{7,3},{8,12},{9,13},{10,... | collective-permute-start | bytes 178184 | tf_op jit(solution)/shard_map/ppermute | solution.py:486
  35.4 1.7 %collective-permute-start.11 = (bf16[8,3712]{1,0:T(8,128)(2,1)S(1)}, bf16[8,3712]{1,0:T(8,128)(2,1)S(1)}, u32[]{:S(2)}, u32[]{:S(2)}) collective-permute-start(bf16[8,3712]{1,0:T(8,128)(2,1)S(1)} %get-tuple-element.65), channel_id=1, source_target_pairs={{0,6},{1,7},{2,4},{3,5},{4,2},{5,3},{6,0},{7,1},{8,14},{9,15},{10,... | collective-permute-start | bytes 178184 | tf_op jit(solution)/shard_map/ppermute | solution.py:486
  37.1 0.5 collective-permute-start.12
  37.7 2.6 %collective-permute-done.10.refs_1_ = bf16[8,3712]{1,0:T(8,128)(2,1)S(1)} collective-permute-done((bf16[8,3712]{1,0:T(8,128)(2,1)S(1)}, bf16[8,3712]{1,0:T(8,128)(2,1)S(1)}, u32[]{:S(2)}, u32[]{:S(2)}) %collective-permute-start.10) | collective-permute-done | bytes 59424 | tf_op jit(solution)/shard_map/ppermute | solution.py:486
  40.2 1.3 %collective-permute-done.11.refs_2_ = bf16[8,3712]{1,0:T(8,128)(2,1)S(1)} collective-permute-done((bf16[8,3712]{1,0:T(8,128)(2,1)S(1)}, bf16[8,3712]{1,0:T(8,128)(2,1)S(1)}, u32[]{:S(2)}, u32[]{:S(2)}) %collective-permute-start.11) | collective-permute-done | bytes 59424 | tf_op jit(solution)/shard_map/ppermute | solution.py:486
  41.6 0.4 collective-permute-done.12.refs_3_
  42.1 1.5 %collective-permute-done.13.refs_2_ = bf16[32,3712]{1,0:T(8,128)(2,1)S(1)} collective-permute-done((bf16[32,3712]{1,0:T(8,128)(2,1)S(1)}, bf16[32,3712]{1,0:T(8,128)(2,1)S(1)}, u32[]{:S(2)}, u32[]{:S(2)}) %collective-permute-start.13) | collective-permute-done | bytes 237600 | tf_op jit(solution)/shard_map/ppermute | solution.py:495
  43.6 2.6 %experts.3 = (bf16[32,3584]{1,0:T(8,128)(2,1)S(1)}, bf16[32,3584]{1,0:T(8,128)(2,1)S(1)}, f32[64,128]{1,0:T(8,128)S(1)}) custom-call(bf16[2,3584,512]{2,1,0:T(8,128)(2,1)S(1)} %bitcast.21, bf16[2,512,3584]{2,1,0:T(8,128)(2,1)S(1)} %bitcast.27, s32[1,2]{1,0:T(1,128)S(1)} %add_bitcast_fusion.refs_4_.refs_1_.refs_6_.refs_0_.me_ref, ...), custom_call_target="tpu_custom_call" | custom-call | flops 469762048 | bytes 7340032 | tf_op jit(solution)/shard_map/experts/pallas_call | solution.py:391
  46.4 0.7 %collective-permute-start.18 = (f32[64,128]{1,0:T(8,128)S(1)}, f32[64,128]{1,0:T(8,128)S(1)}, u32[]{:S(2)}, u32[]{:S(2)}) collective-permute-start(f32[64,128]{1,0:T(8,128)S(1)} %get-tuple-element.73), channel_id=1, source_target_pairs={{0,8},{8,0},{16,24},{24,16},{1,9},{9,1},{17,25},{25,17},{2,10},{10... | collective-permute-start | bytes 98312 | tf_op jit(solution)/shard_map/ppermute | solution.py:511
  47.1 0.7 %collective-permute-done.14.refs_1_ = bf16[32,3584]{1,0:T(8,128)(2,1)S(1)} collective-permute-done((bf16[32,3584]{1,0:T(8,128)(2,1)S(1)}, bf16[32,3584]{1,0:T(8,128)(2,1)S(1)}, u32[]{:S(2)}, u32[]{:S(2)}) %collective-permute-start.14) | collective-permute-done | bytes 229408 | tf_op jit(solution)/shard_map/ppermute | solution.py:495
  47.9 2.0 %collective-permute-start.15 = (bf16[8,3584]{1,0:T(8,128)(2,1)S(1)}, bf16[8,3584]{1,0:T(8,128)(2,1)S(1)}, u32[]{:S(2)}, u32[]{:S(2)}) collective-permute-start(bf16[8,3584]{1,0:T(8,128)(2,1)S(1)} %get-tuple-element.70), channel_id=1, source_target_pairs={{0,6},{1,7},{2,4},{3,5},{4,2},{5,3},{6,0},{7,1},{8,14},{9,15},{10,... | collective-permute-start | bytes 172040 | tf_op jit(solution)/shard_map/ppermute | solution.py:486
  49.8 2.5 %collective-permute-start.17 = (bf16[8,3584]{1,0:T(8,128)(2,1)S(1)}, bf16[8,3584]{1,0:T(8,128)(2,1)S(1)}, u32[]{:S(2)}, u32[]{:S(2)}) collective-permute-start(bf16[8,3584]{1,0:T(8,128)(2,1)S(1)} %get-tuple-element.72), channel_id=1, source_target_pairs={{0,2},{1,3},{2,0},{3,1},{4,6},{5,7},{6,4},{7,5},{8,10},{9,11},{10,... | collective-permute-start | bytes 172040 | tf_op jit(solution)/shard_map/ppermute | solution.py:486
  52.3 0.5 collective-permute-start.19
  52.8 3.1 %collective-permute-done.19.refs_5_ = f32[4,128]{1,0:T(4,128)S(1)} collective-permute-done((f32[4,128]{1,0:T(4,128)S(1)}, f32[4,128]{1,0:T(4,128)S(1)}, u32[]{:S(2)}, u32[]{:S(2)}) %collective-permute-start.19) | collective-permute-done | bytes 2080 | tf_op jit(solution)/shard_map/ppermute | solution.py:511
  56.2 0.8 %finish.3 = (bf16[8,3584]{1,0:T(8,128)(2,1)}, bf16[8,3584]{1,0:T(8,128)(2,1)}, f32[4,4]{1,0:T(4,128)}) custom-call(bf16[2,8,3584]{2,1,0:T(8,128)(2,1)S(1)} %get-tuple-element.61.x_ref, s32[1,2]{1,0:T(1,128)S(1)} %add_bitcast_fusion.refs_4_.refs_1_.refs_6_.refs_0_.me_ref, f32[2,8,128]{2,1,0:T(8,128)S(1)} %get-tuple-element.62.coefficient_ref, ...), custom_call_target="tpu_custom_call" | custom-call | flops 3670016 | bytes 344064 | tf_op jit(solution)/shard_map/finish/pallas_call | solution.py:465
  (25 shorter events, 1.9 us)
Async XLA Ops:
  0.7 13.3 %copy-start = (bf16[2,1,3584,512]{3,2,1,0:T(8,128)(2,1)S(1)}, bf16[2,1,3584,512]{3,2,1,0:T(8,128)(2,1)}, u32[]{:S(2)}) copy-start(bf16[2,1,3584,512]{3,2,1,0:T(8,128)(2,1)} %param.9) | copy-start | bytes 22020100
  0.7 13.3 %copy-start.1 = (bf16[2,1,512,3584]{3,2,1,0:T(8,128)(2,1)S(1)}, bf16[2,1,512,3584]{3,2,1,0:T(8,128)(2,1)}, u32[]{:S(2)}) copy-start(bf16[2,1,512,3584]{3,2,1,0:T(8,128)(2,1)} %param.10) | copy-start | bytes 22020100
  2.1 6.9 %collective-permute-start = (bf16[8,3584]{1,0:T(8,128)(2,1)S(1)}, bf16[8,3584]{1,0:T(8,128)(2,1)S(1)}, u32[]{:S(2)}, u32[]{:S(2)}) collective-permute-start(bf16[8,3584]{1,0:T(8,128)(2,1)S(1)} %get-tuple-element.47), channel_id=1, source_target_pairs={{0,4},{1,5},{2,6},{3,7},{4,0},{5,1},{6,2},{7,3},{8,12},{9,13},{10,... | collective-permute-start | bytes 172040 | tf_op jit(solution)/shard_map/ppermute | solution.py:486
  6.2 6.1 %collective-permute-start.1 = (bf16[8,3584]{1,0:T(8,128)(2,1)S(1)}, bf16[8,3584]{1,0:T(8,128)(2,1)S(1)}, u32[]{:S(2)}, u32[]{:S(2)}) collective-permute-start(bf16[8,3584]{1,0:T(8,128)(2,1)S(1)} %get-tuple-element.48), channel_id=1, source_target_pairs={{0,6},{1,7},{2,4},{3,5},{4,2},{5,3},{6,0},{7,1},{8,14},{9,15},{10,... | collective-permute-start | bytes 172040 | tf_op jit(solution)/shard_map/ppermute | solution.py:486
  7.6 4.8 %collective-permute-start.2 = (bf16[8,3584]{1,0:T(8,128)(2,1)S(1)}, bf16[8,3584]{1,0:T(8,128)(2,1)S(1)}, u32[]{:S(2)}, u32[]{:S(2)}) collective-permute-start(bf16[8,3584]{1,0:T(8,128)(2,1)S(1)} %get-tuple-element.49), channel_id=1, source_target_pairs={{0,2},{1,3},{2,0},{3,1},{4,6},{5,7},{6,4},{7,5},{8,10},{9,11},{10,... | collective-permute-start | bytes 172040 | tf_op jit(solution)/shard_map/ppermute | solution.py:486
  12.4 1.6 %collective-permute-start.3 = (bf16[32,3584]{1,0:T(8,128)(2,1)S(1)}, bf16[32,3584]{1,0:T(8,128)(2,1)S(1)}, u32[]{:S(2)}, u32[]{:S(2)}) collective-permute-start(bf16[32,3584]{1,0:T(8,128)(2,1)S(1)} %join.2.refs_0_), channel_id=1, source_target_pairs={{0,1},{1,0},{2,3},{3,2},{4,5},{5,4},{6,7},{7,6},{8,9},{9,8},{10,11... | collective-permute-start | bytes 688136 | tf_op jit(solution)/shard_map/ppermute | solution.py:495
  16.6 1.5 %collective-permute-start.4 = (bf16[32,3584]{1,0:T(8,128)(2,1)S(1)}, bf16[32,3584]{1,0:T(8,128)(2,1)S(1)}, u32[]{:S(2)}, u32[]{:S(2)}) collective-permute-start(bf16[32,3584]{1,0:T(8,128)(2,1)S(1)} %get-tuple-element.51), channel_id=1, source_target_pairs={{0,1},{1,0},{2,3},{3,2},{4,5},{5,4},{6,7},{7,6},{8,9},{9,8},{10,11... | collective-permute-start | bytes 688136 | tf_op jit(solution)/shard_map/ppermute | solution.py:495
  18.2 6.6 %collective-permute-start.5 = (bf16[8,3584]{1,0:T(8,128)(2,1)S(1)}, bf16[8,3584]{1,0:T(8,128)(2,1)S(1)}, u32[]{:S(2)}, u32[]{:S(2)}) collective-permute-start(bf16[8,3584]{1,0:T(8,128)(2,1)S(1)} %get-tuple-element.53), channel_id=1, source_target_pairs={{0,6},{1,7},{2,4},{3,5},{4,2},{5,3},{6,0},{7,1},{8,14},{9,15},{10,... | collective-permute-start | bytes 172040 | tf_op jit(solution)/shard_map/ppermute | solution.py:486
  20.8 5.9 %collective-permute-start.6 = (bf16[8,3584]{1,0:T(8,128)(2,1)S(1)}, bf16[8,3584]{1,0:T(8,128)(2,1)S(1)}, u32[]{:S(2)}, u32[]{:S(2)}) collective-permute-start(bf16[8,3584]{1,0:T(8,128)(2,1)S(1)} %get-tuple-element.54), channel_id=1, source_target_pairs={{0,4},{1,5},{2,6},{3,7},{4,0},{5,1},{6,2},{7,3},{8,12},{9,13},{10,... | collective-permute-start | bytes 172040 | tf_op jit(solution)/shard_map/ppermute | solution.py:486
  20.8 5.9 %collective-permute-start.7 = (bf16[8,3584]{1,0:T(8,128)(2,1)S(1)}, bf16[8,3584]{1,0:T(8,128)(2,1)S(1)}, u32[]{:S(2)}, u32[]{:S(2)}) collective-permute-start(bf16[8,3584]{1,0:T(8,128)(2,1)S(1)} %get-tuple-element.55), channel_id=1, source_target_pairs={{0,2},{1,3},{2,0},{3,1},{4,6},{5,7},{6,4},{7,5},{8,10},{9,11},{10,... | collective-permute-start | bytes 172040 | tf_op jit(solution)/shard_map/ppermute | solution.py:486
  27.0 5.5 %collective-permute-start.8 = (bf16[8,3584]{1,0:T(8,128)(2,1)S(1)}, bf16[8,3584]{1,0:T(8,128)(2,1)S(1)}, u32[]{:S(2)}, u32[]{:S(2)}) collective-permute-start(bf16[8,3584]{1,0:T(8,128)(2,1)S(1)} %get-tuple-element.56), channel_id=1, source_target_pairs={{0,24},{8,16},{16,8},{24,0},{1,25},{9,17},{17,9},{25,1},{2,26},{10... | collective-permute-start | bytes 172040 | tf_op jit(solution)/shard_map/ppermute | solution.py:499
  29.5 4.2 %collective-permute-start.9 = (bf16[8,3584]{1,0:T(8,128)(2,1)S(1)}, bf16[8,3584]{1,0:T(8,128)(2,1)S(1)}, u32[]{:S(2)}, u32[]{:S(2)}) collective-permute-start(bf16[8,3584]{1,0:T(8,128)(2,1)S(1)} %get-tuple-element.57), channel_id=1, source_target_pairs={{0,8},{8,0},{16,24},{24,16},{1,9},{9,1},{17,25},{25,17},{2,10},{10... | collective-permute-start | bytes 172040 | tf_op jit(solution)/shard_map/ppermute | solution.py:502
  34.1 6.1 %collective-permute-start.10 = (bf16[8,3712]{1,0:T(8,128)(2,1)S(1)}, bf16[8,3712]{1,0:T(8,128)(2,1)S(1)}, u32[]{:S(2)}, u32[]{:S(2)}) collective-permute-start(bf16[8,3712]{1,0:T(8,128)(2,1)S(1)} %get-tuple-element.64), channel_id=1, source_target_pairs={{0,4},{1,5},{2,6},{3,7},{4,0},{5,1},{6,2},{7,3},{8,12},{9,13},{10,... | collective-permute-start | bytes 178184 | tf_op jit(solution)/shard_map/ppermute | solution.py:486
  35.4 6.2 %collective-permute-start.11 = (bf16[8,3712]{1,0:T(8,128)(2,1)S(1)}, bf16[8,3712]{1,0:T(8,128)(2,1)S(1)}, u32[]{:S(2)}, u32[]{:S(2)}) collective-permute-start(bf16[8,3712]{1,0:T(8,128)(2,1)S(1)} %get-tuple-element.65), channel_id=1, source_target_pairs={{0,6},{1,7},{2,4},{3,5},{4,2},{5,3},{6,0},{7,1},{8,14},{9,15},{10,... | collective-permute-start | bytes 178184 | tf_op jit(solution)/shard_map/ppermute | solution.py:486
  37.1 4.8 %collective-permute-start.12 = (bf16[8,3712]{1,0:T(8,128)(2,1)S(1)}, bf16[8,3712]{1,0:T(8,128)(2,1)S(1)}, u32[]{:S(2)}, u32[]{:S(2)}) collective-permute-start(bf16[8,3712]{1,0:T(8,128)(2,1)S(1)} %get-tuple-element.66), channel_id=1, source_target_pairs={{0,2},{1,3},{2,0},{3,1},{4,6},{5,7},{6,4},{7,5},{8,10},{9,11},{10,... | collective-permute-start | bytes 178184 | tf_op jit(solution)/shard_map/ppermute | solution.py:486
  42.1 1.6 %collective-permute-start.13 = (bf16[32,3712]{1,0:T(8,128)(2,1)S(1)}, bf16[32,3712]{1,0:T(8,128)(2,1)S(1)}, u32[]{:S(2)}, u32[]{:S(2)}) collective-permute-start(bf16[32,3712]{1,0:T(8,128)(2,1)S(1)} %join.3.refs_1_), channel_id=1, source_target_pairs={{0,1},{1,0},{2,3},{3,2},{4,5},{5,4},{6,7},{7,6},{8,9},{9,8},{10,11... | collective-permute-start | bytes 712712 | tf_op jit(solution)/shard_map/ppermute | solution.py:495
  46.3 1.5 %collective-permute-start.14 = (bf16[32,3584]{1,0:T(8,128)(2,1)S(1)}, bf16[32,3584]{1,0:T(8,128)(2,1)S(1)}, u32[]{:S(2)}, u32[]{:S(2)}) collective-permute-start(bf16[32,3584]{1,0:T(8,128)(2,1)S(1)} %get-tuple-element.68), channel_id=1, source_target_pairs={{0,1},{1,0},{2,3},{3,2},{4,5},{5,4},{6,7},{7,6},{8,9},{9,8},{10,11... | collective-permute-start | bytes 688136 | tf_op jit(solution)/shard_map/ppermute | solution.py:495
  46.4 5.9 %collective-permute-start.18 = (f32[64,128]{1,0:T(8,128)S(1)}, f32[64,128]{1,0:T(8,128)S(1)}, u32[]{:S(2)}, u32[]{:S(2)}) collective-permute-start(f32[64,128]{1,0:T(8,128)S(1)} %get-tuple-element.73), channel_id=1, source_target_pairs={{0,8},{8,0},{16,24},{24,16},{1,9},{9,1},{17,25},{25,17},{2,10},{10... | collective-permute-start | bytes 98312 | tf_op jit(solution)/shard_map/ppermute | solution.py:511
  47.9 8.1 %collective-permute-start.15 = (bf16[8,3584]{1,0:T(8,128)(2,1)S(1)}, bf16[8,3584]{1,0:T(8,128)(2,1)S(1)}, u32[]{:S(2)}, u32[]{:S(2)}) collective-permute-start(bf16[8,3584]{1,0:T(8,128)(2,1)S(1)} %get-tuple-element.70), channel_id=1, source_target_pairs={{0,6},{1,7},{2,4},{3,5},{4,2},{5,3},{6,0},{7,1},{8,14},{9,15},{10,... | collective-permute-start | bytes 172040 | tf_op jit(solution)/shard_map/ppermute | solution.py:486
  49.8 6.3 %collective-permute-start.16 = (bf16[8,3584]{1,0:T(8,128)(2,1)S(1)}, bf16[8,3584]{1,0:T(8,128)(2,1)S(1)}, u32[]{:S(2)}, u32[]{:S(2)}) collective-permute-start(bf16[8,3584]{1,0:T(8,128)(2,1)S(1)} %get-tuple-element.71), channel_id=1, source_target_pairs={{0,4},{1,5},{2,6},{3,7},{4,0},{5,1},{6,2},{7,3},{8,12},{9,13},{10,... | collective-permute-start | bytes 172040 | tf_op jit(solution)/shard_map/ppermute | solution.py:486
  49.8 6.3 %collective-permute-start.17 = (bf16[8,3584]{1,0:T(8,128)(2,1)S(1)}, bf16[8,3584]{1,0:T(8,128)(2,1)S(1)}, u32[]{:S(2)}, u32[]{:S(2)}) collective-permute-start(bf16[8,3584]{1,0:T(8,128)(2,1)S(1)} %get-tuple-element.72), channel_id=1, source_target_pairs={{0,2},{1,3},{2,0},{3,1},{4,6},{5,7},{6,4},{7,5},{8,10},{9,11},{10,... | collective-permute-start | bytes 172040 | tf_op jit(solution)/shard_map/ppermute | solution.py:486
  52.3 3.6 %collective-permute-start.19 = (f32[4,128]{1,0:T(4,128)S(1)}, f32[4,128]{1,0:T(4,128)S(1)}, u32[]{:S(2)}, u32[]{:S(2)}) collective-permute-start(f32[4,128]{1,0:T(4,128)S(1)} %slice_add_fusion.refs_4_), channel_id=1, source_target_pairs={{0,16},{8,24},{16,0},{24,8},{1,17},{9,25},{17,1},{25,9},{2,18},{10... | collective-permute-start | bytes 6152 | tf_op jit(solution)/shard_map/ppermute | solution.py:511

commit v5 on v4

--- a/solution.py
+++ b/solution.py
@@ -142,10 +142,9 @@
         block_ref[:, :features] = jnp.concatenate(rows).astype(jnp.bfloat16)
 
 
-def prepare_body(group, experts, capacity, *refs):
+def fetch_body(group, experts, capacity, *refs):
     sources, me_ref = refs[:4], refs[4]
-    block_refs = refs[5 : 5 + experts]
-    x_ref, normed_ref, place_ref, router_ref, routes_ref, sems = refs[5 + experts :]
+    x_ref, place_ref, turned_ref, router_ref, routes_ref, sems = refs[5:]
     targets = [x_ref.at[0], x_ref.at[1], router_ref, routes_ref]
     copies = [
         pltpu.make_async_copy(source, target, sems.at[i])
@@ -154,49 +153,64 @@
     for copy in copies:
         copy.start()
     mine = lax.div(me_ref[0, 0], group)
-    rows = x_ref.shape[1]
     copies[3].wait()
-    places = [
-        place_rows(chosen_by(routes_ref[0, stream]), mine, rows, capacity)
-        for stream in range(STREAMS)
-    ]
+    for stream in range(STREAMS):
+        place = place_rows(
+            chosen_by(routes_ref[0, stream]), mine, x_ref.shape[1], capacity
+        )
+        place_ref[stream] = place
+        turned_ref[stream] = turned(place, experts * capacity)
     for copy in copies[:3]:
         copy.wait()
-    packed = []
-    for stream in range(STREAMS):
-        normed = normalize(x_ref[stream])
-        normed_ref[stream] = normed
-        place_ref[stream] = places[stream]
-        packed.append(pack_rows(turned(places[stream], experts * capacity), normed))
-    store_blocks(packed, block_refs, capacity)
-
-
-def prepare(inputs, group, capacity):
+
+
+def fetch(inputs, group, capacity):
     x, _, router, routes, _ = inputs
     rows, features = x.shape
     experts = router.shape[1]
-    both = jax.ShapeDtypeStruct((STREAMS, rows, features), jnp.bfloat16)
     outs = [
-        jax.ShapeDtypeStruct((STREAMS * capacity, features), jnp.bfloat16) for _ in range(experts)
-    ]
-    outs += [
-        both,
-        both,
+        jax.ShapeDtypeStruct((STREAMS, rows, features), jnp.bfloat16),
         jax.ShapeDtypeStruct((STREAMS, rows, LANES), jnp.float32),
+        jax.ShapeDtypeStruct((STREAMS, experts * capacity, rows), jnp.bfloat16),
         jax.ShapeDtypeStruct(router.shape, router.dtype),
         jax.ShapeDtypeStruct(routes.shape, routes.dtype),
     ]
-    result = call(
-        functools.partial(prepare_body, group, experts, capacity),
+    return call(
+        functools.partial(fetch_body, group, experts, capacity),
         outs,
-        "prepare",
-        EARLY_FLOPS,
+        "fetch",
+        0,
         4 * rows * features,
         [pl.BlockSpec(memory_space=pl.ANY)] * 4 + [pl.BlockSpec(memory_space=pltpu.VMEM)],
         None,
         [pltpu.SemaphoreType.DMA((4,))],
     )(*[in_hbm(value) for value in inputs[:4]], inputs[4])
-    return result[:experts], result[experts:]
+
+
+def prepare_body(experts, capacity, x_ref, turned_ref, *refs):
+    block_refs, normed_ref = refs[:experts], refs[experts]
+    packed = []
+    for stream in range(STREAMS):
+        normed = normalize(x_ref[stream])
+        normed_ref[stream] = normed
+        packed.append(pack_rows(turned_ref[stream], normed))
+    store_blocks(packed, block_refs, capacity)
+
+
+def prepare(x, packing, experts, capacity):
+    features = x.shape[2]
+    outs = [
+        jax.ShapeDtypeStruct((STREAMS * capacity, features), jnp.bfloat16) for _ in range(experts)
+    ]
+    outs.append(jax.ShapeDtypeStruct(x.shape, x.dtype))
+    result = call(
+        functools.partial(prepare_body, experts, capacity),
+        outs,
+        "prepare",
+        EARLY_FLOPS,
+        4 * x.size,
+    )(x, packing)
+    return result[:experts], result[experts]
 
 
 def gates_body(group, experts, capacity, spare, *refs):
@@ -530,10 +544,10 @@
         first, last = step == 0, step == TICKS - 1
         room = spare if last else 0
         if first:
-            blocks, others = prepare(
+            x, slots, packing, router, picks = fetch(
                 [stream_a[0], stream_b[0], router, picks, me], ring.group, capacity
             )
-            x, normed, slots, router, picks = others
+            blocks, normed = prepare(x, packing, experts, capacity)
             coefficient, mass, slots, packing = gates(
                 normed, slots, router, picks, me, ring.group, capacity, spare
             )

time: 57.2 us -> 57.1 us (level)
    pallas_call x1 -> x2, Pallas kernels: 1.38 us -> 1.3 us  [the longest x1 0.98 us: fetch(): call(functools.partial(fetch_body, group, experts, capacity), outs, 'fetc...]
where the time goes in v5:
time: 57.1 us; the launch traced here: 56.9 us
  waiting for transfers between devices  24.6 us (43%)
  starting transfers between devices  22.8 us (40%)
  Pallas kernels  8.66 us (15%)
  between operations  0.74 us (1%)
    ppermute x12, starting transfers between devices, across(): lax.ppermute(blocks[k], 'expert', [(j, j ^ k * self.group) for j in range...  18.1 us
    ppermute x12, waiting for transfers between devices, across(): lax.ppermute(blocks[k], 'expert', [(j, j ^ k * self.group) for j in range...  12.9 us
    pallas_call x2, Pallas kernels, expert_rows(): call(functools.partial(expert_body, group, capacity, experts, spare, laye...  5.26 us
    ppermute x4, waiting for transfers between devices, within(): return lax.ppermute(array, 'expert', pairs)  5.03 us
    ppermute x2, waiting for transfers between devices, over_sections(): lax.ppermute(table, 'pipe', [(i, i ^ step) for i in range(self.pipe)])  3.08 us
    ppermute x1, starting transfers between devices, far(): return lax.ppermute(array, 'pipe', list(enumerate(steps)))  2.52 us
    ppermute x1, waiting for transfers between devices, far(): return lax.ppermute(array, 'pipe', list(enumerate(steps)))  2.45 us
    ppermute x1, waiting for transfers between devices, near(): return lax.ppermute(array, 'pipe', [(i, i ^ 1) for i in range(self.pipe)])  1.2 us
  transfers between devices with their start and end apart: 20, of which 16 were waited for; matrix products, arithmetic and copies ran while one was open for 0% of the time, Pallas kernels for 1%

profile of v5, /device:TPU:0, one launch (start us, length us, event | category | flops | bytes accessed | tf_op | source)
XLA Modules:
  0.0 56.9 jit_solution(14465502108568396487)
XLA Ops:
  0.7 1.0 %fetch.1 = (bf16[2,8,3584]{2,1,0:T(8,128)(2,1)S(1)}, f32[2,8,128]{2,1,0:T(8,128)S(1)}, bf16[2,16,8]{2,1,0:T(8,128)(2,1)S(1)}, bf16[2,4,3584]{2,1,0:T(4,128)(2,1)S(1)}, s32[2,2,2,8]{3,2,1,0:T(2,128)S(1)}) custom-call(bf16[8,3584]{1,0:T(8,128)(2,1)} %bitcast.28, bf16[8,3584]{1,0:T(8,128)(2,1)} %bitcast.29, bf16[2,4,3584]{2,1,0:T(4,128)(2,1)} %bitcast.30, ...), custom_call_target="tpu_custom_call" | custom-call | bytes 114688 | tf_op jit(solution)/shard_map/fetch/pallas_call | solution.py:178
  2.0 4.1 %collective-permute-start = (bf16[8,3584]{1,0:T(8,128)(2,1)S(1)}, bf16[8,3584]{1,0:T(8,128)(2,1)S(1)}, u32[]{:S(2)}, u32[]{:S(2)}) collective-permute-start(bf16[8,3584]{1,0:T(8,128)(2,1)S(1)} %get-tuple-element.49), channel_id=1, source_target_pairs={{0,4},{1,5},{2,6},{3,7},{4,0},{5,1},{6,2},{7,3},{8,12},{9,13},{10,... | collective-permute-start | bytes 172040 | tf_op jit(solution)/shard_map/ppermute | solution.py:500
  6.2 1.4 %collective-permute-start.1 = (bf16[8,3584]{1,0:T(8,128)(2,1)S(1)}, bf16[8,3584]{1,0:T(8,128)(2,1)S(1)}, u32[]{:S(2)}, u32[]{:S(2)}) collective-permute-start(bf16[8,3584]{1,0:T(8,128)(2,1)S(1)} %get-tuple-element.50), channel_id=1, source_target_pairs={{0,6},{1,7},{2,4},{3,5},{4,2},{5,3},{6,0},{7,1},{8,14},{9,15},{10,... | collective-permute-start | bytes 172040 | tf_op jit(solution)/shard_map/ppermute | solution.py:500
  7.7 1.2 %collective-permute-done.refs_1_ = bf16[8,3584]{1,0:T(8,128)(2,1)S(1)} collective-permute-done((bf16[8,3584]{1,0:T(8,128)(2,1)S(1)}, bf16[8,3584]{1,0:T(8,128)(2,1)S(1)}, u32[]{:S(2)}, u32[]{:S(2)}) %collective-permute-start) | collective-permute-done | bytes 57376 | tf_op jit(solution)/shard_map/ppermute | solution.py:500
  8.9 3.3 %collective-permute-done.1.refs_2_ = bf16[8,3584]{1,0:T(8,128)(2,1)S(1)} collective-permute-done((bf16[8,3584]{1,0:T(8,128)(2,1)S(1)}, bf16[8,3584]{1,0:T(8,128)(2,1)S(1)}, u32[]{:S(2)}, u32[]{:S(2)}) %collective-permute-start.1) | collective-permute-done | bytes 57376 | tf_op jit(solution)/shard_map/ppermute | solution.py:500
  12.4 1.5 %collective-permute-done.3.refs_1_ = bf16[32,3584]{1,0:T(8,128)(2,1)S(1)} collective-permute-done((bf16[32,3584]{1,0:T(8,128)(2,1)S(1)}, bf16[32,3584]{1,0:T(8,128)(2,1)S(1)}, u32[]{:S(2)}, u32[]{:S(2)}) %collective-permute-start.3) | collective-permute-done | bytes 229408 | tf_op jit(solution)/shard_map/ppermute | solution.py:509
  13.9 2.6 %experts.2 = (bf16[32,3584]{1,0:T(8,128)(2,1)S(1)}, bf16[32,3584]{1,0:T(8,128)(2,1)S(1)}) custom-call(bf16[2,3584,512]{2,1,0:T(8,128)(2,1)S(1)} %bitcast.16, bf16[2,512,3584]{2,1,0:T(8,128)(2,1)S(1)} %bitcast.22, bf16[32,3584]{1,0:T(8,128)(2,1)S(1)} %join.2.refs_0_, bf16[32,3584]{1,0:T(8,128)(2,1)S(1)} %collective-permute-done.3.refs_1_), custom_call_target="tpu_custom_call" | custom-call | flops 469762048 | bytes 7340032 | tf_op jit(solution)/shard_map/experts/pallas_call | solution.py:405
  16.7 1.4 %collective-permute-done.4.refs_1_ = bf16[32,3584]{1,0:T(8,128)(2,1)S(1)} collective-permute-done((bf16[32,3584]{1,0:T(8,128)(2,1)S(1)}, bf16[32,3584]{1,0:T(8,128)(2,1)S(1)}, u32[]{:S(2)}, u32[]{:S(2)}) %collective-permute-start.4) | collective-permute-done | bytes 229408 | tf_op jit(solution)/shard_map/ppermute | solution.py:509
  18.2 2.6 %collective-permute-start.5 = (bf16[8,3584]{1,0:T(8,128)(2,1)S(1)}, bf16[8,3584]{1,0:T(8,128)(2,1)S(1)}, u32[]{:S(2)}, u32[]{:S(2)}) collective-permute-start(bf16[8,3584]{1,0:T(8,128)(2,1)S(1)} %get-tuple-element.55), channel_id=1, source_target_pairs={{0,6},{1,7},{2,4},{3,5},{4,2},{5,3},{6,0},{7,1},{8,14},{9,15},{10,... | collective-permute-start | bytes 172040 | tf_op jit(solution)/shard_map/ppermute | solution.py:500
  20.8 1.8 %collective-permute-start.7 = (bf16[8,3584]{1,0:T(8,128)(2,1)S(1)}, bf16[8,3584]{1,0:T(8,128)(2,1)S(1)}, u32[]{:S(2)}, u32[]{:S(2)}) collective-permute-start(bf16[8,3584]{1,0:T(8,128)(2,1)S(1)} %get-tuple-element.57), channel_id=1, source_target_pairs={{0,2},{1,3},{2,0},{3,1},{4,6},{5,7},{6,4},{7,5},{8,10},{9,11},{10,... | collective-permute-start | bytes 172040 | tf_op jit(solution)/shard_map/ppermute | solution.py:500
  22.9 1.9 %collective-permute-done.5.refs_4_ = bf16[8,3584]{1,0:T(8,128)(2,1)S(1)} collective-permute-done((bf16[8,3584]{1,0:T(8,128)(2,1)S(1)}, bf16[8,3584]{1,0:T(8,128)(2,1)S(1)}, u32[]{:S(2)}, u32[]{:S(2)}) %collective-permute-start.5) | collective-permute-done | bytes 57376 | tf_op jit(solution)/shard_map/ppermute | solution.py:500
  24.8 1.9 %collective-permute-done.6.refs_5_ = bf16[8,3584]{1,0:T(8,128)(2,1)S(1)} collective-permute-done((bf16[8,3584]{1,0:T(8,128)(2,1)S(1)}, bf16[8,3584]{1,0:T(8,128)(2,1)S(1)}, u32[]{:S(2)}, u32[]{:S(2)}) %collective-permute-start.6) | collective-permute-done | bytes 57376 | tf_op jit(solution)/shard_map/ppermute | solution.py:500
  26.9 2.5 %collective-permute-start.8 = (bf16[8,3584]{1,0:T(8,128)(2,1)S(1)}, bf16[8,3584]{1,0:T(8,128)(2,1)S(1)}, u32[]{:S(2)}, u32[]{:S(2)}) collective-permute-start(bf16[8,3584]{1,0:T(8,128)(2,1)S(1)} %get-tuple-element.58), channel_id=1, source_target_pairs={{0,24},{8,16},{16,8},{24,0},{1,25},{9,17},{17,9},{25,1},{2,26},{10... | collective-permute-start | bytes 172040 | tf_op jit(solution)/shard_map/ppermute | solution.py:513
  29.4 0.5 collective-permute-start.9
  29.9 2.4 %collective-permute-done.8.refs_0_ = bf16[8,3584]{1,0:T(8,128)(2,1)S(1)} collective-permute-done((bf16[8,3584]{1,0:T(8,128)(2,1)S(1)}, bf16[8,3584]{1,0:T(8,128)(2,1)S(1)}, u32[]{:S(2)}, u32[]{:S(2)}) %collective-permute-start.8) | collective-permute-done | bytes 57376 | tf_op jit(solution)/shard_map/ppermute | solution.py:513
  32.4 1.2 %collective-permute-done.9.refs_1_ = bf16[8,3584]{1,0:T(8,128)(2,1)S(1)} collective-permute-done((bf16[8,3584]{1,0:T(8,128)(2,1)S(1)}, bf16[8,3584]{1,0:T(8,128)(2,1)S(1)}, u32[]{:S(2)}, u32[]{:S(2)}) %collective-permute-start.9) | collective-permute-done | bytes 57376 | tf_op jit(solution)/shard_map/ppermute | solution.py:516
  33.6 0.5 prepare.3
  34.1 1.3 %collective-permute-start.10 = (bf16[8,3712]{1,0:T(8,128)(2,1)S(1)}, bf16[8,3712]{1,0:T(8,128)(2,1)S(1)}, u32[]{:S(2)}, u32[]{:S(2)}) collective-permute-start(bf16[8,3712]{1,0:T(8,128)(2,1)S(1)} %get-tuple-element.66), channel_id=1, source_target_pairs={{0,4},{1,5},{2,6},{3,7},{4,0},{5,1},{6,2},{7,3},{8,12},{9,13},{10,... | collective-permute-start | bytes 178184 | tf_op jit(solution)/shard_map/ppermute | solution.py:500
  35.4 1.7 %collective-permute-start.11 = (bf16[8,3712]{1,0:T(8,128)(2,1)S(1)}, bf16[8,3712]{1,0:T(8,128)(2,1)S(1)}, u32[]{:S(2)}, u32[]{:S(2)}) collective-permute-start(bf16[8,3712]{1,0:T(8,128)(2,1)S(1)} %get-tuple-element.67), channel_id=1, source_target_pairs={{0,6},{1,7},{2,4},{3,5},{4,2},{5,3},{6,0},{7,1},{8,14},{9,15},{10,... | collective-permute-start | bytes 178184 | tf_op jit(solution)/shard_map/ppermute | solution.py:500
  37.1 0.6 collective-permute-start.12
  37.6 2.6 %collective-permute-done.10.refs_1_ = bf16[8,3712]{1,0:T(8,128)(2,1)S(1)} collective-permute-done((bf16[8,3712]{1,0:T(8,128)(2,1)S(1)}, bf16[8,3712]{1,0:T(8,128)(2,1)S(1)}, u32[]{:S(2)}, u32[]{:S(2)}) %collective-permute-start.10) | collective-permute-done | bytes 59424 | tf_op jit(solution)/shard_map/ppermute | solution.py:500
  40.2 1.3 %collective-permute-done.11.refs_2_ = bf16[8,3712]{1,0:T(8,128)(2,1)S(1)} collective-permute-done((bf16[8,3712]{1,0:T(8,128)(2,1)S(1)}, bf16[8,3712]{1,0:T(8,128)(2,1)S(1)}, u32[]{:S(2)}, u32[]{:S(2)}) %collective-permute-start.11) | collective-permute-done | bytes 59424 | tf_op jit(solution)/shard_map/ppermute | solution.py:500
  41.5 0.4 collective-permute-done.12.refs_3_
  42.1 1.5 %collective-permute-done.13.refs_2_ = bf16[32,3712]{1,0:T(8,128)(2,1)S(1)} collective-permute-done((bf16[32,3712]{1,0:T(8,128)(2,1)S(1)}, bf16[32,3712]{1,0:T(8,128)(2,1)S(1)}, u32[]{:S(2)}, u32[]{:S(2)}) %collective-permute-start.13) | collective-permute-done | bytes 237600 | tf_op jit(solution)/shard_map/ppermute | solution.py:509
  43.5 2.6 %experts.3 = (bf16[32,3584]{1,0:T(8,128)(2,1)S(1)}, bf16[32,3584]{1,0:T(8,128)(2,1)S(1)}, f32[64,128]{1,0:T(8,128)S(1)}) custom-call(bf16[2,3584,512]{2,1,0:T(8,128)(2,1)S(1)} %bitcast.21, bf16[2,512,3584]{2,1,0:T(8,128)(2,1)S(1)} %bitcast.27, s32[1,2]{1,0:T(1,128)S(1)} %add_bitcast_fusion.refs_4_.refs_1_.refs_6_.refs_0_.me_ref, ...), custom_call_target="tpu_custom_call" | custom-call | flops 469762048 | bytes 7340032 | tf_op jit(solution)/shard_map/experts/pallas_call | solution.py:405
  46.4 0.6 %collective-permute-start.18 = (f32[64,128]{1,0:T(8,128)S(1)}, f32[64,128]{1,0:T(8,128)S(1)}, u32[]{:S(2)}, u32[]{:S(2)}) collective-permute-start(f32[64,128]{1,0:T(8,128)S(1)} %get-tuple-element.75), channel_id=1, source_target_pairs={{0,8},{8,0},{16,24},{24,16},{1,9},{9,1},{17,25},{25,17},{2,10},{10... | collective-permute-start | bytes 98312 | tf_op jit(solution)/shard_map/ppermute | solution.py:525
  47.0 0.7 %collective-permute-done.14.refs_1_ = bf16[32,3584]{1,0:T(8,128)(2,1)S(1)} collective-permute-done((bf16[32,3584]{1,0:T(8,128)(2,1)S(1)}, bf16[32,3584]{1,0:T(8,128)(2,1)S(1)}, u32[]{:S(2)}, u32[]{:S(2)}) %collective-permute-start.14) | collective-permute-done | bytes 229408 | tf_op jit(solution)/shard_map/ppermute | solution.py:509
  47.8 2.0 %collective-permute-start.15 = (bf16[8,3584]{1,0:T(8,128)(2,1)S(1)}, bf16[8,3584]{1,0:T(8,128)(2,1)S(1)}, u32[]{:S(2)}, u32[]{:S(2)}) collective-permute-start(bf16[8,3584]{1,0:T(8,128)(2,1)S(1)} %get-tuple-element.72), channel_id=1, source_target_pairs={{0,6},{1,7},{2,4},{3,5},{4,2},{5,3},{6,0},{7,1},{8,14},{9,15},{10,... | collective-permute-start | bytes 172040 | tf_op jit(solution)/shard_map/ppermute | solution.py:500
  49.8 2.5 %collective-permute-start.17 = (bf16[8,3584]{1,0:T(8,128)(2,1)S(1)}, bf16[8,3584]{1,0:T(8,128)(2,1)S(1)}, u32[]{:S(2)}, u32[]{:S(2)}) collective-permute-start(bf16[8,3584]{1,0:T(8,128)(2,1)S(1)} %get-tuple-element.74), channel_id=1, source_target_pairs={{0,2},{1,3},{2,0},{3,1},{4,6},{5,7},{6,4},{7,5},{8,10},{9,11},{10,... | collective-permute-start | bytes 172040 | tf_op jit(solution)/shard_map/ppermute | solution.py:500
  52.3 0.5 collective-permute-start.19
  52.8 3.1 %collective-permute-done.19.refs_5_ = f32[4,128]{1,0:T(4,128)S(1)} collective-permute-done((f32[4,128]{1,0:T(4,128)S(1)}, f32[4,128]{1,0:T(4,128)S(1)}, u32[]{:S(2)}, u32[]{:S(2)}) %collective-permute-start.19) | collective-permute-done | bytes 2080 | tf_op jit(solution)/shard_map/ppermute | solution.py:525
  56.1 0.8 %finish.3 = (bf16[8,3584]{1,0:T(8,128)(2,1)}, bf16[8,3584]{1,0:T(8,128)(2,1)}, f32[4,4]{1,0:T(4,128)}) custom-call(bf16[2,8,3584]{2,1,0:T(8,128)(2,1)S(1)} %get-tuple-element.63.x_ref, s32[1,2]{1,0:T(1,128)S(1)} %add_bitcast_fusion.refs_4_.refs_1_.refs_6_.refs_0_.me_ref, f32[2,8,128]{2,1,0:T(8,128)S(1)} %get-tuple-element.64.coefficient_ref, ...), custom_call_target="tpu_custom_call" | custom-call | flops 3670016 | bytes 344064 | tf_op jit(solution)/shard_map/finish/pallas_call | solution.py:479
  (26 shorter events, 2.2 us)
Async XLA Ops:
  1.7 12.2 %copy-start = (bf16[2,1,3584,512]{3,2,1,0:T(8,128)(2,1)S(1)}, bf16[2,1,3584,512]{3,2,1,0:T(8,128)(2,1)}, u32[]{:S(2)}) copy-start(bf16[2,1,3584,512]{3,2,1,0:T(8,128)(2,1)} %param.9) | copy-start | bytes 22020100
  1.7 12.2 %copy-start.1 = (bf16[2,1,512,3584]{3,2,1,0:T(8,128)(2,1)S(1)}, bf16[2,1,512,3584]{3,2,1,0:T(8,128)(2,1)}, u32[]{:S(2)}) copy-start(bf16[2,1,512,3584]{3,2,1,0:T(8,128)(2,1)} %param.10) | copy-start | bytes 22020100
  2.0 6.9 %collective-permute-start = (bf16[8,3584]{1,0:T(8,128)(2,1)S(1)}, bf16[8,3584]{1,0:T(8,128)(2,1)S(1)}, u32[]{:S(2)}, u32[]{:S(2)}) collective-permute-start(bf16[8,3584]{1,0:T(8,128)(2,1)S(1)} %get-tuple-element.49), channel_id=1, source_target_pairs={{0,4},{1,5},{2,6},{3,7},{4,0},{5,1},{6,2},{7,3},{8,12},{9,13},{10,... | collective-permute-start | bytes 172040 | tf_op jit(solution)/shard_map/ppermute | solution.py:500
  6.2 6.1 %collective-permute-start.1 = (bf16[8,3584]{1,0:T(8,128)(2,1)S(1)}, bf16[8,3584]{1,0:T(8,128)(2,1)S(1)}, u32[]{:S(2)}, u32[]{:S(2)}) collective-permute-start(bf16[8,3584]{1,0:T(8,128)(2,1)S(1)} %get-tuple-element.50), channel_id=1, source_target_pairs={{0,6},{1,7},{2,4},{3,5},{4,2},{5,3},{6,0},{7,1},{8,14},{9,15},{10,... | collective-permute-start | bytes 172040 | tf_op jit(solution)/shard_map/ppermute | solution.py:500
  7.5 4.8 %collective-permute-start.2 = (bf16[8,3584]{1,0:T(8,128)(2,1)S(1)}, bf16[8,3584]{1,0:T(8,128)(2,1)S(1)}, u32[]{:S(2)}, u32[]{:S(2)}) collective-permute-start(bf16[8,3584]{1,0:T(8,128)(2,1)S(1)} %get-tuple-element.51), channel_id=1, source_target_pairs={{0,2},{1,3},{2,0},{3,1},{4,6},{5,7},{6,4},{7,5},{8,10},{9,11},{10,... | collective-permute-start | bytes 172040 | tf_op jit(solution)/shard_map/ppermute | solution.py:500
  12.4 1.6 %collective-permute-start.3 = (bf16[32,3584]{1,0:T(8,128)(2,1)S(1)}, bf16[32,3584]{1,0:T(8,128)(2,1)S(1)}, u32[]{:S(2)}, u32[]{:S(2)}) collective-permute-start(bf16[32,3584]{1,0:T(8,128)(2,1)S(1)} %join.2.refs_0_), channel_id=1, source_target_pairs={{0,1},{1,0},{2,3},{3,2},{4,5},{5,4},{6,7},{7,6},{8,9},{9,8},{10,11... | collective-permute-start | bytes 688136 | tf_op jit(solution)/shard_map/ppermute | solution.py:509
  16.6 1.5 %collective-permute-start.4 = (bf16[32,3584]{1,0:T(8,128)(2,1)S(1)}, bf16[32,3584]{1,0:T(8,128)(2,1)S(1)}, u32[]{:S(2)}, u32[]{:S(2)}) collective-permute-start(bf16[32,3584]{1,0:T(8,128)(2,1)S(1)} %get-tuple-element.53), channel_id=1, source_target_pairs={{0,1},{1,0},{2,3},{3,2},{4,5},{5,4},{6,7},{7,6},{8,9},{9,8},{10,11... | collective-permute-start | bytes 688136 | tf_op jit(solution)/shard_map/ppermute | solution.py:509
  18.2 6.6 %collective-permute-start.5 = (bf16[8,3584]{1,0:T(8,128)(2,1)S(1)}, bf16[8,3584]{1,0:T(8,128)(2,1)S(1)}, u32[]{:S(2)}, u32[]{:S(2)}) collective-permute-start(bf16[8,3584]{1,0:T(8,128)(2,1)S(1)} %get-tuple-element.55), channel_id=1, source_target_pairs={{0,6},{1,7},{2,4},{3,5},{4,2},{5,3},{6,0},{7,1},{8,14},{9,15},{10,... | collective-permute-start | bytes 172040 | tf_op jit(solution)/shard_map/ppermute | solution.py:500
  20.8 5.9 %collective-permute-start.6 = (bf16[8,3584]{1,0:T(8,128)(2,1)S(1)}, bf16[8,3584]{1,0:T(8,128)(2,1)S(1)}, u32[]{:S(2)}, u32[]{:S(2)}) collective-permute-start(bf16[8,3584]{1,0:T(8,128)(2,1)S(1)} %get-tuple-element.56), channel_id=1, source_target_pairs={{0,4},{1,5},{2,6},{3,7},{4,0},{5,1},{6,2},{7,3},{8,12},{9,13},{10,... | collective-permute-start | bytes 172040 | tf_op jit(solution)/shard_map/ppermute | solution.py:500
  20.8 5.9 %collective-permute-start.7 = (bf16[8,3584]{1,0:T(8,128)(2,1)S(1)}, bf16[8,3584]{1,0:T(8,128)(2,1)S(1)}, u32[]{:S(2)}, u32[]{:S(2)}) collective-permute-start(bf16[8,3584]{1,0:T(8,128)(2,1)S(1)} %get-tuple-element.57), channel_id=1, source_target_pairs={{0,2},{1,3},{2,0},{3,1},{4,6},{5,7},{6,4},{7,5},{8,10},{9,11},{10,... | collective-permute-start | bytes 172040 | tf_op jit(solution)/shard_map/ppermute | solution.py:500
  26.9 5.5 %collective-permute-start.8 = (bf16[8,3584]{1,0:T(8,128)(2,1)S(1)}, bf16[8,3584]{1,0:T(8,128)(2,1)S(1)}, u32[]{:S(2)}, u32[]{:S(2)}) collective-permute-start(bf16[8,3584]{1,0:T(8,128)(2,1)S(1)} %get-tuple-element.58), channel_id=1, source_target_pairs={{0,24},{8,16},{16,8},{24,0},{1,25},{9,17},{17,9},{25,1},{2,26},{10... | collective-permute-start | bytes 172040 | tf_op jit(solution)/shard_map/ppermute | solution.py:513
  29.4 4.2 %collective-permute-start.9 = (bf16[8,3584]{1,0:T(8,128)(2,1)S(1)}, bf16[8,3584]{1,0:T(8,128)(2,1)S(1)}, u32[]{:S(2)}, u32[]{:S(2)}) collective-permute-start(bf16[8,3584]{1,0:T(8,128)(2,1)S(1)} %get-tuple-element.59), channel_id=1, source_target_pairs={{0,8},{8,0},{16,24},{24,16},{1,9},{9,1},{17,25},{25,17},{2,10},{10... | collective-permute-start | bytes 172040 | tf_op jit(solution)/shard_map/ppermute | solution.py:516
  34.1 6.1 %collective-permute-start.10 = (bf16[8,3712]{1,0:T(8,128)(2,1)S(1)}, bf16[8,3712]{1,0:T(8,128)(2,1)S(1)}, u32[]{:S(2)}, u32[]{:S(2)}) collective-permute-start(bf16[8,3712]{1,0:T(8,128)(2,1)S(1)} %get-tuple-element.66), channel_id=1, source_target_pairs={{0,4},{1,5},{2,6},{3,7},{4,0},{5,1},{6,2},{7,3},{8,12},{9,13},{10,... | collective-permute-start | bytes 178184 | tf_op jit(solution)/shard_map/ppermute | solution.py:500
  35.4 6.2 %collective-permute-start.11 = (bf16[8,3712]{1,0:T(8,128)(2,1)S(1)}, bf16[8,3712]{1,0:T(8,128)(2,1)S(1)}, u32[]{:S(2)}, u32[]{:S(2)}) collective-permute-start(bf16[8,3712]{1,0:T(8,128)(2,1)S(1)} %get-tuple-element.67), channel_id=1, source_target_pairs={{0,6},{1,7},{2,4},{3,5},{4,2},{5,3},{6,0},{7,1},{8,14},{9,15},{10,... | collective-permute-start | bytes 178184 | tf_op jit(solution)/shard_map/ppermute | solution.py:500
  37.1 4.8 %collective-permute-start.12 = (bf16[8,3712]{1,0:T(8,128)(2,1)S(1)}, bf16[8,3712]{1,0:T(8,128)(2,1)S(1)}, u32[]{:S(2)}, u32[]{:S(2)}) collective-permute-start(bf16[8,3712]{1,0:T(8,128)(2,1)S(1)} %get-tuple-element.68), channel_id=1, source_target_pairs={{0,2},{1,3},{2,0},{3,1},{4,6},{5,7},{6,4},{7,5},{8,10},{9,11},{10,... | collective-permute-start | bytes 178184 | tf_op jit(solution)/shard_map/ppermute | solution.py:500
  42.0 1.6 %collective-permute-start.13 = (bf16[32,3712]{1,0:T(8,128)(2,1)S(1)}, bf16[32,3712]{1,0:T(8,128)(2,1)S(1)}, u32[]{:S(2)}, u32[]{:S(2)}) collective-permute-start(bf16[32,3712]{1,0:T(8,128)(2,1)S(1)} %join.3.refs_1_), channel_id=1, source_target_pairs={{0,1},{1,0},{2,3},{3,2},{4,5},{5,4},{6,7},{7,6},{8,9},{9,8},{10,11... | collective-permute-start | bytes 712712 | tf_op jit(solution)/shard_map/ppermute | solution.py:509
  46.2 1.5 %collective-permute-start.14 = (bf16[32,3584]{1,0:T(8,128)(2,1)S(1)}, bf16[32,3584]{1,0:T(8,128)(2,1)S(1)}, u32[]{:S(2)}, u32[]{:S(2)}) collective-permute-start(bf16[32,3584]{1,0:T(8,128)(2,1)S(1)} %get-tuple-element.70), channel_id=1, source_target_pairs={{0,1},{1,0},{2,3},{3,2},{4,5},{5,4},{6,7},{7,6},{8,9},{9,8},{10,11... | collective-permute-start | bytes 688136 | tf_op jit(solution)/shard_map/ppermute | solution.py:509
  46.4 5.9 %collective-permute-start.18 = (f32[64,128]{1,0:T(8,128)S(1)}, f32[64,128]{1,0:T(8,128)S(1)}, u32[]{:S(2)}, u32[]{:S(2)}) collective-permute-start(f32[64,128]{1,0:T(8,128)S(1)} %get-tuple-element.75), channel_id=1, source_target_pairs={{0,8},{8,0},{16,24},{24,16},{1,9},{9,1},{17,25},{25,17},{2,10},{10... | collective-permute-start | bytes 98312 | tf_op jit(solution)/shard_map/ppermute | solution.py:525
  47.8 8.1 %collective-permute-start.15 = (bf16[8,3584]{1,0:T(8,128)(2,1)S(1)}, bf16[8,3584]{1,0:T(8,128)(2,1)S(1)}, u32[]{:S(2)}, u32[]{:S(2)}) collective-permute-start(bf16[8,3584]{1,0:T(8,128)(2,1)S(1)} %get-tuple-element.72), channel_id=1, source_target_pairs={{0,6},{1,7},{2,4},{3,5},{4,2},{5,3},{6,0},{7,1},{8,14},{9,15},{10,... | collective-permute-start | bytes 172040 | tf_op jit(solution)/shard_map/ppermute | solution.py:500
  49.8 6.3 %collective-permute-start.16 = (bf16[8,3584]{1,0:T(8,128)(2,1)S(1)}, bf16[8,3584]{1,0:T(8,128)(2,1)S(1)}, u32[]{:S(2)}, u32[]{:S(2)}) collective-permute-start(bf16[8,3584]{1,0:T(8,128)(2,1)S(1)} %get-tuple-element.73), channel_id=1, source_target_pairs={{0,4},{1,5},{2,6},{3,7},{4,0},{5,1},{6,2},{7,3},{8,12},{9,13},{10,... | collective-permute-start | bytes 172040 | tf_op jit(solution)/shard_map/ppermute | solution.py:500
  49.8 6.3 %collective-permute-start.17 = (bf16[8,3584]{1,0:T(8,128)(2,1)S(1)}, bf16[8,3584]{1,0:T(8,128)(2,1)S(1)}, u32[]{:S(2)}, u32[]{:S(2)}) collective-permute-start(bf16[8,3584]{1,0:T(8,128)(2,1)S(1)} %get-tuple-element.74), channel_id=1, source_target_pairs={{0,2},{1,3},{2,0},{3,1},{4,6},{5,7},{6,4},{7,5},{8,10},{9,11},{10,... | collective-permute-start | bytes 172040 | tf_op jit(solution)/shard_map/ppermute | solution.py:500
  52.3 3.6 %collective-permute-start.19 = (f32[4,128]{1,0:T(4,128)S(1)}, f32[4,128]{1,0:T(4,128)S(1)}, u32[]{:S(2)}, u32[]{:S(2)}) collective-permute-start(f32[4,128]{1,0:T(4,128)S(1)} %slice_add_fusion.refs_4_), channel_id=1, source_target_pairs={{0,16},{8,24},{16,0},{24,8},{1,17},{9,25},{17,1},{25,9},{2,18},{10... | collective-permute-start | bytes 6152 | tf_op jit(solution)/shard_map/ppermute | solution.py:525
